TPU v7x, 256 devices: a whole 4x4x8 slice. The times are simulated.
256 devices in a mesh: row: 16 (over z_lo, y), col: 16 (over x, z_hi, core).
Axes of the slice: x: 4, y: 4, z: 8 (z_hi: 2, z_lo: 4; z = z_hi * 4 + z_lo), core: 2. Of those that a mesh axis runs over, the one named last changes fastest.
Arguments:
- activations: bfloat16 [512, 28672], P('row', 'col'), may hold values from -6 to 6
- act_grads: bfloat16 [512, 8192], P('col', 'row'), may hold values from -1.5 to 1.5
- eigen_act: bfloat16 [28672, 28672], P('col', 'row'), may hold values from -0.03125 to 0.03125
- eigen_grad: bfloat16 [8192, 8192], P('row', 'col'), may hold values from -0.0625 to 0.0625
- example_ids: int32 [512], replicated, may hold values from 0 to 31, never falling along the last dimension, each value on 1 to 32 neighbouring positions
Outputs:
- lambda_out: float32 [8192, 28672], P('col', 'row')
Inputs may be any that keep to these rules, and one draw needn't show every extreme that they name: `example_ids`: example ids never fall along the tokens; each example has 1 to 32 tokens and one has exactly 32.
All inputs are finite; a program needn't handle non-finite values.
Results may differ from a plain program's by a relative error of at most 0.0023.
Values may be sent and summed in bfloat16 or wider, within the bound.
No kernel may reach another device: no remote copies, remote signals or barrier semaphores. Data moves between devices by JAX's collectives and lax.ppermute only.
A program may use at most 64 MiB of HBM per device.

v0:
```python
import jax
import jax.numpy as jnp
from jax import lax
from jax.sharding import PartitionSpec as P

MOST_LEN = 32


def example_slots(example_ids, examples, most):
    total = example_ids.shape[0]
    numbers = jnp.arange(examples)
    below = (example_ids[None, :] < numbers[:, None]).astype(jnp.int32)
    starts = jnp.sum(below, axis=1)
    positions = starts[:, None] + jnp.arange(most)[None, :]
    clipped = jnp.minimum(positions, total - 1)
    valid = (positions < total) & (example_ids[clipped] == numbers[:, None])
    return (clipped, valid)


def local(activations, act_grads, eigen_act, eigen_grad, example_ids):
    act_part = jnp.dot(
        lax.all_gather(activations, "row", axis=0, tiled=True),
        eigen_act,
        preferred_element_type=jnp.float32,
    )
    act_rot = lax.psum(act_part, "col").astype(jnp.bfloat16)
    grad_part = jnp.dot(
        lax.all_gather(act_grads, "col", axis=0, tiled=True),
        eigen_grad,
        preferred_element_type=jnp.float32,
    )
    grad_rot = lax.psum(grad_part, "row").astype(jnp.bfloat16)
    examples = example_ids.shape[0] // 16
    slots, valid = example_slots(example_ids, examples, MOST_LEN)
    groups = examples // 4

    def step(index, total):
        rows = lax.dynamic_slice_in_dim(slots, index * 4, 4, 0)
        keep = lax.dynamic_slice_in_dim(valid, index * 4, 4, 0)[:, :, None]
        grad_rows = jnp.take(grad_rot, rows, axis=0)
        act_rows = jnp.take(act_rot, rows, axis=0)
        grad_rows = jnp.where(keep, grad_rows, jnp.zeros_like(grad_rows))
        act_rows = jnp.where(keep, act_rows, jnp.zeros_like(act_rows))
        blocks = jnp.einsum("eki,ekj->eij", grad_rows, act_rows, preferred_element_type=jnp.float32)
        return total + jnp.sum(blocks * blocks, axis=0)

    start = jnp.zeros((grad_rot.shape[1], act_rot.shape[1]), jnp.float32)
    total = lax.fori_loop(0, groups, step, start)
    return total / examples


def solution(mesh):
    in_specs = (P("row", "col"), P("col", "row"), P("col", "row"), P("row", "col"), P())
    out_specs = P("col", "row")
    return jax.shard_map(local, mesh=mesh, in_specs=in_specs, out_specs=out_specs, check_vma=False)
```

profile of v0, /device:TPU:80, one launch (start us, length us, event | category | flops | bytes accessed | tf_op | source)
XLA Modules:
  0.0 387.9 jit_solution(595297121387783496)
XLA Ops:
  8.2 6.9 %gather_fusion.2 = s32[1024]{0:T(1024)S(1)} fusion(s32[512]{0:T(512)S(1)} %copy-done.1, s32[1024]{0:T(1024)S(1)} %broadcast_clamp_fusion), kind=kCustom, calls=%fused_computation.2 | custom fusion | bytes 12288 | tf_op jit(solution)/shard_map/gather | solution.py:16
  15.2 36.6 %all_gather.6 = bf16[512,512]{1,0:T(8,128)(2,1)S(1)} all-gather(bf16[32,512]{1,0:T(8,128)(2,1)S(1)} %copy-done.4), channel_id=1, replica_groups=mesh['row'=16,'col'=16] {'col'}, dimensions={0}, use_global_device_ids=true | all-gather | bytes 557056 | tf_op jit(solution)/shard_map/all_gather | solution.py:28
  52.4 86.3 %all-reduce.2 = bf16[512,512]{1,0:T(8,128)(2,1)S(1)} all-reduce(f32[512,512]{1,0:T(8,128)S(1)} %fusion.17), channel_id=1, replica_groups=mesh['row'=16,'col'=16] {'row'}, use_global_device_ids=true, to_apply=%region_1.0 | all-reduce | flops 262144 | bytes 1572864 | tf_op jit(solution)/shard_map/psum | solution.py:32
  138.8 8.7 %fusion.18 = f32[512,1792]{1,0:T(8,128)} fusion(bf16[512,1792]{1,0:T(8,128)(2,1)} %all-gather.2.cloned.1.call-done, bf16[1792,1792]{1,0:T(8,128)(2,1)} %param.9), kind=kOutput, calls=%fused_computation.34 | convolution fusion | flops 3288334336 | bytes 11927552 | tf_op jit(solution)/shard_map/dot_general | solution.py:21
  147.4 174.2 %all-reduce.3 = bf16[512,1792]{1,0:T(8,128)(2,1)S(1)} all-reduce(f32[512,1792]{1,0:T(8,128)} %fusion.18), channel_id=1, replica_groups=mesh['row'=16,'col'=16] {'col'}, use_global_device_ids=true, to_apply=%region_2.0 | all-reduce | flops 917504 | bytes 5505024 | tf_op jit(solution)/shard_map/psum | solution.py:26
  321.6 55.4 %while.14 = (s32[]{:T(128)}, f32[512,1792]{1,0:T(8,128)}, pred[32,32]{1,0:T(8,128)(4,1)S(1)}, s32[32,32]{1,0:T(8,128)S(1)}, bf16[512,512]{1,0:T(8,128)(2,1)S(1)}...) while((s32[]{:T(128)}, f32[512,1792]{1,0:T(8,128)}, ...), condition=%wide.region_5.6_spmd.clone, body=%wide.region_3.5_spmd.clone.sunk | while | flops 243730176 | bytes 45818208 | solution.py:48
  322.6 0.9 gather_fusion
  323.5 2.2 multiply_reduce_fusion.2
  325.8 0.9 select_add_fusion.2
  326.7 1.8 copy-done.3
  330.5 2.2 multiply_reduce_fusion.2
  332.7 0.9 select_add_fusion.2
  333.6 1.8 copy-done.3
  337.4 2.2 multiply_reduce_fusion.2
  339.6 0.9 select_add_fusion.2
  340.6 1.8 copy-done.3
  344.3 2.2 multiply_reduce_fusion.2
  346.5 0.9 select_add_fusion.2
  347.5 1.8 copy-done.3
  351.2 2.2 multiply_reduce_fusion.2
  353.4 0.9 select_add_fusion.2
  354.4 1.8 copy-done.3
  358.1 2.2 multiply_reduce_fusion.2
  360.3 0.9 select_add_fusion.2
  361.3 1.8 copy-done.3
  365.0 2.2 multiply_reduce_fusion.2
  367.3 0.9 select_add_fusion.2
  368.2 1.8 copy-done.3
  372.0 2.2 multiply_reduce_fusion.2
  374.2 0.9 select_add_fusion.2
  375.1 1.8 copy-done.3
  377.0 4.1 %broadcast_multiply_fusion = f32[512,1792]{1,0:T(8,128)} fusion(f32[512,1792]{1,0:T(8,128)} %get-tuple-element.114), kind=kLoop, calls=%fused_computation.23 | loop fusion | flops 917504 | bytes 7340032 | tf_op jit(solution)/shard_map/div | solution.py:49
  (81 shorter events, 16.6 us)
Async XLA Ops:
  6.5 45.3 %copy-start = (bf16[512,512]{1,0:T(8,128)(2,1)S(1)}, bf16[512,512]{1,0:T(8,128)(2,1)}, u32[]{:S(2)}) copy-start(bf16[512,512]{1,0:T(8,128)(2,1)} %param.10) | copy-start | bytes 1572868
  6.5 1.7 copy-start.1
  6.5 132.2 %all-gather.2.cloned.1.call-start = ((), (), s32[]{:S(2)}) async-start(), calls=%async_computation | async-start | bytes 1949696 | tf_op jit(solution)/shard_map/all_gather | solution.py:22
  8.2 7.0 %copy-start.4 = (bf16[32,512]{1,0:T(8,128)(2,1)S(1)}, bf16[32,512]{1,0:T(8,128)(2,1)}, u32[]{:S(2)}) copy-start(bf16[32,512]{1,0:T(8,128)(2,1)} %param.8) | copy-start | bytes 98308
  323.5 2.2 copy-start.2
  326.7 1.8 copy-start.3
  330.4 2.2 copy-start.2
  333.6 1.8 copy-start.3
  337.4 2.2 copy-start.2
  340.5 1.8 copy-start.3
  344.3 2.2 copy-start.2
  347.5 1.8 copy-start.3
  351.2 2.2 copy-start.2
  354.4 1.8 copy-start.3
  358.1 2.2 copy-start.2
  361.3 1.8 copy-start.3
  365.0 2.2 copy-start.2
  368.2 1.8 copy-start.3
  371.9 2.2 copy-start.2
  375.1 1.8 copy-start.3
Sparse Core Ops, SparseCore 0:
  9.1 78.9 all-gather.1
where the time goes:
time: 388 us
  blocking collectives  297 us (77%)
  local copies, waits for them, and re-layouts  36.6 us (9%)
  matrix products  26.7 us (7%)
  between operations  13.4 us (3%)
  other arithmetic  12.9 us (3%)
    psum x1, blocking collectives, local(): act_rot = lax.psum(act_part, 'col').astype(jnp.bfloat16)  174 us
    psum x1, blocking collectives, local(): grad_rot = lax.psum(grad_part, 'row').astype(jnp.bfloat16)  86.3 us
    all_gather x1, blocking collectives, local(): lax.all_gather(act_grads, 'col', axis=0, tiled=True)  36.6 us
    dot_general x8, matrix products, step(): jnp.einsum('eki,ekj->eij', grad_rows, act_rows, preferred_element_type=jn...  17.6 us
    while x32, local copies, waits for them, and re-layouts  14.7 us
    dot_general x1, matrix products, local(): jnp.dot(lax.all_gather(activations, 'row', axis=0, tiled=True), eigen_act...  8.66 us
  transfers between devices with their start and end apart: 1, of which 0 were waited for; matrix products, arithmetic and copies ran while one was open for 2% of the time, Pallas kernels for 0%

commit v1 on v0

v1 whole, which is shorter than its diff:
```python
import jax
import jax.numpy as jnp
from jax import lax
from jax.sharding import Mesh, PartitionSpec as P

MOST_LEN = 32
ROW = ("zl", "y")
COL = ("x", "zh", "core")
F32 = jnp.float32
BF16 = jnp.bfloat16


def shifts(size, by):
    return [(i, (i + by) % size) for i in range(size)]


def swaps(size, by):
    return [(i, i ^ by) for i in range(size)]


def dot(a, b):
    return jnp.dot(a, b, preferred_element_type=F32)


def gather_grads(act_grads):
    pair = jnp.stack([act_grads, lax.ppermute(act_grads, "core", swaps(2, 1))])
    quad = jnp.stack([pair, lax.ppermute(pair, "zh", swaps(2, 1))])
    parts = [quad] + [lax.ppermute(quad, "x", shifts(4, s)) for s in (1, 2, 3)]
    return jnp.stack(parts).reshape(-1, act_grads.shape[1])


def grad_blocks(x, zh, core):
    return jnp.array(
        [((x - s) % 4) * 4 + (zh ^ h) * 2 + (core ^ c) for s in range(4) for h in range(2) for c in range(2)]
    )


def sum_grads(part, y, zl):
    blocks = part.reshape(4, 4, -1, part.shape[1])
    piece = lambda a, i: lax.dynamic_index_in_dim(a, i % 4, 0, False)
    total = piece(blocks, y)
    for s in (1, 2, 3):
        total = total + lax.ppermute(piece(blocks, y + s), "y", shifts(4, s))
    own = piece(total, zl)
    for s in (1, 2, 3):
        own = own + lax.ppermute(piece(total, zl ^ s), "zl", swaps(4, s))
    own = own.astype(BF16)
    line = jnp.stack([own] + [lax.ppermute(own, "zl", swaps(4, s)) for s in (1, 2, 3)])
    ring = jnp.stack([line] + [lax.ppermute(line, "y", shifts(4, s)) for s in (1, 2, 3)])
    return ring.reshape(-1, part.shape[1])


def local(activations, act_grads, eigen_act, eigen_grad, example_ids):
    zl, y, x, zh, core = (lax.axis_index(name) for name in ("zl", "y", "x", "zh", "core"))
    half = eigen_act.shape[1] // 2
    eigen_own = lax.dynamic_slice_in_dim(eigen_act, core * half, half, 1)
    eigen_other = lax.dynamic_slice_in_dim(eigen_act, (1 - core) * half, half, 1)

    with jax.named_scope("gather_line"):
        line = jnp.concatenate([activations] + [lax.ppermute(activations, "zl", swaps(4, s)) for s in (1, 2, 3)])
    with jax.named_scope("gather_grads"):
        grads = gather_grads(act_grads)

    pairs = []
    for s in (1, 2, 3, 0):
        with jax.named_scope("rotate"):
            route = [(j * 4 + i, (j + i + s) % 4 * 4 + i) for j in range(4) for i in range(4)]
            rows = lax.ppermute(line, ("y", "x"), route)
            away = dot(rows, eigen_other).astype(BF16)
            pair = dot(rows, eigen_own) + lax.ppermute(away, "core", swaps(2, 1)).astype(F32)
        with jax.named_scope("sum_ring"):
            pairs.append(lax.ppermute(pair.astype(BF16), "x", shifts(4, s)).astype(F32) if s else pair)
    with jax.named_scope("sum_far"):
        total = pairs[3] + pairs[0] + pairs[1] + pairs[2]
        total = total + lax.ppermute(total.astype(BF16), "zh", swaps(2, 1)).astype(F32)
        mine = total.astype(BF16)
    with jax.named_scope("gather_ring"):
        own = jnp.concatenate([mine] + [lax.ppermute(mine, "x", shifts(4, s)) for s in (1, 2, 3)])
        other = lax.ppermute(own, "core", swaps(2, 1))
        act_rot = jnp.concatenate([jnp.where(core == 0, own, other), jnp.where(core == 0, other, own)], axis=1)

    with jax.named_scope("sum_grads"):
        grad_rot = sum_grads(dot(grads, eigen_grad), y, zl)

    with jax.named_scope("slots"):
        tokens = example_ids.shape[0]
        examples = tokens // 16
        step = tokens // 16
        act_block = jnp.array([(zl ^ h) * 4 + (y - x + s) % 4 for s in range(4) for h in range(4)])
        blocks = grad_blocks(x, zh, core)
        grad_block = jnp.concatenate(
            [blocks[None, ((y - s) % 4) * 4 + (zl ^ h)] for s in range(4) for h in range(4)]
        )
        within = jnp.arange(step)
        act_token = (act_block[:, None] * step + within).reshape(-1)
        grad_token = (grad_block[:, None] * step + within).reshape(-1)
        bounds = jnp.sum(example_ids[None, :] < jnp.arange(examples + 1)[:, None], axis=1)
        slot = bounds[:-1, None] + jnp.arange(MOST_LEN)
        slot = jnp.where(slot < bounds[1:, None], slot, -1).reshape(-1, 1)
        take_act = (slot == act_token).astype(BF16)
        take_grad = (slot == grad_token).astype(BF16)
    with jax.named_scope("squares"):
        act_rows = dot(take_act, act_rot).astype(BF16).reshape(examples, MOST_LEN, -1)
        grad_rows = dot(take_grad, grad_rot).astype(BF16).reshape(examples, MOST_LEN, -1)
        blocks = jnp.einsum("eki,ekj->eij", grad_rows, act_rows, preferred_element_type=F32)
        return jnp.sum(blocks * blocks * (1 / examples), axis=0)


def solution(mesh):
    fine = Mesh(mesh.devices.reshape(4, 4, 4, 2, 2), ROW + COL)
    in_specs = (P(ROW, COL), P(COL, ROW), P(COL, ROW), P(ROW, COL), P())
    return jax.shard_map(local, mesh=fine, in_specs=in_specs, out_specs=P(COL, ROW), check_vma=False)
```

time: 388 us -> 145 us (0.37)
  the two profiles are of different devices: /device:TPU:80 before, /device:TPU:1 now
where the time goes in v1:
time: 145 us; the launch traced here: 144 us
  starting transfers between devices  66.6 us (46%)
  matrix products  31.8 us (22%)
  waiting for transfers between devices  30.3 us (21%)
  local copies, waits for them, and re-layouts  12.4 us (9%)
  other arithmetic  2.48 us (2%)
    dot_general x1, matrix products, local(): jnp.einsum('eki,ekj->eij', grad_rows, act_rows, preferred_element_type=F32)  19.3 us
    dot_general x11, matrix products, dot(): return jnp.dot(a, b, preferred_element_type=F32)  12.6 us
    concatenate x1, local copies, waits for them, and re-layouts, local(): jnp.concatenate([blocks[None, (y - s) % 4 * 4 + (zl ^ h)] for s in range(...  9.94 us
    ppermute x3, starting transfers between devices, local(): lax.ppermute(pair.astype(BF16), 'x', shifts(4, s)).astype(F32)  9.04 us
    ppermute x4, starting transfers between devices, local(): rows = lax.ppermute(line, ('y', 'x'), route)  8.69 us
    ppermute x4, waiting for transfers between devices, local(): rows = lax.ppermute(line, ('y', 'x'), route)  7.58 us
    ppermute x1, starting transfers between devices, gather_grads(): quad = jnp.stack([pair, lax.ppermute(pair, 'zh', swaps(2, 1))])  6.19 us
    ppermute x3, waiting for transfers between devices, sum_grads(): own = own + lax.ppermute(piece(total, zl ^ s), 'zl', swaps(4, s))  6.19 us
  transfers between devices with their start and end apart: 36, of which 11 were waited for; matrix products, arithmetic and copies ran while one was open for 17% of the time, Pallas kernels for 0%

profile of v1, /device:TPU:1, one launch (start us, length us, event | category | flops | bytes accessed | tf_op | source)
XLA Modules:
  0.0 144.1 jit_solution(2135654346397050291)
XLA Ops:
  0.0 3.8 %collective-permute-start.18 = (bf16[32,1792]{1,0:T(8,128)(2,1)}, bf16[32,1792]{1,0:T(8,128)(2,1)S(1)}, u32[]{:S(2)}, u32[]{:S(2)}) collective-permute-start(bf16[32,1792]{1,0:T(8,128)(2,1)} %param.5), channel_id=1, source_target_pairs={{0,128},{64,192},{128,0},{192,64},{1,129},{65,193},{129,1},{193,65... | collective-permute-start | bytes 344072 | tf_op jit(solution)/shard_map/gather_line/ppermute | solution.py:60
  3.8 1.6 %collective-permute-start.17 = (bf16[32,1792]{1,0:T(8,128)(2,1)}, bf16[32,1792]{1,0:T(8,128)(2,1)S(1)}, u32[]{:S(2)}, u32[]{:S(2)}) collective-permute-start(bf16[32,1792]{1,0:T(8,128)(2,1)} %param.5), channel_id=1, source_target_pairs={{0,64},{64,0},{128,192},{192,128},{1,65},{65,1},{129,193},{193,129... | collective-permute-start | bytes 344072 | tf_op jit(solution)/shard_map/gather_line/ppermute | solution.py:60
  5.5 2.2 %collective-permute-start = (bf16[32,512]{1,0:T(8,128)(2,1)}, bf16[32,512]{1,0:T(8,128)(2,1)S(1)}, u32[]{:S(2)}, u32[]{:S(2)}) collective-permute-start(bf16[32,512]{1,0:T(8,128)(2,1)} %param.6), channel_id=1, source_target_pairs={{0,1},{1,0},{2,3},{3,2},{4,5},{5,4},{6,7},{7,6},{8,9},{9,8},{10,11... | collective-permute-start | bytes 98312 | tf_op jit(solution)/shard_map/gather_grads/ppermute | solution.py:26
  10.5 9.9 %concatenate.60 = s32[16]{0:T(128)S(1)} concatenate(s32[1]{0:T(128)} %get-tuple-element.34, s32[1]{0:T(128)} %get-tuple-element.33, s32[1]{0:T(128)} %get-tuple-element.32, s32[1]{0:T(128)} %get-tuple-element.31, s32[1]{0:T(128)} %get-tuple-element.30, s32[1]{0:T(128)} %get-tuple-element.29, s32[1]{0:T(128)} %get-tuple-element.28, s32[1]{0:T(128)} %get-tuple-element.27, ...), dimensions={0} | concatenate | bytes 128 | tf_op jit(solution)/shard_map/slots/concatenate | solution.py:91
  20.6 3.7 %collective-permute-start.28 = (bf16[128,1792]{1,0:T(8,128)(2,1)S(1)}, bf16[128,1792]{1,0:T(8,128)(2,1)S(1)}, u32[]{:S(2)}, u32[]{:S(2)}) collective-permute-start(bf16[128,1792]{1,0:T(8,128)(2,1)S(1)} %constant_dynamic-update-slice_fusion), channel_id=1, source_target_pairs={{0,48},{4,4},{8,24},{12,44},{16,0},{20,20},{24,40},{28,60},{32,16}... | collective-permute-start | bytes 1376264 | tf_op jit(solution)/shard_map/rotate/ppermute | solution.py:68
  25.1 6.2 %collective-permute-start.1 = (bf16[2,32,512]{2,1,0:T(8,128)(2,1)S(1)}, bf16[2,32,512]{2,1,0:T(8,128)(2,1)S(1)}, u32[]{:S(2)}, u32[]{:S(2)}) collective-permute-start(bf16[2,32,512]{2,1,0:T(8,128)(2,1)S(1)} %get-tuple-element.16), channel_id=1, source_target_pairs={{0,2},{2,0},{1,3},{3,1},{4,6},{6,4},{5,7},{7,5},{8,10},{10,8},{9,1... | collective-permute-start | bytes 196616 | tf_op jit(solution)/shard_map/gather_grads/ppermute | solution.py:27
  31.3 2.2 %collective-permute-start.25 = (bf16[128,1792]{1,0:T(8,128)(2,1)S(1)}, bf16[128,1792]{1,0:T(8,128)(2,1)S(1)}, u32[]{:S(2)}, u32[]{:S(2)}) collective-permute-start(bf16[128,1792]{1,0:T(8,128)(2,1)S(1)} %constant_dynamic-update-slice_fusion), channel_id=1, source_target_pairs={{0,32},{4,52},{8,8},{12,28},{16,48},{20,4},{24,24},{28,44},{32,0},... | collective-permute-start | bytes 1376264 | tf_op jit(solution)/shard_map/rotate/ppermute | solution.py:68
  33.7 2.8 %collective-permute-start.4 = (bf16[2,2,32,512]{3,2,1,0:T(8,128)(2,1)S(1)}, bf16[2,2,32,512]{3,2,1,0:T(8,128)(2,1)S(1)}, u32[]{:S(2)}, u32[]{:S(2)}) collective-permute-start(bf16[2,2,32,512]{3,2,1,0:T(8,128)(2,1)S(1)} %pad_maximum_fusion.2), channel_id=1, source_target_pairs={{0,12},{4,0},{8,4},{12,8},{1,13},{5,1},{9,5},{13,9},{2,14},{6,2},{... | collective-permute-start | bytes 393224 | tf_op jit(solution)/shard_map/gather_grads/ppermute | solution.py:28
  37.2 2.1 %collective-permute-start.22 = (bf16[128,1792]{1,0:T(8,128)(2,1)S(1)}, bf16[128,1792]{1,0:T(8,128)(2,1)S(1)}, u32[]{:S(2)}, u32[]{:S(2)}) collective-permute-start(bf16[128,1792]{1,0:T(8,128)(2,1)S(1)} %constant_dynamic-update-slice_fusion), channel_id=1, source_target_pairs={{0,16},{4,36},{8,56},{12,12},{16,32},{20,52},{24,8},{28,28},{32,48... | collective-permute-start | bytes 1376264 | tf_op jit(solution)/shard_map/rotate/ppermute | solution.py:68
  39.2 2.6 %fusion.55 = bf16[128,896]{1,0:T(8,128)(2,1)S(1)} fusion(bf16[128,1792]{1,0:T(8,128)(2,1)S(1)} %collective-permute-done.28, bf16[1792,1792]{1,0:T(8,128)(2,1)} %param.7, s32[]{:T(128)S(6)} %select_n.299), kind=kOutput, calls=%fused_computation.35 | convolution fusion | flops 411156480 | bytes 3899396 | tf_op jit(solution)/shard_map/rotate/dot_general | solution.py:22
  41.8 4.4 %collective-permute-done.25 = bf16[128,1792]{1,0:T(8,128)(2,1)S(1)} collective-permute-done((bf16[128,1792]{1,0:T(8,128)(2,1)S(1)}, bf16[128,1792]{1,0:T(8,128)(2,1)S(1)}, u32[]{:S(2)}, u32[]{:S(2)}) %collective-permute-start.25) | collective-permute-done | bytes 458784 | tf_op jit(solution)/shard_map/rotate/ppermute | solution.py:68
  46.8 2.6 %fusion.52 = bf16[128,896]{1,0:T(8,128)(2,1)S(1)} fusion(bf16[128,1792]{1,0:T(8,128)(2,1)S(1)} %collective-permute-done.25, bf16[1792,1792]{1,0:T(8,128)(2,1)} %param.7, s32[]{:T(128)S(6)} %select_n.299), kind=kOutput, calls=%fused_computation.34 | convolution fusion | flops 411156480 | bytes 3899396 | tf_op jit(solution)/shard_map/rotate/dot_general | solution.py:22
  49.4 3.2 %collective-permute-done.22 = bf16[128,1792]{1,0:T(8,128)(2,1)S(1)} collective-permute-done((bf16[128,1792]{1,0:T(8,128)(2,1)S(1)}, bf16[128,1792]{1,0:T(8,128)(2,1)S(1)}, u32[]{:S(2)}, u32[]{:S(2)}) %collective-permute-start.22) | collective-permute-done | bytes 458784 | tf_op jit(solution)/shard_map/rotate/ppermute | solution.py:68
  52.6 4.8 %collective-permute-start.29 = (bf16[128,896]{1,0:T(8,128)(2,1)S(1)}, bf16[128,896]{1,0:T(8,128)(2,1)S(1)}, u32[]{:S(2)}, u32[]{:S(2)}) collective-permute-start(bf16[128,896]{1,0:T(8,128)(2,1)S(1)} %fusion.55), channel_id=1, source_target_pairs={{0,1},{1,0},{2,3},{3,2},{4,5},{5,4},{6,7},{7,6},{8,9},{9,8},{10,11... | collective-permute-start | bytes 688136 | tf_op jit(solution)/shard_map/rotate/ppermute | solution.py:70
  61.1 5.2 %collective-permute-start.30 = (bf16[128,896]{1,0:T(8,128)(2,1)S(1)}, bf16[128,896]{1,0:T(8,128)(2,1)S(1)}, u32[]{:S(2)}, u32[]{:S(2)}) collective-permute-start(bf16[128,896]{1,0:T(8,128)(2,1)S(1)} %fusion.58), channel_id=1, source_target_pairs={{0,12},{4,0},{8,4},{12,8},{1,13},{5,1},{9,5},{13,9},{2,14},{6,2},{... | collective-permute-start | bytes 688136 | tf_op jit(solution)/shard_map/sum_ring/ppermute | solution.py:72
  67.0 3.9 %collective-permute-start.27 = (bf16[128,896]{1,0:T(8,128)(2,1)S(1)}, bf16[128,896]{1,0:T(8,128)(2,1)S(1)}, u32[]{:S(2)}, u32[]{:S(2)}) collective-permute-start(bf16[128,896]{1,0:T(8,128)(2,1)S(1)} %fusion.61), channel_id=1, source_target_pairs={{0,8},{4,12},{8,0},{12,4},{1,9},{5,13},{9,1},{13,5},{2,10},{6,14},... | collective-permute-start | bytes 688136 | tf_op jit(solution)/shard_map/sum_ring/ppermute | solution.py:72
  71.6 2.6 %collective-permute-start.7 = (f32[4,32,512]{2,1,0:T(8,128)S(1)}, f32[4,32,512]{2,1,0:T(8,128)S(1)}, u32[]{:S(2)}, u32[]{:S(2)}) collective-permute-start(f32[4,32,512]{2,1,0:T(8,128)S(1)} %get-tuple-element.8), channel_id=1, source_target_pairs={{0,48},{16,0},{32,16},{48,32},{1,49},{17,1},{33,17},{49,33},{2,50}... | collective-permute-start | bytes 786440 | tf_op jit(solution)/shard_map/sum_grads/ppermute | solution.py:43
  76.7 5.2 %collective-permute-done.24 = bf16[128,896]{1,0:T(8,128)(2,1)S(1)} collective-permute-done((bf16[128,896]{1,0:T(8,128)(2,1)S(1)}, bf16[128,896]{1,0:T(8,128)(2,1)S(1)}, u32[]{:S(2)}, u32[]{:S(2)}) %collective-permute-start.24) | collective-permute-done | bytes 229408 | tf_op jit(solution)/shard_map/sum_ring/ppermute | solution.py:72
  82.6 4.7 %collective-permute-start.31 = (bf16[128,896]{1,0:T(8,128)(2,1)S(1)}, bf16[128,896]{1,0:T(8,128)(2,1)S(1)}, u32[]{:S(2)}, u32[]{:S(2)}) collective-permute-start(bf16[128,896]{1,0:T(8,128)(2,1)S(1)} %get-tuple-element.35), channel_id=1, source_target_pairs={{0,2},{2,0},{1,3},{3,1},{4,6},{6,4},{5,7},{7,5},{8,10},{10,8},{9,1... | collective-permute-start | bytes 688136 | tf_op jit(solution)/shard_map/sum_far/ppermute | solution.py:75
  87.5 1.7 %collective-permute-start.10 = (f32[32,512]{1,0:T(8,128)S(1)}, f32[32,512]{1,0:T(8,128)S(1)}, u32[]{:S(2)}, u32[]{:S(2)}) collective-permute-start(f32[32,512]{1,0:T(8,128)S(1)} %get-tuple-element.11), channel_id=1, source_target_pairs={{0,192},{64,128},{128,64},{192,0},{1,193},{65,129},{129,65},{193,1... | collective-permute-start | bytes 196616 | tf_op jit(solution)/shard_map/sum_grads/ppermute | solution.py:46
  90.2 5.7 %collective-permute-done.31 = bf16[128,896]{1,0:T(8,128)(2,1)S(1)} collective-permute-done((bf16[128,896]{1,0:T(8,128)(2,1)S(1)}, bf16[128,896]{1,0:T(8,128)(2,1)S(1)}, u32[]{:S(2)}, u32[]{:S(2)}) %collective-permute-start.31) | collective-permute-done | bytes 229408 | tf_op jit(solution)/shard_map/sum_far/ppermute | solution.py:75
  96.0 2.0 %collective-permute-start.33 = (bf16[128,896]{1,0:T(8,128)(2,1)S(1)}, bf16[128,896]{1,0:T(8,128)(2,1)S(1)}, u32[]{:S(2)}, u32[]{:S(2)}) collective-permute-start(bf16[128,896]{1,0:T(8,128)(2,1)S(1)} %add_convert_fusion), channel_id=1, source_target_pairs={{0,8},{4,12},{8,0},{12,4},{1,9},{5,13},{9,1},{13,5},{2,10},{6,14},... | collective-permute-start | bytes 688136 | tf_op jit(solution)/shard_map/gather_ring/ppermute | solution.py:78
  98.7 2.8 %collective-permute-done.10 = f32[32,512]{1,0:T(8,128)S(1)} collective-permute-done((f32[32,512]{1,0:T(8,128)S(1)}, f32[32,512]{1,0:T(8,128)S(1)}, u32[]{:S(2)}, u32[]{:S(2)}) %collective-permute-start.10) | collective-permute-done | bytes 65568 | tf_op jit(solution)/shard_map/sum_grads/ppermute | solution.py:46
  101.5 2.7 %collective-permute-done.9 = f32[32,512]{1,0:T(8,128)S(1)} collective-permute-done((f32[32,512]{1,0:T(8,128)S(1)}, f32[32,512]{1,0:T(8,128)S(1)}, u32[]{:S(2)}, u32[]{:S(2)}) %collective-permute-start.9) | collective-permute-done | bytes 65568 | tf_op jit(solution)/shard_map/sum_grads/ppermute | solution.py:46
  104.2 1.7 %collective-permute-start.13 = (bf16[32,512]{1,0:T(8,128)(2,1)S(1)}, bf16[32,512]{1,0:T(8,128)(2,1)S(1)}, u32[]{:S(2)}, u32[]{:S(2)}) collective-permute-start(bf16[32,512]{1,0:T(8,128)(2,1)S(1)} %fusion.84), channel_id=1, source_target_pairs={{0,192},{64,128},{128,64},{192,0},{1,193},{65,129},{129,65},{193,1... | collective-permute-start | bytes 98312 | tf_op jit(solution)/shard_map/sum_grads/ppermute | solution.py:48
  106.0 1.9 %collective-permute-start.11 = (bf16[32,512]{1,0:T(8,128)(2,1)S(1)}, bf16[32,512]{1,0:T(8,128)(2,1)S(1)}, u32[]{:S(2)}, u32[]{:S(2)}) collective-permute-start(bf16[32,512]{1,0:T(8,128)(2,1)S(1)} %fusion.84), channel_id=1, source_target_pairs={{0,64},{64,0},{128,192},{192,128},{1,65},{65,1},{129,193},{193,129... | collective-permute-start | bytes 98312 | tf_op jit(solution)/shard_map/sum_grads/ppermute | solution.py:48
  107.9 3.3 %collective-permute-start.35 = (bf16[512,896]{1,0:T(8,128)(2,1)S(1)}, bf16[512,896]{1,0:T(8,128)(2,1)S(1)}, u32[]{:S(2)}, u32[]{:S(2)}) collective-permute-start(bf16[512,896]{1,0:T(8,128)(2,1)S(1)} %pad_maximum_fusion), channel_id=1, source_target_pairs={{0,1},{1,0},{2,3},{3,2},{4,5},{5,4},{6,7},{7,6},{8,9},{9,8},{10,11... | collective-permute-start | bytes 2752520 | tf_op jit(solution)/shard_map/gather_ring/ppermute | solution.py:79
  111.8 2.4 %collective-permute-start.15 = (bf16[4,32,512]{2,1,0:T(8,128)(2,1)S(1)}, bf16[4,32,512]{2,1,0:T(8,128)(2,1)S(1)}, u32[]{:S(2)}, u32[]{:S(2)}) collective-permute-start(bf16[4,32,512]{2,1,0:T(8,128)(2,1)S(1)} %get-tuple-element.14), channel_id=1, source_target_pairs={{0,32},{16,48},{32,0},{48,16},{1,33},{17,49},{33,1},{49,17},{2,34}... | collective-permute-start | bytes 393224 | tf_op jit(solution)/shard_map/sum_grads/ppermute | solution.py:49
  115.0 1.9 %collective-permute-start.16 = (bf16[4,32,512]{2,1,0:T(8,128)(2,1)S(1)}, bf16[4,32,512]{2,1,0:T(8,128)(2,1)S(1)}, u32[]{:S(2)}, u32[]{:S(2)}) collective-permute-start(bf16[4,32,512]{2,1,0:T(8,128)(2,1)S(1)} %get-tuple-element.14), channel_id=1, source_target_pairs={{0,48},{16,0},{32,16},{48,32},{1,49},{17,1},{33,17},{49,33},{2,50}... | collective-permute-start | bytes 393224 | tf_op jit(solution)/shard_map/sum_grads/ppermute | solution.py:49
  118.5 3.0 %collective-permute-done.14 = bf16[4,32,512]{2,1,0:T(8,128)(2,1)S(1)} collective-permute-done((bf16[4,32,512]{2,1,0:T(8,128)(2,1)S(1)}, bf16[4,32,512]{2,1,0:T(8,128)(2,1)S(1)}, u32[]{:S(2)}, u32[]{:S(2)}) %collective-permute-start.14) | collective-permute-done | bytes 131104 | tf_op jit(solution)/shard_map/sum_grads/ppermute | solution.py:49
  122.6 2.1 %convolution_convert_fusion = bf16[1024,1792]{1,0:T(8,128)(2,1)S(1)} fusion(bf16[512,896]{1,0:T(8,128)(2,1)S(1)} %get-tuple-element.6, bf16[512,896]{1,0:T(8,128)(2,1)S(1)} %get-tuple-element.5, s32[512]{0:T(512)S(1)} %add.608, s32[1024]{0:T(1024)S(1)} %compare_select_fusion), kind=kOutput, calls=%fused_computation.1 | convolution fusion | flops 1885077504 | bytes 5511168 | tf_op jit(solution)/shard_map/squares/dot_general | solution.py:22
  124.8 19.3 %multiply_reduce_fusion = f32[512,1792]{1,0:T(8,128)} fusion(bf16[32,32,512]{2,1,0:T(8,128)(2,1)S(1)} %bitcast.111, bf16[32,32,1792]{2,1,0:T(8,128)(2,1)S(1)} %bitcast.110), kind=kOutput, calls=%fused_computation | convolution fusion | flops 1966211072 | bytes 8388608 | tf_op jit(solution)/shard_map/squares/eki,ekj->eij/dot_general | solution.py:105
  (88 shorter events, 19.4 us)
Async XLA Ops:
  0.0 20.5 %collective-permute-start.18 = (bf16[32,1792]{1,0:T(8,128)(2,1)}, bf16[32,1792]{1,0:T(8,128)(2,1)S(1)}, u32[]{:S(2)}, u32[]{:S(2)}) collective-permute-start(bf16[32,1792]{1,0:T(8,128)(2,1)} %param.5), channel_id=1, source_target_pairs={{0,128},{64,192},{128,0},{192,64},{1,129},{65,193},{129,1},{193,65... | collective-permute-start | bytes 344072 | tf_op jit(solution)/shard_map/gather_line/ppermute | solution.py:60
  3.8 16.7 %collective-permute-start.17 = (bf16[32,1792]{1,0:T(8,128)(2,1)}, bf16[32,1792]{1,0:T(8,128)(2,1)S(1)}, u32[]{:S(2)}, u32[]{:S(2)}) collective-permute-start(bf16[32,1792]{1,0:T(8,128)(2,1)} %param.5), channel_id=1, source_target_pairs={{0,64},{64,0},{128,192},{192,128},{1,65},{65,1},{129,193},{193,129... | collective-permute-start | bytes 344072 | tf_op jit(solution)/shard_map/gather_line/ppermute | solution.py:60
  5.5 15.1 %collective-permute-start.19 = (bf16[32,1792]{1,0:T(8,128)(2,1)}, bf16[32,1792]{1,0:T(8,128)(2,1)S(1)}, u32[]{:S(2)}, u32[]{:S(2)}) collective-permute-start(bf16[32,1792]{1,0:T(8,128)(2,1)} %param.5), channel_id=1, source_target_pairs={{0,192},{64,128},{128,64},{192,0},{1,193},{65,129},{129,65},{193,1... | collective-permute-start | bytes 344072 | tf_op jit(solution)/shard_map/gather_line/ppermute | solution.py:60
  5.5 18.8 %collective-permute-start = (bf16[32,512]{1,0:T(8,128)(2,1)}, bf16[32,512]{1,0:T(8,128)(2,1)S(1)}, u32[]{:S(2)}, u32[]{:S(2)}) collective-permute-start(bf16[32,512]{1,0:T(8,128)(2,1)} %param.6), channel_id=1, source_target_pairs={{0,1},{1,0},{2,3},{3,2},{4,5},{5,4},{6,7},{7,6},{8,9},{9,8},{10,11... | collective-permute-start | bytes 98312 | tf_op jit(solution)/shard_map/gather_grads/ppermute | solution.py:26
  20.6 16.6 %collective-permute-start.28 = (bf16[128,1792]{1,0:T(8,128)(2,1)S(1)}, bf16[128,1792]{1,0:T(8,128)(2,1)S(1)}, u32[]{:S(2)}, u32[]{:S(2)}) collective-permute-start(bf16[128,1792]{1,0:T(8,128)(2,1)S(1)} %constant_dynamic-update-slice_fusion), channel_id=1, source_target_pairs={{0,48},{4,4},{8,24},{12,44},{16,0},{20,20},{24,40},{28,60},{32,16}... | collective-permute-start | bytes 1376264 | tf_op jit(solution)/shard_map/rotate/ppermute | solution.py:68
  25.1 8.6 %collective-permute-start.1 = (bf16[2,32,512]{2,1,0:T(8,128)(2,1)S(1)}, bf16[2,32,512]{2,1,0:T(8,128)(2,1)S(1)}, u32[]{:S(2)}, u32[]{:S(2)}) collective-permute-start(bf16[2,32,512]{2,1,0:T(8,128)(2,1)S(1)} %get-tuple-element.16), channel_id=1, source_target_pairs={{0,2},{2,0},{1,3},{3,1},{4,6},{6,4},{5,7},{7,5},{8,10},{10,8},{9,1... | collective-permute-start | bytes 196616 | tf_op jit(solution)/shard_map/gather_grads/ppermute | solution.py:27
  31.3 14.9 %collective-permute-start.25 = (bf16[128,1792]{1,0:T(8,128)(2,1)S(1)}, bf16[128,1792]{1,0:T(8,128)(2,1)S(1)}, u32[]{:S(2)}, u32[]{:S(2)}) collective-permute-start(bf16[128,1792]{1,0:T(8,128)(2,1)S(1)} %constant_dynamic-update-slice_fusion), channel_id=1, source_target_pairs={{0,32},{4,52},{8,8},{12,28},{16,48},{20,4},{24,24},{28,44},{32,0},... | collective-permute-start | bytes 1376264 | tf_op jit(solution)/shard_map/rotate/ppermute | solution.py:68
  33.7 33.3 %collective-permute-start.4 = (bf16[2,2,32,512]{3,2,1,0:T(8,128)(2,1)S(1)}, bf16[2,2,32,512]{3,2,1,0:T(8,128)(2,1)S(1)}, u32[]{:S(2)}, u32[]{:S(2)}) collective-permute-start(bf16[2,2,32,512]{3,2,1,0:T(8,128)(2,1)S(1)} %pad_maximum_fusion.2), channel_id=1, source_target_pairs={{0,12},{4,0},{8,4},{12,8},{1,13},{5,1},{9,5},{13,9},{2,14},{6,2},{... | collective-permute-start | bytes 393224 | tf_op jit(solution)/shard_map/gather_grads/ppermute | solution.py:28
  36.5 34.4 %collective-permute-start.3 = (bf16[2,2,32,512]{3,2,1,0:T(8,128)(2,1)S(1)}, bf16[2,2,32,512]{3,2,1,0:T(8,128)(2,1)S(1)}, u32[]{:S(2)}, u32[]{:S(2)}) collective-permute-start(bf16[2,2,32,512]{3,2,1,0:T(8,128)(2,1)S(1)} %pad_maximum_fusion.2), channel_id=1, source_target_pairs={{0,8},{4,12},{8,0},{12,4},{1,9},{5,13},{9,1},{13,5},{2,10},{6,14},... | collective-permute-start | bytes 393224 | tf_op jit(solution)/shard_map/gather_grads/ppermute | solution.py:28
  36.5 34.4 %collective-permute-start.2 = (bf16[2,2,32,512]{3,2,1,0:T(8,128)(2,1)S(1)}, bf16[2,2,32,512]{3,2,1,0:T(8,128)(2,1)S(1)}, u32[]{:S(2)}, u32[]{:S(2)}) collective-permute-start(bf16[2,2,32,512]{3,2,1,0:T(8,128)(2,1)S(1)} %pad_maximum_fusion.2), channel_id=1, source_target_pairs={{0,4},{4,8},{8,12},{12,0},{1,5},{5,9},{9,13},{13,1},{2,6},{6,10},{... | collective-permute-start | bytes 393224 | tf_op jit(solution)/shard_map/gather_grads/ppermute | solution.py:28
  37.2 15.5 %collective-permute-start.22 = (bf16[128,1792]{1,0:T(8,128)(2,1)S(1)}, bf16[128,1792]{1,0:T(8,128)(2,1)S(1)}, u32[]{:S(2)}, u32[]{:S(2)}) collective-permute-start(bf16[128,1792]{1,0:T(8,128)(2,1)S(1)} %constant_dynamic-update-slice_fusion), channel_id=1, source_target_pairs={{0,16},{4,36},{8,56},{12,12},{16,32},{20,52},{24,8},{28,28},{32,48... | collective-permute-start | bytes 1376264 | tf_op jit(solution)/shard_map/rotate/ppermute | solution.py:68
  46.2 11.9 %collective-permute-start.20 = (bf16[128,1792]{1,0:T(8,128)(2,1)S(1)}, bf16[128,1792]{1,0:T(8,128)(2,1)S(1)}, u32[]{:S(2)}, u32[]{:S(2)}) collective-permute-start(bf16[128,1792]{1,0:T(8,128)(2,1)S(1)} %constant_dynamic-update-slice_fusion), channel_id=1, source_target_pairs={{0,0},{4,20},{8,40},{12,60},{16,16},{20,36},{24,56},{28,12},{32,32... | collective-permute-start | bytes 1376264 | tf_op jit(solution)/shard_map/rotate/ppermute | solution.py:68
  52.6 6.2 %collective-permute-start.29 = (bf16[128,896]{1,0:T(8,128)(2,1)S(1)}, bf16[128,896]{1,0:T(8,128)(2,1)S(1)}, u32[]{:S(2)}, u32[]{:S(2)}) collective-permute-start(bf16[128,896]{1,0:T(8,128)(2,1)S(1)} %fusion.55), channel_id=1, source_target_pairs={{0,1},{1,0},{2,3},{3,2},{4,5},{5,4},{6,7},{7,6},{8,9},{9,8},{10,11... | collective-permute-start | bytes 688136 | tf_op jit(solution)/shard_map/rotate/ppermute | solution.py:70
  60.1 11.4 %collective-permute-start.21 = (bf16[128,896]{1,0:T(8,128)(2,1)S(1)}, bf16[128,896]{1,0:T(8,128)(2,1)S(1)}, u32[]{:S(2)}, u32[]{:S(2)}) collective-permute-start(bf16[128,896]{1,0:T(8,128)(2,1)S(1)} %fusion.46), channel_id=1, source_target_pairs={{0,1},{1,0},{2,3},{3,2},{4,5},{5,4},{6,7},{7,6},{8,9},{9,8},{10,11... | collective-permute-start | bytes 688136 | tf_op jit(solution)/shard_map/rotate/ppermute | solution.py:70
  61.1 13.1 %collective-permute-start.30 = (bf16[128,896]{1,0:T(8,128)(2,1)S(1)}, bf16[128,896]{1,0:T(8,128)(2,1)S(1)}, u32[]{:S(2)}, u32[]{:S(2)}) collective-permute-start(bf16[128,896]{1,0:T(8,128)(2,1)S(1)} %fusion.58), channel_id=1, source_target_pairs={{0,12},{4,0},{8,4},{12,8},{1,13},{5,1},{9,5},{13,9},{2,14},{6,2},{... | collective-permute-start | bytes 688136 | tf_op jit(solution)/shard_map/sum_ring/ppermute | solution.py:72
  67.0 9.7 %collective-permute-start.27 = (bf16[128,896]{1,0:T(8,128)(2,1)S(1)}, bf16[128,896]{1,0:T(8,128)(2,1)S(1)}, u32[]{:S(2)}, u32[]{:S(2)}) collective-permute-start(bf16[128,896]{1,0:T(8,128)(2,1)S(1)} %fusion.61), channel_id=1, source_target_pairs={{0,8},{4,12},{8,0},{12,4},{1,9},{5,13},{9,1},{13,5},{2,10},{6,14},... | collective-permute-start | bytes 688136 | tf_op jit(solution)/shard_map/sum_ring/ppermute | solution.py:72
  70.9 11.0 %collective-permute-start.24 = (bf16[128,896]{1,0:T(8,128)(2,1)S(1)}, bf16[128,896]{1,0:T(8,128)(2,1)S(1)}, u32[]{:S(2)}, u32[]{:S(2)}) collective-permute-start(bf16[128,896]{1,0:T(8,128)(2,1)S(1)} %fusion.64), channel_id=1, source_target_pairs={{0,4},{4,8},{8,12},{12,0},{1,5},{5,9},{9,13},{13,1},{2,6},{6,10},{... | collective-permute-start | bytes 688136 | tf_op jit(solution)/shard_map/sum_ring/ppermute | solution.py:72
  71.4 15.9 %collective-permute-start.5 = (f32[4,32,512]{2,1,0:T(8,128)S(1)}, f32[4,32,512]{2,1,0:T(8,128)S(1)}, u32[]{:S(2)}, u32[]{:S(2)}) collective-permute-start(f32[4,32,512]{2,1,0:T(8,128)S(1)} %get-tuple-element.7), channel_id=1, source_target_pairs={{0,16},{16,32},{32,48},{48,0},{1,17},{17,33},{33,49},{49,1},{2,18}... | collective-permute-start | bytes 786440 | tf_op jit(solution)/shard_map/sum_grads/ppermute | solution.py:43
  71.6 15.7 %collective-permute-start.7 = (f32[4,32,512]{2,1,0:T(8,128)S(1)}, f32[4,32,512]{2,1,0:T(8,128)S(1)}, u32[]{:S(2)}, u32[]{:S(2)}) collective-permute-start(f32[4,32,512]{2,1,0:T(8,128)S(1)} %get-tuple-element.8), channel_id=1, source_target_pairs={{0,48},{16,0},{32,16},{48,32},{1,49},{17,1},{33,17},{49,33},{2,50}... | collective-permute-start | bytes 786440 | tf_op jit(solution)/shard_map/sum_grads/ppermute | solution.py:43
  74.3 13.0 %collective-permute-start.6 = (f32[4,32,512]{2,1,0:T(8,128)S(1)}, f32[4,32,512]{2,1,0:T(8,128)S(1)}, u32[]{:S(2)}, u32[]{:S(2)}) collective-permute-start(f32[4,32,512]{2,1,0:T(8,128)S(1)} %get-tuple-element.9), channel_id=1, source_target_pairs={{0,32},{16,48},{32,0},{48,16},{1,33},{17,49},{33,1},{49,17},{2,34}... | collective-permute-start | bytes 786440 | tf_op jit(solution)/shard_map/sum_grads/ppermute | solution.py:43
  82.6 13.3 %collective-permute-start.31 = (bf16[128,896]{1,0:T(8,128)(2,1)S(1)}, bf16[128,896]{1,0:T(8,128)(2,1)S(1)}, u32[]{:S(2)}, u32[]{:S(2)}) collective-permute-start(bf16[128,896]{1,0:T(8,128)(2,1)S(1)} %get-tuple-element.35), channel_id=1, source_target_pairs={{0,2},{2,0},{1,3},{3,1},{4,6},{6,4},{5,7},{7,5},{8,10},{10,8},{9,1... | collective-permute-start | bytes 688136 | tf_op jit(solution)/shard_map/sum_far/ppermute | solution.py:75
  87.4 11.2 %collective-permute-start.8 = (f32[32,512]{1,0:T(8,128)S(1)}, f32[32,512]{1,0:T(8,128)S(1)}, u32[]{:S(2)}, u32[]{:S(2)}) collective-permute-start(f32[32,512]{1,0:T(8,128)S(1)} %get-tuple-element.10), channel_id=1, source_target_pairs={{0,64},{64,0},{128,192},{192,128},{1,65},{65,1},{129,193},{193,129... | collective-permute-start | bytes 196616 | tf_op jit(solution)/shard_map/sum_grads/ppermute | solution.py:46
  87.5 14.0 %collective-permute-start.10 = (f32[32,512]{1,0:T(8,128)S(1)}, f32[32,512]{1,0:T(8,128)S(1)}, u32[]{:S(2)}, u32[]{:S(2)}) collective-permute-start(f32[32,512]{1,0:T(8,128)S(1)} %get-tuple-element.11), channel_id=1, source_target_pairs={{0,192},{64,128},{128,64},{192,0},{1,193},{65,129},{129,65},{193,1... | collective-permute-start | bytes 196616 | tf_op jit(solution)/shard_map/sum_grads/ppermute | solution.py:46
  89.2 15.0 %collective-permute-start.9 = (f32[32,512]{1,0:T(8,128)S(1)}, f32[32,512]{1,0:T(8,128)S(1)}, u32[]{:S(2)}, u32[]{:S(2)}) collective-permute-start(f32[32,512]{1,0:T(8,128)S(1)} %get-tuple-element.12), channel_id=1, source_target_pairs={{0,128},{64,192},{128,0},{192,64},{1,129},{65,193},{129,1},{193,65... | collective-permute-start | bytes 196616 | tf_op jit(solution)/shard_map/sum_grads/ppermute | solution.py:46
  96.0 10.0 %collective-permute-start.34 = (bf16[128,896]{1,0:T(8,128)(2,1)S(1)}, bf16[128,896]{1,0:T(8,128)(2,1)S(1)}, u32[]{:S(2)}, u32[]{:S(2)}) collective-permute-start(bf16[128,896]{1,0:T(8,128)(2,1)S(1)} %add_convert_fusion), channel_id=1, source_target_pairs={{0,12},{4,0},{8,4},{12,8},{1,13},{5,1},{9,5},{13,9},{2,14},{6,2},{... | collective-permute-start | bytes 688136 | tf_op jit(solution)/shard_map/gather_ring/ppermute | solution.py:78
  96.0 11.8 %collective-permute-start.33 = (bf16[128,896]{1,0:T(8,128)(2,1)S(1)}, bf16[128,896]{1,0:T(8,128)(2,1)S(1)}, u32[]{:S(2)}, u32[]{:S(2)}) collective-permute-start(bf16[128,896]{1,0:T(8,128)(2,1)S(1)} %add_convert_fusion), channel_id=1, source_target_pairs={{0,8},{4,12},{8,0},{12,4},{1,9},{5,13},{9,1},{13,5},{2,10},{6,14},... | collective-permute-start | bytes 688136 | tf_op jit(solution)/shard_map/gather_ring/ppermute | solution.py:78
  98.7 9.2 %collective-permute-start.32 = (bf16[128,896]{1,0:T(8,128)(2,1)S(1)}, bf16[128,896]{1,0:T(8,128)(2,1)S(1)}, u32[]{:S(2)}, u32[]{:S(2)}) collective-permute-start(bf16[128,896]{1,0:T(8,128)(2,1)S(1)} %add_convert_fusion), channel_id=1, source_target_pairs={{0,4},{4,8},{8,12},{12,0},{1,5},{5,9},{9,13},{13,1},{2,6},{6,10},{... | collective-permute-start | bytes 688136 | tf_op jit(solution)/shard_map/gather_ring/ppermute | solution.py:78
  104.2 7.5 %collective-permute-start.13 = (bf16[32,512]{1,0:T(8,128)(2,1)S(1)}, bf16[32,512]{1,0:T(8,128)(2,1)S(1)}, u32[]{:S(2)}, u32[]{:S(2)}) collective-permute-start(bf16[32,512]{1,0:T(8,128)(2,1)S(1)} %fusion.84), channel_id=1, source_target_pairs={{0,192},{64,128},{128,64},{192,0},{1,193},{65,129},{129,65},{193,1... | collective-permute-start | bytes 98312 | tf_op jit(solution)/shard_map/sum_grads/ppermute | solution.py:48
  107.9 14.3 %collective-permute-start.35 = (bf16[512,896]{1,0:T(8,128)(2,1)S(1)}, bf16[512,896]{1,0:T(8,128)(2,1)S(1)}, u32[]{:S(2)}, u32[]{:S(2)}) collective-permute-start(bf16[512,896]{1,0:T(8,128)(2,1)S(1)} %pad_maximum_fusion), channel_id=1, source_target_pairs={{0,1},{1,0},{2,3},{3,2},{4,5},{5,4},{6,7},{7,6},{8,9},{9,8},{10,11... | collective-permute-start | bytes 2752520 | tf_op jit(solution)/shard_map/gather_ring/ppermute | solution.py:79
  111.8 6.7 %collective-permute-start.15 = (bf16[4,32,512]{2,1,0:T(8,128)(2,1)S(1)}, bf16[4,32,512]{2,1,0:T(8,128)(2,1)S(1)}, u32[]{:S(2)}, u32[]{:S(2)}) collective-permute-start(bf16[4,32,512]{2,1,0:T(8,128)(2,1)S(1)} %get-tuple-element.14), channel_id=1, source_target_pairs={{0,32},{16,48},{32,0},{48,16},{1,33},{17,49},{33,1},{49,17},{2,34}... | collective-permute-start | bytes 393224 | tf_op jit(solution)/shard_map/sum_grads/ppermute | solution.py:49
  114.2 7.3 %collective-permute-start.14 = (bf16[4,32,512]{2,1,0:T(8,128)(2,1)S(1)}, bf16[4,32,512]{2,1,0:T(8,128)(2,1)S(1)}, u32[]{:S(2)}, u32[]{:S(2)}) collective-permute-start(bf16[4,32,512]{2,1,0:T(8,128)(2,1)S(1)} %get-tuple-element.14), channel_id=1, source_target_pairs={{0,16},{16,32},{32,48},{48,0},{1,17},{17,33},{33,49},{49,1},{2,18}... | collective-permute-start | bytes 393224 | tf_op jit(solution)/shard_map/sum_grads/ppermute | solution.py:49
  115.0 6.5 %collective-permute-start.16 = (bf16[4,32,512]{2,1,0:T(8,128)(2,1)S(1)}, bf16[4,32,512]{2,1,0:T(8,128)(2,1)S(1)}, u32[]{:S(2)}, u32[]{:S(2)}) collective-permute-start(bf16[4,32,512]{2,1,0:T(8,128)(2,1)S(1)} %get-tuple-element.14), channel_id=1, source_target_pairs={{0,48},{16,0},{32,16},{48,32},{1,49},{17,1},{33,17},{49,33},{2,50}... | collective-permute-start | bytes 393224 | tf_op jit(solution)/shard_map/sum_grads/ppermute | solution.py:49
  (6 other events, 110.5 us)

commit v2 on v1

v2 whole, which is shorter than its diff:
```python
import jax
import jax.numpy as jnp
from jax import lax
from jax.experimental import pallas as pl
from jax.experimental.pallas import tpu as pltpu
from jax.sharding import Mesh, PartitionSpec as P

MOST_LEN = 32
ROW = ("zl", "y")
COL = ("x", "zh", "core")
F32 = jnp.float32
BF16 = jnp.bfloat16


def shift(a, axis, by):
    return lax.ppermute(a, axis, [(i, (i + by) % 4) for i in range(4)])


def swap(a, axis, by=1):
    size = 2 if axis in ("zh", "core") else 4
    return lax.ppermute(a, axis, [(i, i ^ by) for i in range(size)])


def tie(*arrays):
    return lax.optimization_barrier(arrays)


def dot(a, b):
    return jnp.dot(a, b, preferred_element_type=F32)


def piece(a, i):
    return lax.dynamic_index_in_dim(a, i, 0, False)


def rotate_kernel(which_ref, rows_ref, eigen_ref, out_ref, sum_ref):
    step = pl.program_id(0)

    @pl.when(step == 0)
    def _():
        sum_ref[...] = dot(rows_ref[...], eigen_ref[...])

    @pl.when(step == 1)
    def _():
        out_ref[...] = (sum_ref[...] + dot(rows_ref[...], eigen_ref[...])).astype(out_ref.dtype)


def rotate(rows, eigen, which, dtype):
    tokens, depth = rows.shape
    half, deep = eigen.shape[1] // 2, depth // 2
    return pl.pallas_call(
        rotate_kernel,
        out_shape=jax.ShapeDtypeStruct((tokens, half), dtype),
        grid_spec=pltpu.PrefetchScalarGridSpec(
            num_scalar_prefetch=1,
            grid=(2,),
            in_specs=[
                pl.BlockSpec((tokens, deep), lambda k, w: (0, k)),
                pl.BlockSpec((deep, half), lambda k, w: (k, w[0])),
            ],
            out_specs=pl.BlockSpec((tokens, half), lambda k, w: (0, 0)),
            scratch_shapes=[pltpu.VMEM((tokens, half), F32)],
        ),
        compiler_params=pltpu.CompilerParams(vmem_limit_bytes=56 << 20),
        cost_estimate=pl.CostEstimate(flops=2 * tokens * depth * half, bytes_accessed=2 * depth * half, transcendentals=0),
        name="rotate",
    )(which.reshape(1), rows, eigen)


def local(activations, act_grads, eigen_act, eigen_grad, example_ids):
    zl, y, x, zh, core = (lax.axis_index(name) for name in ("zl", "y", "x", "zh", "core"))
    block = activations.shape[0]
    group = 4 * block

    with jax.named_scope("gather_line"):
        line = jnp.concatenate([activations, swap(activations, "zl", 1)])
        line = jnp.concatenate([line, swap(line, "zl", 2)])
    with jax.named_scope("gather_grads"):
        grads = jnp.concatenate([act_grads, swap(act_grads, "zh")])
        grads = jnp.concatenate([grads] + [shift(grads, "x", s) for s in (1, 2, 3)])
        grads = jnp.concatenate([grads, swap(grads, "core")])
    with jax.named_scope("sum_grads"):
        part = dot(grads, eigen_grad)
        line, part = tie(line, part)
        part = part + swap(part.astype(BF16), "zl", 2).astype(F32)
    with jax.named_scope("gather_plane"):
        ring = [line] + [shift(line, "y", s) for s in (1, 2, 3)]
        ring[1], ring[2], ring[3], part = tie(ring[1], ring[2], ring[3], part)
        tokens = jnp.concatenate(ring)
    with jax.named_scope("sum_grads"):
        part = part + swap(part.astype(BF16), "zl", 1).astype(F32)

    with jax.named_scope("rotate"):
        away = rotate(tokens, eigen_act, 1 - core, BF16)
        pair = rotate(tokens, eigen_act, core, F32) + swap(away, "core").astype(F32)
        pairs = [[pair.reshape(4, group, -1)]]
    totals = []
    for parts in pairs:
        with jax.named_scope("sum_ring"):
            at = lambda i: piece(parts[0], i % 4)
            total = at(x)
            for s in (1, 2, 3):
                total = total + shift(at(x + s).astype(BF16), "x", s).astype(F32)
        totals.append(total)
    totals[0], part = tie(totals[0], part)
    with jax.named_scope("sum_grads"):
        part = part + swap(part.astype(BF16), "y", 1).astype(F32)
    columns = []
    for total in totals:
        with jax.named_scope("sum_far"):
            mine = (total + swap(total.astype(BF16), "zh").astype(F32)).astype(BF16)
        if not columns:
            mine, part = tie(mine, part)
            with jax.named_scope("sum_grads"):
                grad_rot = (part + swap(part.astype(BF16), "y", 2).astype(F32)).astype(BF16)
        with jax.named_scope("gather_ring"):
            own = jnp.concatenate([mine] + [shift(mine, "x", s) for s in (1, 2, 3)])
            if not columns:
                own, grad_rot = tie(own, grad_rot)
            other = swap(own, "core")
            columns.append((jnp.where(core == 0, own, other), jnp.where(core == 0, other, own)))

    with jax.named_scope("slots"):
        examples = example_ids.shape[0] // 16
        row = lax.broadcasted_iota(jnp.int32, (1, example_ids.shape[0]), 1)
        within, outer, inner = row % block, row // group, row // block % 4
        act_token = ((zl ^ inner) * 4 + (y - x + outer) % 4) * block + within
        gathered = row // block
        from_x = (x - gathered // 2 % 4) % 4
        grad_token = (from_x * 4 + (zh ^ (gathered % 2)) * 2 + (core ^ (gathered // 8))) * block + within
        bounds = jnp.sum(example_ids[None, :] < jnp.arange(examples + 1)[:, None], axis=1)
        slot = bounds[:-1, None] + jnp.arange(MOST_LEN)
        slot = jnp.where(slot < bounds[1:, None], slot, -1).reshape(-1, 1)
        take_act = (slot == act_token).astype(BF16)
        take_grad = (slot == grad_token).astype(BF16)
    with jax.named_scope("squares"):
        grad_rows = dot(take_grad, grad_rot).astype(BF16).reshape(examples, MOST_LEN, -1)
        sums = [[], []]
        for two in columns:
            act_rows = dot(take_act, jnp.concatenate(two, axis=1)).astype(BF16).reshape(examples, MOST_LEN, -1)
            blocks = jnp.einsum("eki,ekj->eij", grad_rows, act_rows, preferred_element_type=F32)
            squares = jnp.sum(blocks * blocks * (1 / examples), axis=0)
            sums[0].append(squares[:, : two[0].shape[1]])
            sums[1].append(squares[:, two[0].shape[1] :])
        return jnp.concatenate(sums[0] + sums[1], axis=1)


def solution(mesh):
    fine = Mesh(mesh.devices.reshape(4, 4, 4, 2, 2), ROW + COL)
    in_specs = (P(ROW, COL), P(COL, ROW), P(COL, ROW), P(ROW, COL), P())
    return jax.shard_map(local, mesh=fine, in_specs=in_specs, out_specs=P(COL, ROW), check_vma=False)
```

time: 145 us -> 148 us (1.021)
  the two profiles are of different devices: /device:TPU:1 before, /device:TPU:33 now
where the time goes in v2:
time: 148 us; the launch traced here: 147 us
  waiting for transfers between devices  61.8 us (42%)
  starting transfers between devices  40.7 us (28%)
  matrix products  22.6 us (15%)
  Pallas kernels  10.5 us (7%)
  other arithmetic  8.18 us (6%)
  local copies, waits for them, and re-layouts  3.28 us (2%)
    ppermute x11, waiting for transfers between devices, swap(): return lax.ppermute(a, axis, [(i, i ^ by) for i in range(size)])  38.4 us
    ppermute x11, starting transfers between devices, swap(): return lax.ppermute(a, axis, [(i, i ^ by) for i in range(size)])  25.8 us
    ppermute x12, waiting for transfers between devices, shift(): return lax.ppermute(a, axis, [(i, (i + by) % 4) for i in range(4)])  23.4 us
    dot_general x1, matrix products, local(): jnp.einsum('eki,ekj->eij', grad_rows, act_rows, preferred_element_type=F32)  19.3 us
    ppermute x12, starting transfers between devices, shift(): return lax.ppermute(a, axis, [(i, (i + by) % 4) for i in range(4)])  14.9 us
    pallas_call x2, Pallas kernels, rotate(): pl.pallas_call(rotate_kernel, out_shape=jax.ShapeDtypeStruct((tokens, hal...  10.5 us
    dot_general x3, matrix products, dot(): return jnp.dot(a, b, preferred_element_type=F32)  3.33 us
  transfers between devices with their start and end apart: 23, of which 13 were waited for; matrix products, arithmetic and copies ran while one was open for 6% of the time, Pallas kernels for 4%

profile of v2, /device:TPU:33, one launch (start us, length us, event | category | flops | bytes accessed | tf_op | source)
XLA Modules:
  0.0 147.3 jit_solution(8462713301704391592)
XLA Ops:
  0.0 6.0 %collective-permute-start.2 = (bf16[32,512]{1,0:T(8,128)(2,1)}, bf16[32,512]{1,0:T(8,128)(2,1)S(1)}, u32[]{:S(2)}, u32[]{:S(2)}) collective-permute-start(bf16[32,512]{1,0:T(8,128)(2,1)} %param.6), channel_id=1, source_target_pairs={{0,2},{2,0},{1,3},{3,1},{4,6},{6,4},{5,7},{7,5},{8,10},{10,8},{9,1... | collective-permute-start | bytes 98312 | tf_op jit(solution)/shard_map/gather_grads/ppermute | solution.py:21
  7.5 1.3 collective-permute-start.3
  9.6 1.5 collective-permute-start.5
  11.0 1.5 %collective-permute-start.4 = (bf16[64,512]{1,0:T(8,128)(2,1)S(1)}, bf16[64,512]{1,0:T(8,128)(2,1)S(1)}, u32[]{:S(2)}, u32[]{:S(2)}) collective-permute-start(bf16[64,512]{1,0:T(8,128)(2,1)S(1)} %get-tuple-element.42), channel_id=1, source_target_pairs={{0,8},{4,12},{8,0},{12,4},{1,9},{5,13},{9,1},{13,5},{2,10},{6,14},... | collective-permute-start | bytes 196616 | tf_op jit(solution)/shard_map/gather_grads/ppermute | solution.py:16
  13.6 2.4 %collective-permute-start.1 = (bf16[64,1792]{1,0:T(8,128)(2,1)S(1)}, bf16[64,1792]{1,0:T(8,128)(2,1)S(1)}, u32[]{:S(2)}, u32[]{:S(2)}) collective-permute-start(bf16[64,1792]{1,0:T(8,128)(2,1)S(1)} %pad_maximum_fusion.2), channel_id=1, source_target_pairs={{0,128},{64,192},{128,0},{192,64},{1,129},{65,193},{129,1},{193,65... | collective-permute-start | bytes 688136 | tf_op jit(solution)/shard_map/gather_line/ppermute | solution.py:21
  16.1 3.7 %collective-permute-start.6 = (bf16[256,512]{1,0:T(8,128)(2,1)S(1)}, bf16[256,512]{1,0:T(8,128)(2,1)S(1)}, u32[]{:S(2)}, u32[]{:S(2)}) collective-permute-start(bf16[256,512]{1,0:T(8,128)(2,1)S(1)} %get-tuple-element.34), channel_id=1, source_target_pairs={{0,1},{1,0},{2,3},{3,2},{4,5},{5,4},{6,7},{7,6},{8,9},{9,8},{10,11... | collective-permute-start | bytes 786440 | tf_op jit(solution)/shard_map/gather_grads/ppermute | solution.py:21
  19.8 5.3 %collective-permute-done.1 = bf16[64,1792]{1,0:T(8,128)(2,1)S(1)} collective-permute-done((bf16[64,1792]{1,0:T(8,128)(2,1)S(1)}, bf16[64,1792]{1,0:T(8,128)(2,1)S(1)}, u32[]{:S(2)}, u32[]{:S(2)}) %collective-permute-start.1) | collective-permute-done | bytes 229408 | tf_op jit(solution)/shard_map/gather_line/ppermute | solution.py:21
  26.5 3.2 %collective-permute-start.10 = (bf16[512,512]{1,0:T(8,128)(2,1)S(1)}, bf16[512,512]{1,0:T(8,128)(2,1)}, u32[]{:S(2)}, u32[]{:S(2)}) collective-permute-start(bf16[512,512]{1,0:T(8,128)(2,1)S(1)} %convert_element_type.78), channel_id=1, source_target_pairs={{0,128},{64,192},{128,0},{192,64},{1,129},{65,193},{129,1},{193,65... | collective-permute-start | bytes 1572872 | tf_op jit(solution)/shard_map/sum_grads/ppermute | solution.py:21
  29.7 2.7 %collective-permute-start.9 = (bf16[128,1792]{1,0:T(8,128)(2,1)S(1)}, bf16[128,1792]{1,0:T(8,128)(2,1)S(1)}, u32[]{:S(2)}, u32[]{:S(2)}) collective-permute-start(bf16[128,1792]{1,0:T(8,128)(2,1)S(1)} %pad_maximum_fusion.1), channel_id=1, source_target_pairs={{0,48},{16,0},{32,16},{48,32},{1,49},{17,1},{33,17},{49,33},{2,50}... | collective-permute-start | bytes 1376264 | tf_op jit(solution)/shard_map/gather_plane/ppermute | solution.py:16
  33.5 17.5 %collective-permute-done.10 = bf16[512,512]{1,0:T(8,128)(2,1)} collective-permute-done((bf16[512,512]{1,0:T(8,128)(2,1)S(1)}, bf16[512,512]{1,0:T(8,128)(2,1)}, u32[]{:S(2)}, u32[]{:S(2)}) %collective-permute-start.10) | collective-permute-done | bytes 524320 | tf_op jit(solution)/shard_map/sum_grads/ppermute | solution.py:21
  51.0 1.2 convert_add_fusion.3
  52.2 4.0 %collective-permute-done.7 = bf16[128,1792]{1,0:T(8,128)(2,1)S(1)} collective-permute-done((bf16[128,1792]{1,0:T(8,128)(2,1)S(1)}, bf16[128,1792]{1,0:T(8,128)(2,1)S(1)}, u32[]{:S(2)}, u32[]{:S(2)}) %collective-permute-start.7) | collective-permute-done | bytes 458784 | tf_op jit(solution)/shard_map/gather_plane/ppermute | solution.py:16
  56.4 1.2 copy-done.1
  57.6 5.1 %rotate.3 = bf16[512,896]{1,0:T(8,128)(2,1)} custom-call(s32[1]{0:T(128)} %bitcast.1.which_ref, bf16[512,1792]{1,0:T(8,128)(2,1)} %copy-done.1, bf16[1792,1792]{1,0:T(8,128)(2,1)} %eigen_ref.3), custom_call_target="tpu_custom_call" | custom-call | flops 1644167168 | bytes 3211264 | tf_op jit(solution)/shard_map/rotate/rotate/pallas_call | solution.py:51
  63.5 5.4 %rotate.2 = f32[512,896]{1,0:T(8,128)} custom-call(s32[1]{0:T(128)} %bitcast.which_ref, bf16[512,1792]{1,0:T(8,128)(2,1)} %copy-done.1, bf16[1792,1792]{1,0:T(8,128)(2,1)} %eigen_ref.3), custom_call_target="tpu_custom_call" | custom-call | flops 1644167168 | bytes 3211264 | tf_op jit(solution)/shard_map/rotate/rotate/pallas_call | solution.py:51
  68.9 1.6 %convert_add_fusion = f32[512,896]{1,0:T(8,128)S(1)} fusion(f32[512,896]{1,0:T(8,128)} %rotate.2, bf16[512,896]{1,0:T(8,128)(2,1)S(1)} %collective-permute-done.11), kind=kLoop, calls=%fused_computation.8 | loop fusion | flops 917504 | bytes 4587520 | tf_op jit(solution)/shard_map/rotate/add | solution.py:95
  70.7 1.6 %collective-permute-start.12 = (bf16[128,896]{1,0:T(8,128)(2,1)S(1)}, bf16[128,896]{1,0:T(8,128)(2,1)S(1)}, u32[]{:S(2)}, u32[]{:S(2)}) collective-permute-start(bf16[128,896]{1,0:T(8,128)(2,1)S(1)} %get-tuple-element.31), channel_id=1, source_target_pairs={{0,4},{4,8},{8,12},{12,0},{1,5},{5,9},{9,13},{13,1},{2,6},{6,10},{... | collective-permute-start | bytes 688136 | tf_op jit(solution)/shard_map/sum_ring/ppermute | solution.py:16
  72.2 1.2 collective-permute-start.14
  73.4 1.5 %collective-permute-start.13 = (bf16[128,896]{1,0:T(8,128)(2,1)S(1)}, bf16[128,896]{1,0:T(8,128)(2,1)S(1)}, u32[]{:S(2)}, u32[]{:S(2)}) collective-permute-start(bf16[128,896]{1,0:T(8,128)(2,1)S(1)} %get-tuple-element.33), channel_id=1, source_target_pairs={{0,8},{4,12},{8,0},{12,4},{1,9},{5,13},{9,1},{13,5},{2,10},{6,14},... | collective-permute-start | bytes 688136 | tf_op jit(solution)/shard_map/sum_ring/ppermute | solution.py:16
  74.9 2.1 %collective-permute-done.15 = bf16[512,512]{1,0:T(8,128)(2,1)S(1)} collective-permute-done((bf16[512,512]{1,0:T(8,128)(2,1)S(1)}, bf16[512,512]{1,0:T(8,128)(2,1)S(1)}, u32[]{:S(2)}, u32[]{:S(2)}) %collective-permute-start.15) | collective-permute-done | bytes 524320 | tf_op jit(solution)/shard_map/sum_grads/ppermute | solution.py:21
  77.2 2.0 %collective-permute-done.12 = bf16[128,896]{1,0:T(8,128)(2,1)S(1)} collective-permute-done((bf16[128,896]{1,0:T(8,128)(2,1)S(1)}, bf16[128,896]{1,0:T(8,128)(2,1)S(1)}, u32[]{:S(2)}, u32[]{:S(2)}) %collective-permute-start.12) | collective-permute-done | bytes 229408 | tf_op jit(solution)/shard_map/sum_ring/ppermute | solution.py:16
  79.2 5.1 %collective-permute-done.13 = bf16[128,896]{1,0:T(8,128)(2,1)S(1)} collective-permute-done((bf16[128,896]{1,0:T(8,128)(2,1)S(1)}, bf16[128,896]{1,0:T(8,128)(2,1)S(1)}, u32[]{:S(2)}, u32[]{:S(2)}) %collective-permute-start.13) | collective-permute-done | bytes 229408 | tf_op jit(solution)/shard_map/sum_ring/ppermute | solution.py:16
  85.4 4.7 %collective-permute-start.16 = (bf16[128,896]{1,0:T(8,128)(2,1)S(1)}, bf16[128,896]{1,0:T(8,128)(2,1)S(1)}, u32[]{:S(2)}, u32[]{:S(2)}) collective-permute-start(bf16[128,896]{1,0:T(8,128)(2,1)S(1)} %convert_element_type.92), channel_id=1, source_target_pairs={{0,2},{2,0},{1,3},{3,1},{4,6},{6,4},{5,7},{7,5},{8,10},{10,8},{9,1... | collective-permute-start | bytes 688136 | tf_op jit(solution)/shard_map/sum_far/ppermute | solution.py:21
  90.0 11.6 %collective-permute-done.16 = bf16[128,896]{1,0:T(8,128)(2,1)S(1)} collective-permute-done((bf16[128,896]{1,0:T(8,128)(2,1)S(1)}, bf16[128,896]{1,0:T(8,128)(2,1)S(1)}, u32[]{:S(2)}, u32[]{:S(2)}) %collective-permute-start.16) | collective-permute-done | bytes 229408 | tf_op jit(solution)/shard_map/sum_far/ppermute | solution.py:21
  102.0 2.7 %collective-permute-start.21 = (bf16[512,512]{1,0:T(8,128)(2,1)S(1)}, bf16[512,512]{1,0:T(8,128)(2,1)}, u32[]{:S(2)}, u32[]{:S(2)}) collective-permute-start(bf16[512,512]{1,0:T(8,128)(2,1)S(1)} %convert_element_type.97), channel_id=1, source_target_pairs={{0,32},{16,48},{32,0},{48,16},{1,33},{17,49},{33,1},{49,17},{2,34}... | collective-permute-start | bytes 1572872 | tf_op jit(solution)/shard_map/sum_grads/ppermute | solution.py:21
  104.6 1.8 %collective-permute-start.20 = (bf16[128,896]{1,0:T(8,128)(2,1)S(1)}, bf16[128,896]{1,0:T(8,128)(2,1)S(1)}, u32[]{:S(2)}, u32[]{:S(2)}) collective-permute-start(bf16[128,896]{1,0:T(8,128)(2,1)S(1)} %add_convert_fusion.1), channel_id=1, source_target_pairs={{0,12},{4,0},{8,4},{12,8},{1,13},{5,1},{9,5},{13,9},{2,14},{6,2},{... | collective-permute-start | bytes 688136 | tf_op jit(solution)/shard_map/gather_ring/ppermute | solution.py:16
  107.6 3.5 %collective-permute-done.20 = bf16[128,896]{1,0:T(8,128)(2,1)S(1)} collective-permute-done((bf16[128,896]{1,0:T(8,128)(2,1)S(1)}, bf16[128,896]{1,0:T(8,128)(2,1)S(1)}, u32[]{:S(2)}, u32[]{:S(2)}) %collective-permute-start.20) | collective-permute-done | bytes 229408 | tf_op jit(solution)/shard_map/gather_ring/ppermute | solution.py:16
  111.1 2.5 %collective-permute-done.19 = bf16[128,896]{1,0:T(8,128)(2,1)S(1)} collective-permute-done((bf16[128,896]{1,0:T(8,128)(2,1)S(1)}, bf16[128,896]{1,0:T(8,128)(2,1)S(1)}, u32[]{:S(2)}, u32[]{:S(2)}) %collective-permute-start.19) | collective-permute-done | bytes 229408 | tf_op jit(solution)/shard_map/gather_ring/ppermute | solution.py:16
  114.3 6.2 %collective-permute-done.18 = bf16[128,896]{1,0:T(8,128)(2,1)} collective-permute-done((bf16[128,896]{1,0:T(8,128)(2,1)S(1)}, bf16[128,896]{1,0:T(8,128)(2,1)}, u32[]{:S(2)}, u32[]{:S(2)}) %collective-permute-start.18) | collective-permute-done | bytes 229408 | tf_op jit(solution)/shard_map/gather_ring/ppermute | solution.py:16
  121.6 1.2 add_convert_fusion
  125.9 2.1 %convolution_convert_fusion = bf16[1024,1792]{1,0:T(8,128)(2,1)S(1)} fusion(bf16[512,896]{1,0:T(8,128)(2,1)S(1)} %get-tuple-element.30, bf16[512,896]{1,0:T(8,128)(2,1)S(1)} %get-tuple-element.29, s32[512]{0:T(512)S(1)} %fusion.38, s32[1024]{0:T(1024)S(1)} %compare_select_fusion), kind=kOutput, calls=%fused_computation.1 | convolution fusion | flops 1885077504 | bytes 5511168 | tf_op jit(solution)/shard_map/squares/dot_general | solution.py:29
  128.0 19.3 %multiply_reduce_fusion = f32[512,1792]{1,0:T(8,128)} fusion(bf16[32,32,512]{2,1,0:T(8,128)(2,1)S(1)} %bitcast.25, bf16[32,32,1792]{2,1,0:T(8,128)(2,1)S(1)} %bitcast.24), kind=kOutput, calls=%fused_computation | convolution fusion | flops 1966211072 | bytes 8388608 | tf_op jit(solution)/shard_map/squares/eki,ekj->eij/dot_general | solution.py:141
  (64 shorter events, 14.3 us)
Async XLA Ops:
  0.0 26.0 %copy-start = (bf16[512,512]{1,0:T(8,128)(2,1)S(1)}, bf16[512,512]{1,0:T(8,128)(2,1)}, u32[]{:S(2)}) copy-start(bf16[512,512]{1,0:T(8,128)(2,1)} %param.8) | copy-start | bytes 1572868
  0.0 7.5 %collective-permute-start.2 = (bf16[32,512]{1,0:T(8,128)(2,1)}, bf16[32,512]{1,0:T(8,128)(2,1)S(1)}, u32[]{:S(2)}, u32[]{:S(2)}) collective-permute-start(bf16[32,512]{1,0:T(8,128)(2,1)} %param.6), channel_id=1, source_target_pairs={{0,2},{2,0},{1,3},{3,1},{4,6},{6,4},{5,7},{7,5},{8,10},{10,8},{9,1... | collective-permute-start | bytes 98312 | tf_op jit(solution)/shard_map/gather_grads/ppermute | solution.py:21
  7.5 5.0 %collective-permute-start.3 = (bf16[64,512]{1,0:T(8,128)(2,1)S(1)}, bf16[64,512]{1,0:T(8,128)(2,1)S(1)}, u32[]{:S(2)}, u32[]{:S(2)}) collective-permute-start(bf16[64,512]{1,0:T(8,128)(2,1)S(1)} %get-tuple-element.42), channel_id=1, source_target_pairs={{0,4},{4,8},{8,12},{12,0},{1,5},{5,9},{9,13},{13,1},{2,6},{6,10},{... | collective-permute-start | bytes 196616 | tf_op jit(solution)/shard_map/gather_grads/ppermute | solution.py:16
  8.8 3.9 %collective-permute-start = (bf16[32,1792]{1,0:T(8,128)(2,1)}, bf16[32,1792]{1,0:T(8,128)(2,1)S(1)}, u32[]{:S(2)}, u32[]{:S(2)}) collective-permute-start(bf16[32,1792]{1,0:T(8,128)(2,1)} %param.5), channel_id=1, source_target_pairs={{0,64},{64,0},{128,192},{192,128},{1,65},{65,1},{129,193},{193,129... | collective-permute-start | bytes 344072 | tf_op jit(solution)/shard_map/gather_line/ppermute | solution.py:21
  9.6 6.5 %collective-permute-start.5 = (bf16[64,512]{1,0:T(8,128)(2,1)S(1)}, bf16[64,512]{1,0:T(8,128)(2,1)S(1)}, u32[]{:S(2)}, u32[]{:S(2)}) collective-permute-start(bf16[64,512]{1,0:T(8,128)(2,1)S(1)} %get-tuple-element.42), channel_id=1, source_target_pairs={{0,12},{4,0},{8,4},{12,8},{1,13},{5,1},{9,5},{13,9},{2,14},{6,2},{... | collective-permute-start | bytes 196616 | tf_op jit(solution)/shard_map/gather_grads/ppermute | solution.py:16
  11.0 5.0 %collective-permute-start.4 = (bf16[64,512]{1,0:T(8,128)(2,1)S(1)}, bf16[64,512]{1,0:T(8,128)(2,1)S(1)}, u32[]{:S(2)}, u32[]{:S(2)}) collective-permute-start(bf16[64,512]{1,0:T(8,128)(2,1)S(1)} %get-tuple-element.42), channel_id=1, source_target_pairs={{0,8},{4,12},{8,0},{12,4},{1,9},{5,13},{9,1},{13,5},{2,10},{6,14},... | collective-permute-start | bytes 196616 | tf_op jit(solution)/shard_map/gather_grads/ppermute | solution.py:16
  13.6 11.4 %collective-permute-start.1 = (bf16[64,1792]{1,0:T(8,128)(2,1)S(1)}, bf16[64,1792]{1,0:T(8,128)(2,1)S(1)}, u32[]{:S(2)}, u32[]{:S(2)}) collective-permute-start(bf16[64,1792]{1,0:T(8,128)(2,1)S(1)} %pad_maximum_fusion.2), channel_id=1, source_target_pairs={{0,128},{64,192},{128,0},{192,64},{1,129},{65,193},{129,1},{193,65... | collective-permute-start | bytes 688136 | tf_op jit(solution)/shard_map/gather_line/ppermute | solution.py:21
  16.1 9.9 %collective-permute-start.6 = (bf16[256,512]{1,0:T(8,128)(2,1)S(1)}, bf16[256,512]{1,0:T(8,128)(2,1)S(1)}, u32[]{:S(2)}, u32[]{:S(2)}) collective-permute-start(bf16[256,512]{1,0:T(8,128)(2,1)S(1)} %get-tuple-element.34), channel_id=1, source_target_pairs={{0,1},{1,0},{2,3},{3,2},{4,5},{5,4},{6,7},{7,6},{8,9},{9,8},{10,11... | collective-permute-start | bytes 786440 | tf_op jit(solution)/shard_map/gather_grads/ppermute | solution.py:21
  26.5 24.4 %collective-permute-start.10 = (bf16[512,512]{1,0:T(8,128)(2,1)S(1)}, bf16[512,512]{1,0:T(8,128)(2,1)}, u32[]{:S(2)}, u32[]{:S(2)}) collective-permute-start(bf16[512,512]{1,0:T(8,128)(2,1)S(1)} %convert_element_type.78), channel_id=1, source_target_pairs={{0,128},{64,192},{128,0},{192,64},{1,129},{65,193},{129,1},{193,65... | collective-permute-start | bytes 1572872 | tf_op jit(solution)/shard_map/sum_grads/ppermute | solution.py:21
  29.7 22.5 %collective-permute-start.9 = (bf16[128,1792]{1,0:T(8,128)(2,1)S(1)}, bf16[128,1792]{1,0:T(8,128)(2,1)S(1)}, u32[]{:S(2)}, u32[]{:S(2)}) collective-permute-start(bf16[128,1792]{1,0:T(8,128)(2,1)S(1)} %pad_maximum_fusion.1), channel_id=1, source_target_pairs={{0,48},{16,0},{32,16},{48,32},{1,49},{17,1},{33,17},{49,33},{2,50}... | collective-permute-start | bytes 1376264 | tf_op jit(solution)/shard_map/gather_plane/ppermute | solution.py:16
  32.5 19.7 %collective-permute-start.8 = (bf16[128,1792]{1,0:T(8,128)(2,1)S(1)}, bf16[128,1792]{1,0:T(8,128)(2,1)S(1)}, u32[]{:S(2)}, u32[]{:S(2)}) collective-permute-start(bf16[128,1792]{1,0:T(8,128)(2,1)S(1)} %pad_maximum_fusion.1), channel_id=1, source_target_pairs={{0,32},{16,48},{32,0},{48,16},{1,33},{17,49},{33,1},{49,17},{2,34}... | collective-permute-start | bytes 1376264 | tf_op jit(solution)/shard_map/gather_plane/ppermute | solution.py:16
  32.8 23.4 %collective-permute-start.7 = (bf16[128,1792]{1,0:T(8,128)(2,1)S(1)}, bf16[128,1792]{1,0:T(8,128)(2,1)S(1)}, u32[]{:S(2)}, u32[]{:S(2)}) collective-permute-start(bf16[128,1792]{1,0:T(8,128)(2,1)S(1)} %pad_maximum_fusion.1), channel_id=1, source_target_pairs={{0,16},{16,32},{32,48},{48,0},{1,17},{17,33},{33,49},{49,1},{2,18}... | collective-permute-start | bytes 1376264 | tf_op jit(solution)/shard_map/gather_plane/ppermute | solution.py:16
  56.3 1.2 copy-start.1
  62.7 6.3 %collective-permute-start.11 = (bf16[512,896]{1,0:T(8,128)(2,1)}, bf16[512,896]{1,0:T(8,128)(2,1)S(1)}, u32[]{:S(2)}, u32[]{:S(2)}) collective-permute-start(bf16[512,896]{1,0:T(8,128)(2,1)} %rotate.3), channel_id=1, source_target_pairs={{0,1},{1,0},{2,3},{3,2},{4,5},{5,4},{6,7},{7,6},{8,9},{9,8},{10,11... | collective-permute-start | bytes 2752520 | tf_op jit(solution)/shard_map/rotate/ppermute | solution.py:21
  63.2 13.8 %collective-permute-start.15 = (bf16[512,512]{1,0:T(8,128)(2,1)S(1)}, bf16[512,512]{1,0:T(8,128)(2,1)S(1)}, u32[]{:S(2)}, u32[]{:S(2)}) collective-permute-start(bf16[512,512]{1,0:T(8,128)(2,1)S(1)} %convert_element_type.90), channel_id=1, source_target_pairs={{0,64},{64,0},{128,192},{192,128},{1,65},{65,1},{129,193},{193,129... | collective-permute-start | bytes 1572872 | tf_op jit(solution)/shard_map/sum_grads/ppermute | solution.py:21
  70.7 8.5 %collective-permute-start.12 = (bf16[128,896]{1,0:T(8,128)(2,1)S(1)}, bf16[128,896]{1,0:T(8,128)(2,1)S(1)}, u32[]{:S(2)}, u32[]{:S(2)}) collective-permute-start(bf16[128,896]{1,0:T(8,128)(2,1)S(1)} %get-tuple-element.31), channel_id=1, source_target_pairs={{0,4},{4,8},{8,12},{12,0},{1,5},{5,9},{9,13},{13,1},{2,6},{6,10},{... | collective-permute-start | bytes 688136 | tf_op jit(solution)/shard_map/sum_ring/ppermute | solution.py:16
  72.2 7.0 %collective-permute-start.14 = (bf16[128,896]{1,0:T(8,128)(2,1)S(1)}, bf16[128,896]{1,0:T(8,128)(2,1)S(1)}, u32[]{:S(2)}, u32[]{:S(2)}) collective-permute-start(bf16[128,896]{1,0:T(8,128)(2,1)S(1)} %get-tuple-element.32), channel_id=1, source_target_pairs={{0,12},{4,0},{8,4},{12,8},{1,13},{5,1},{9,5},{13,9},{2,14},{6,2},{... | collective-permute-start | bytes 688136 | tf_op jit(solution)/shard_map/sum_ring/ppermute | solution.py:16
  73.4 10.9 %collective-permute-start.13 = (bf16[128,896]{1,0:T(8,128)(2,1)S(1)}, bf16[128,896]{1,0:T(8,128)(2,1)S(1)}, u32[]{:S(2)}, u32[]{:S(2)}) collective-permute-start(bf16[128,896]{1,0:T(8,128)(2,1)S(1)} %get-tuple-element.33), channel_id=1, source_target_pairs={{0,8},{4,12},{8,0},{12,4},{1,9},{5,13},{9,1},{13,5},{2,10},{6,14},... | collective-permute-start | bytes 688136 | tf_op jit(solution)/shard_map/sum_ring/ppermute | solution.py:16
  84.5 17.2 %collective-permute-start.17 = (bf16[512,512]{1,0:T(8,128)(2,1)S(1)}, bf16[512,512]{1,0:T(8,128)(2,1)S(1)}, u32[]{:S(2)}, u32[]{:S(2)}) collective-permute-start(bf16[512,512]{1,0:T(8,128)(2,1)S(1)} %convert_element_type.95), channel_id=1, source_target_pairs={{0,16},{16,0},{32,48},{48,32},{1,17},{17,1},{33,49},{49,33},{2,18}... | collective-permute-start | bytes 1572872 | tf_op jit(solution)/shard_map/sum_grads/ppermute | solution.py:21
  85.4 16.3 %collective-permute-start.16 = (bf16[128,896]{1,0:T(8,128)(2,1)S(1)}, bf16[128,896]{1,0:T(8,128)(2,1)S(1)}, u32[]{:S(2)}, u32[]{:S(2)}) collective-permute-start(bf16[128,896]{1,0:T(8,128)(2,1)S(1)} %convert_element_type.92), channel_id=1, source_target_pairs={{0,2},{2,0},{1,3},{3,1},{4,6},{6,4},{5,7},{7,5},{8,10},{10,8},{9,1... | collective-permute-start | bytes 688136 | tf_op jit(solution)/shard_map/sum_far/ppermute | solution.py:21
  101.7 5.5 %copy-start.3 = (s32[512]{0:T(512)S(1)}, s32[512]{0:T(512)}, u32[]{:S(2)}) copy-start(s32[512]{0:T(512)} %param.9) | copy-start | bytes 6148
  102.0 19.6 %collective-permute-start.21 = (bf16[512,512]{1,0:T(8,128)(2,1)S(1)}, bf16[512,512]{1,0:T(8,128)(2,1)}, u32[]{:S(2)}, u32[]{:S(2)}) collective-permute-start(bf16[512,512]{1,0:T(8,128)(2,1)S(1)} %convert_element_type.97), channel_id=1, source_target_pairs={{0,32},{16,48},{32,0},{48,16},{1,33},{17,49},{33,1},{49,17},{2,34}... | collective-permute-start | bytes 1572872 | tf_op jit(solution)/shard_map/sum_grads/ppermute | solution.py:21
  104.6 6.5 %collective-permute-start.20 = (bf16[128,896]{1,0:T(8,128)(2,1)S(1)}, bf16[128,896]{1,0:T(8,128)(2,1)S(1)}, u32[]{:S(2)}, u32[]{:S(2)}) collective-permute-start(bf16[128,896]{1,0:T(8,128)(2,1)S(1)} %add_convert_fusion.1), channel_id=1, source_target_pairs={{0,12},{4,0},{8,4},{12,8},{1,13},{5,1},{9,5},{13,9},{2,14},{6,2},{... | collective-permute-start | bytes 688136 | tf_op jit(solution)/shard_map/gather_ring/ppermute | solution.py:16
  106.4 7.2 %collective-permute-start.19 = (bf16[128,896]{1,0:T(8,128)(2,1)S(1)}, bf16[128,896]{1,0:T(8,128)(2,1)S(1)}, u32[]{:S(2)}, u32[]{:S(2)}) collective-permute-start(bf16[128,896]{1,0:T(8,128)(2,1)S(1)} %add_convert_fusion.1), channel_id=1, source_target_pairs={{0,8},{4,12},{8,0},{12,4},{1,9},{5,13},{9,1},{13,5},{2,10},{6,14},... | collective-permute-start | bytes 688136 | tf_op jit(solution)/shard_map/gather_ring/ppermute | solution.py:16
  107.2 13.3 %collective-permute-start.18 = (bf16[128,896]{1,0:T(8,128)(2,1)S(1)}, bf16[128,896]{1,0:T(8,128)(2,1)}, u32[]{:S(2)}, u32[]{:S(2)}) collective-permute-start(bf16[128,896]{1,0:T(8,128)(2,1)S(1)} %add_convert_fusion.1), channel_id=1, source_target_pairs={{0,4},{4,8},{8,12},{12,0},{1,5},{5,9},{9,13},{13,1},{2,6},{6,10},{... | collective-permute-start | bytes 688136 | tf_op jit(solution)/shard_map/gather_ring/ppermute | solution.py:16
  113.6 0.7 copy-start.2
  122.8 2.9 %collective-permute-start.22 = (bf16[512,896]{1,0:T(8,128)(2,1)S(1)}, bf16[512,896]{1,0:T(8,128)(2,1)S(1)}, u32[]{:S(2)}, u32[]{:S(2)}) collective-permute-start(bf16[512,896]{1,0:T(8,128)(2,1)S(1)} %pad_maximum_fusion), channel_id=1, source_target_pairs={{0,1},{1,0},{2,3},{3,2},{4,5},{5,4},{6,7},{7,6},{8,9},{9,8},{10,11... | collective-permute-start | bytes 2752520 | tf_op jit(solution)/shard_map/gather_ring/ppermute | solution.py:21

commit v3 on v2

v3 whole, which is shorter than its diff:
```python
import jax
import jax.numpy as jnp
from jax import lax
from jax.sharding import Mesh, PartitionSpec as P

MOST_LEN = 32
ROW = ("zl", "y")
COL = ("x", "zh", "core")
F32 = jnp.float32
BF16 = jnp.bfloat16


def shift(a, axis, by):
    return lax.ppermute(a, axis, [(i, (i + by) % 4) for i in range(4)])


def swap(a, axis, by=1):
    size = 2 if axis in ("zh", "core") else 4
    return lax.ppermute(a, axis, [(i, i ^ by) for i in range(size)])


def tie(*arrays):
    return lax.optimization_barrier(arrays)


def dot(a, b):
    return jnp.dot(a, b, preferred_element_type=F32)


def piece(a, i):
    return lax.dynamic_index_in_dim(a, i, 0, False)


def local(activations, act_grads, eigen_act, eigen_grad, example_ids):
    zl, y, x, zh, core = (lax.axis_index(name) for name in ("zl", "y", "x", "zh", "core"))
    block = activations.shape[0]
    group = 4 * block
    chunks = (512, eigen_act.shape[1] // 2 - 512)

    with jax.named_scope("gather_line"):
        line = jnp.concatenate([activations] + [swap(activations, "zl", s) for s in (1, 2, 3)])
    with jax.named_scope("gather_grads"):
        grads = jnp.concatenate([act_grads, swap(act_grads, "zh")])
        line, grads = tie(line, grads)

    with jax.named_scope("gather_plane"):
        ring = [line] + [shift(line, "y", s) for s in (1, 2, 3)]
    with jax.named_scope("gather_grads"):
        grads = jnp.concatenate([grads] + [shift(grads, "x", s) for s in (1, 2, 3)])
        ring[1], ring[2], ring[3], grads = tie(ring[1], ring[2], ring[3], grads)
        grads = jnp.concatenate([grads, swap(grads, "core")])
    with jax.named_scope("gather_plane"):
        tokens = jnp.concatenate(ring)

    with jax.named_scope("sum_grads"):
        part = dot(grads, eigen_grad).reshape(2, 2 * group, -1)
        sums = piece(part, y % 2) + swap(piece(part, 1 - y % 2).astype(BF16), "y", 1).astype(F32)
        sums = sums.reshape(2, group, -1)
        sums = piece(sums, y // 2) + swap(piece(sums, 1 - y // 2), "y", 2).astype(F32)

    pairs = []
    lo = 0
    for wide in chunks:
        with jax.named_scope("rotate"):
            eigen_own = lax.dynamic_slice_in_dim(eigen_act, lo + core * wide, wide, 1)
            eigen_away = lax.dynamic_slice_in_dim(eigen_act, lo + (1 - core) * wide, wide, 1)
            away = dot(tokens, eigen_away).astype(BF16)
            pair = dot(tokens, eigen_own) + swap(away, "core").astype(F32)
            pairs.append([pair.reshape(4, group, wide)])
        lo += 2 * wide
    pairs = [pairs[0] + pairs[1]]
    totals = []
    for parts in pairs:
        with jax.named_scope("sum_ring"):
            at = lambda i: jnp.concatenate([piece(p, i % 4) for p in parts], axis=1)
            total = at(x)
            for s in (1, 2, 3):
                total = total + shift(at(x + s).astype(BF16), "x", s).astype(F32)
        totals.append(total)
    totals[0], sums = tie(totals[0], sums)
    with jax.named_scope("sum_grads"):
        sums = sums + swap(sums.astype(BF16), "zl", 1).astype(F32)
        sums = sums + swap(sums.astype(BF16), "zl", 2).astype(F32)
        grad_rot = sums.astype(BF16)
    columns = []
    for total in totals:
        with jax.named_scope("sum_far"):
            mine = (total + swap(total.astype(BF16), "zh").astype(F32)).astype(BF16)
        if not columns:
            mine, grad_rot = tie(mine, grad_rot)
            with jax.named_scope("sum_grads"):
                grad_rot = jnp.concatenate([grad_rot, swap(grad_rot, "y", 2)])
                grad_rot = jnp.concatenate([grad_rot, swap(grad_rot, "y", 1)])
        with jax.named_scope("gather_ring"):
            own = jnp.concatenate([mine] + [shift(mine, "x", s) for s in (1, 2, 3)])
            if not columns:
                own, grad_rot = tie(own, grad_rot)
            other = swap(own, "core")
            lower, upper = jnp.where(core == 0, own, other), jnp.where(core == 0, other, own)
            cuts = chunks if own.shape[1] == sum(chunks) else (own.shape[1],)
            at = 0
            both = []
            for wide in cuts:
                both += [lower[:, at : at + wide], upper[:, at : at + wide]]
                at += wide
            columns.append(jnp.concatenate(both, axis=1))

    with jax.named_scope("slots"):
        examples = example_ids.shape[0] // 16
        row = lax.broadcasted_iota(jnp.int32, (1, example_ids.shape[0]), 1)
        within, outer, inner = row % block, row // group, row // block % 4
        act_token = ((zl ^ inner) * 4 + (y - x + outer) % 4) * block + within
        gathered = ((y % 2) ^ (row // (2 * group))) * 8 + ((y // 2) ^ (outer % 2)) * 4 + inner
        from_x = (x - gathered // 2 % 4) % 4
        grad_token = (from_x * 4 + (zh ^ (gathered % 2)) * 2 + (core ^ (gathered // 8))) * block + within
        bounds = jnp.sum(example_ids[None, :] < jnp.arange(examples + 1)[:, None], axis=1)
        slot = bounds[:-1, None] + jnp.arange(MOST_LEN)
        slot = jnp.where(slot < bounds[1:, None], slot, -1).reshape(-1, 1)
        take_act = (slot == act_token).astype(BF16)
        take_grad = (slot == grad_token).astype(BF16)
    with jax.named_scope("squares"):
        grad_rows = dot(take_grad, grad_rot).astype(BF16).reshape(examples, MOST_LEN, -1)
        sums = []
        for act_rot in columns:
            act_rows = dot(take_act, act_rot).astype(BF16).reshape(examples, MOST_LEN, -1)
            blocks = jnp.einsum("eki,ekj->eij", grad_rows, act_rows, preferred_element_type=F32)
            sums.append(jnp.sum(blocks * blocks * (1 / examples), axis=0))
        return sums[0]


def solution(mesh):
    fine = Mesh(mesh.devices.reshape(4, 4, 4, 2, 2), ROW + COL)
    in_specs = (P(ROW, COL), P(COL, ROW), P(COL, ROW), P(ROW, COL), P())
    return jax.shard_map(local, mesh=fine, in_specs=in_specs, out_specs=P(COL, ROW), check_vma=False)
```

time: 148 us -> 136 us (0.919)
  the two profiles are of different devices: /device:TPU:33 before, /device:TPU:1 now
where the time goes in v3:
time: 136 us
  waiting for transfers between devices  62.7 us (46%)
  starting transfers between devices  40 us (29%)
  matrix products  28.6 us (21%)
  other arithmetic  2.68 us (2%)
    ppermute x12, waiting for transfers between devices, shift(): return lax.ppermute(a, axis, [(i, (i + by) % 4) for i in range(4)])  38.8 us
    ppermute x15, waiting for transfers between devices, swap(): return lax.ppermute(a, axis, [(i, i ^ by) for i in range(size)])  23.9 us
    ppermute x15, starting transfers between devices, swap(): return lax.ppermute(a, axis, [(i, i ^ by) for i in range(size)])  22.1 us
    dot_general x1, matrix products, local(): jnp.einsum('eki,ekj->eij', grad_rows, act_rows, preferred_element_type=F32)  19.3 us
    ppermute x12, starting transfers between devices, shift(): return lax.ppermute(a, axis, [(i, (i + by) % 4) for i in range(4)])  17.9 us
    dot_general x7, matrix products, dot(): return jnp.dot(a, b, preferred_element_type=F32)  9.33 us
  transfers between devices with their start and end apart: 27, of which 18 were waited for; matrix products, arithmetic and copies ran while one was open for 7% of the time, Pallas kernels for 0%

profile of v3, /device:TPU:1, one launch (start us, length us, event | category | flops | bytes accessed | tf_op | source)
XLA Modules:
  0.0 135.5 jit_solution(14111253892505794526)
XLA Ops:
  0.0 7.7 %collective-permute-start.3 = (bf16[32,512]{1,0:T(8,128)(2,1)}, bf16[32,512]{1,0:T(8,128)(2,1)S(1)}, u32[]{:S(2)}, u32[]{:S(2)}) collective-permute-start(bf16[32,512]{1,0:T(8,128)(2,1)} %param.6), channel_id=1, source_target_pairs={{0,2},{2,0},{1,3},{3,1},{4,6},{6,4},{5,7},{7,5},{8,10},{10,8},{9,1... | collective-permute-start | bytes 98312 | tf_op jit(solution)/shard_map/gather_grads/ppermute | solution.py:19
  7.7 1.2 collective-permute-start.1
  9.7 1.6 %collective-permute-start.2 = (bf16[32,1792]{1,0:T(8,128)(2,1)}, bf16[32,1792]{1,0:T(8,128)(2,1)S(1)}, u32[]{:S(2)}, u32[]{:S(2)}) collective-permute-start(bf16[32,1792]{1,0:T(8,128)(2,1)} %param.5), channel_id=1, source_target_pairs={{0,192},{64,128},{128,64},{192,0},{1,193},{65,129},{129,65},{193,1... | collective-permute-start | bytes 344072 | tf_op jit(solution)/shard_map/gather_line/ppermute | solution.py:19
  12.1 4.3 %collective-permute-done.1 = bf16[32,1792]{1,0:T(8,128)(2,1)S(1)} collective-permute-done((bf16[32,1792]{1,0:T(8,128)(2,1)}, bf16[32,1792]{1,0:T(8,128)(2,1)S(1)}, u32[]{:S(2)}, u32[]{:S(2)}) %collective-permute-start.1) | collective-permute-done | bytes 114720 | tf_op jit(solution)/shard_map/gather_line/ppermute | solution.py:19
  16.3 2.3 %collective-permute-done.2 = bf16[32,1792]{1,0:T(8,128)(2,1)S(1)} collective-permute-done((bf16[32,1792]{1,0:T(8,128)(2,1)}, bf16[32,1792]{1,0:T(8,128)(2,1)S(1)}, u32[]{:S(2)}, u32[]{:S(2)}) %collective-permute-start.2) | collective-permute-done | bytes 114720 | tf_op jit(solution)/shard_map/gather_line/ppermute | solution.py:19
  19.6 2.8 %collective-permute-start.6 = (bf16[128,1792]{1,0:T(8,128)(2,1)S(1)}, bf16[128,1792]{1,0:T(8,128)(2,1)S(1)}, u32[]{:S(2)}, u32[]{:S(2)}) collective-permute-start(bf16[128,1792]{1,0:T(8,128)(2,1)S(1)} %pad_maximum_fusion.2), channel_id=1, source_target_pairs={{0,48},{16,0},{32,16},{48,32},{1,49},{17,1},{33,17},{49,33},{2,50}... | collective-permute-start | bytes 1376264 | tf_op jit(solution)/shard_map/gather_plane/ppermute | solution.py:14
  23.4 2.5 %collective-permute-start.9 = (bf16[64,512]{1,0:T(8,128)(2,1)S(1)}, bf16[64,512]{1,0:T(8,128)(2,1)S(1)}, u32[]{:S(2)}, u32[]{:S(2)}) collective-permute-start(bf16[64,512]{1,0:T(8,128)(2,1)S(1)} %pad_maximum_fusion.8), channel_id=1, source_target_pairs={{0,12},{4,0},{8,4},{12,8},{1,13},{5,1},{9,5},{13,9},{2,14},{6,2},{... | collective-permute-start | bytes 196616 | tf_op jit(solution)/shard_map/gather_grads/ppermute | solution.py:14
  28.1 2.7 %collective-permute-done.8 = bf16[64,512]{1,0:T(8,128)(2,1)S(1)} collective-permute-done((bf16[64,512]{1,0:T(8,128)(2,1)S(1)}, bf16[64,512]{1,0:T(8,128)(2,1)S(1)}, u32[]{:S(2)}, u32[]{:S(2)}) %collective-permute-start.8) | collective-permute-done | bytes 65568 | tf_op jit(solution)/shard_map/gather_grads/ppermute | solution.py:14
  30.8 1.4 %collective-permute-done.7 = bf16[64,512]{1,0:T(8,128)(2,1)S(1)} collective-permute-done((bf16[64,512]{1,0:T(8,128)(2,1)S(1)}, bf16[64,512]{1,0:T(8,128)(2,1)S(1)}, u32[]{:S(2)}, u32[]{:S(2)}) %collective-permute-start.7) | collective-permute-done | bytes 65568 | tf_op jit(solution)/shard_map/gather_grads/ppermute | solution.py:14
  32.2 1.9 %collective-permute-done.5 = bf16[128,1792]{1,0:T(8,128)(2,1)S(1)} collective-permute-done((bf16[128,1792]{1,0:T(8,128)(2,1)S(1)}, bf16[128,1792]{1,0:T(8,128)(2,1)S(1)}, u32[]{:S(2)}, u32[]{:S(2)}) %collective-permute-start.5) | collective-permute-done | bytes 458784 | tf_op jit(solution)/shard_map/gather_plane/ppermute | solution.py:14
  34.1 12.1 %collective-permute-done.4 = bf16[128,1792]{1,0:T(8,128)(2,1)S(1)} collective-permute-done((bf16[128,1792]{1,0:T(8,128)(2,1)S(1)}, bf16[128,1792]{1,0:T(8,128)(2,1)S(1)}, u32[]{:S(2)}, u32[]{:S(2)}) %collective-permute-start.4) | collective-permute-done | bytes 458784 | tf_op jit(solution)/shard_map/gather_plane/ppermute | solution.py:14
  46.8 2.6 %fusion.30 = bf16[512,384]{1,0:T(8,128)(2,1)S(1)} fusion(bf16[512,1792]{1,0:T(8,128)(2,1)S(1)} %constant_dynamic-update-slice_fusion, bf16[1792,1792]{1,0:T(8,128)(2,1)} %param.7, s32[]{:T(128)S(6)} %select_n.251), kind=kOutput, calls=%fused_computation.24 | convolution fusion | flops 704839680 | bytes 3604484 | tf_op jit(solution)/shard_map/rotate/dot_general | solution.py:27
  49.9 1.1 fusion.24
  52.0 1.1 fusion.27
  53.2 1.1 fusion.21
  54.5 2.8 %collective-permute-start.13 = (bf16[128,896]{1,0:T(8,128)(2,1)S(1)}, bf16[128,896]{1,0:T(8,128)(2,1)S(1)}, u32[]{:S(2)}, u32[]{:S(2)}) collective-permute-start(bf16[128,896]{1,0:T(8,128)(2,1)S(1)} %pad_maximum_fusion.6), channel_id=1, source_target_pairs={{0,8},{4,12},{8,0},{12,4},{1,9},{5,13},{9,1},{13,5},{2,10},{6,14},... | collective-permute-start | bytes 688136 | tf_op jit(solution)/shard_map/sum_ring/ppermute | solution.py:14
  59.5 1.1 collective-permute-start.17
  60.7 2.1 %collective-permute-done.13 = bf16[128,896]{1,0:T(8,128)(2,1)S(1)} collective-permute-done((bf16[128,896]{1,0:T(8,128)(2,1)S(1)}, bf16[128,896]{1,0:T(8,128)(2,1)S(1)}, u32[]{:S(2)}, u32[]{:S(2)}) %collective-permute-start.13) | collective-permute-done | bytes 229408 | tf_op jit(solution)/shard_map/sum_ring/ppermute | solution.py:14
  62.8 5.0 %collective-permute-done.14 = bf16[128,896]{1,0:T(8,128)(2,1)S(1)} collective-permute-done((bf16[128,896]{1,0:T(8,128)(2,1)S(1)}, bf16[128,896]{1,0:T(8,128)(2,1)S(1)}, u32[]{:S(2)}, u32[]{:S(2)}) %collective-permute-start.14) | collective-permute-done | bytes 229408 | tf_op jit(solution)/shard_map/sum_ring/ppermute | solution.py:14
  68.3 2.9 %collective-permute-start.19 = (bf16[128,512]{1,0:T(8,128)(2,1)S(1)}, bf16[128,512]{1,0:T(8,128)(2,1)S(1)}, u32[]{:S(2)}, u32[]{:S(2)}) collective-permute-start(bf16[128,512]{1,0:T(8,128)(2,1)S(1)} %convert_element_type.82), channel_id=1, source_target_pairs={{0,64},{64,0},{128,192},{192,128},{1,65},{65,1},{129,193},{193,129... | collective-permute-start | bytes 393224 | tf_op jit(solution)/shard_map/sum_grads/ppermute | solution.py:19
  71.2 1.3 collective-permute-start.18
  72.6 1.0 collective-permute-done.19
  73.6 2.0 %collective-permute-start.20 = (bf16[128,512]{1,0:T(8,128)(2,1)S(1)}, bf16[128,512]{1,0:T(8,128)(2,1)S(1)}, u32[]{:S(2)}, u32[]{:S(2)}) collective-permute-start(bf16[128,512]{1,0:T(8,128)(2,1)S(1)} %fusion.44), channel_id=1, source_target_pairs={{0,128},{64,192},{128,0},{192,64},{1,129},{65,193},{129,1},{193,65... | collective-permute-start | bytes 393224 | tf_op jit(solution)/shard_map/sum_grads/ppermute | solution.py:19
  75.6 6.7 %collective-permute-done.18 = bf16[128,896]{1,0:T(8,128)(2,1)S(1)} collective-permute-done((bf16[128,896]{1,0:T(8,128)(2,1)S(1)}, bf16[128,896]{1,0:T(8,128)(2,1)S(1)}, u32[]{:S(2)}, u32[]{:S(2)}) %collective-permute-start.18) | collective-permute-done | bytes 229408 | tf_op jit(solution)/shard_map/sum_far/ppermute | solution.py:19
  82.4 8.2 %collective-permute-done.20 = bf16[128,512]{1,0:T(8,128)(2,1)S(1)} collective-permute-done((bf16[128,512]{1,0:T(8,128)(2,1)S(1)}, bf16[128,512]{1,0:T(8,128)(2,1)S(1)}, u32[]{:S(2)}, u32[]{:S(2)}) %collective-permute-start.20) | collective-permute-done | bytes 131104 | tf_op jit(solution)/shard_map/sum_grads/ppermute | solution.py:19
  90.7 1.4 %collective-permute-start.24 = (bf16[128,512]{1,0:T(8,128)(2,1)S(1)}, bf16[128,512]{1,0:T(8,128)(2,1)S(1)}, u32[]{:S(2)}, u32[]{:S(2)}) collective-permute-start(bf16[128,512]{1,0:T(8,128)(2,1)S(1)} %add_convert_fusion.1), channel_id=1, source_target_pairs={{0,32},{16,48},{32,0},{48,16},{1,33},{17,49},{33,1},{49,17},{2,34}... | collective-permute-start | bytes 393224 | tf_op jit(solution)/shard_map/sum_grads/ppermute | solution.py:19
  92.1 4.7 %collective-permute-start.23 = (bf16[128,896]{1,0:T(8,128)(2,1)S(1)}, bf16[128,896]{1,0:T(8,128)(2,1)S(1)}, u32[]{:S(2)}, u32[]{:S(2)}) collective-permute-start(bf16[128,896]{1,0:T(8,128)(2,1)S(1)} %add_convert_fusion), channel_id=1, source_target_pairs={{0,12},{4,0},{8,4},{12,8},{1,13},{5,1},{9,5},{13,9},{2,14},{6,2},{... | collective-permute-start | bytes 688136 | tf_op jit(solution)/shard_map/gather_ring/ppermute | solution.py:14
  98.1 3.5 %collective-permute-done.23 = bf16[128,896]{1,0:T(8,128)(2,1)S(1)} collective-permute-done((bf16[128,896]{1,0:T(8,128)(2,1)S(1)}, bf16[128,896]{1,0:T(8,128)(2,1)S(1)}, u32[]{:S(2)}, u32[]{:S(2)}) %collective-permute-start.23) | collective-permute-done | bytes 229408 | tf_op jit(solution)/shard_map/gather_ring/ppermute | solution.py:14
  101.7 2.7 %collective-permute-done.22 = bf16[128,896]{1,0:T(8,128)(2,1)S(1)} collective-permute-done((bf16[128,896]{1,0:T(8,128)(2,1)S(1)}, bf16[128,896]{1,0:T(8,128)(2,1)S(1)}, u32[]{:S(2)}, u32[]{:S(2)}) %collective-permute-start.22) | collective-permute-done | bytes 229408 | tf_op jit(solution)/shard_map/gather_ring/ppermute | solution.py:14
  104.3 6.4 %collective-permute-done.21 = bf16[128,896]{1,0:T(8,128)(2,1)S(1)} collective-permute-done((bf16[128,896]{1,0:T(8,128)(2,1)S(1)}, bf16[128,896]{1,0:T(8,128)(2,1)S(1)}, u32[]{:S(2)}, u32[]{:S(2)}) %collective-permute-start.21) | collective-permute-done | bytes 229408 | tf_op jit(solution)/shard_map/gather_ring/ppermute | solution.py:14
  114.1 2.1 %convolution_convert_fusion = bf16[1024,1792]{1,0:T(8,128)(2,1)S(1)} fusion(bf16[512,384]{1,0:T(8,128)(2,1)S(1)} %slice.27, bf16[512,384]{1,0:T(8,128)(2,1)S(1)} %slice.26, bf16[512,512]{1,0:T(8,128)(2,1)S(1)} %slice.25, bf16[512,512]{1,0:T(8,128)(2,1)S(1)} %slice.24, s32[512]{0:T(512)S(1)} %get-tuple-element.39, s32[1024]{0:T(1024)S(1)} %compare_select_fusion), kind=kOutput, calls=%fused_computation.1 | convolution fusion | flops 1888747520 | bytes 5511168 | tf_op jit(solution)/shard_map/squares/dot_general | solution.py:27
  116.2 19.3 %multiply_reduce_fusion = f32[512,1792]{1,0:T(8,128)} fusion(bf16[32,32,512]{2,1,0:T(8,128)(2,1)S(1)} %bitcast.47, bf16[32,32,1792]{2,1,0:T(8,128)(2,1)S(1)} %bitcast.46), kind=kOutput, calls=%fused_computation | convolution fusion | flops 1966211072 | bytes 8388608 | tf_op jit(solution)/shard_map/squares/eki,ekj->eij/dot_general | solution.py:126
  (76 shorter events, 15.3 us)
Async XLA Ops:
  0.0 51.2 %copy-start = (bf16[512,512]{1,0:T(8,128)(2,1)S(1)}, bf16[512,512]{1,0:T(8,128)(2,1)}, u32[]{:S(2)}) copy-start(bf16[512,512]{1,0:T(8,128)(2,1)} %param.8) | copy-start | bytes 1572868
  0.0 11.3 %collective-permute-start.3 = (bf16[32,512]{1,0:T(8,128)(2,1)}, bf16[32,512]{1,0:T(8,128)(2,1)S(1)}, u32[]{:S(2)}, u32[]{:S(2)}) collective-permute-start(bf16[32,512]{1,0:T(8,128)(2,1)} %param.6), channel_id=1, source_target_pairs={{0,2},{2,0},{1,3},{3,1},{4,6},{6,4},{5,7},{7,5},{8,10},{10,8},{9,1... | collective-permute-start | bytes 98312 | tf_op jit(solution)/shard_map/gather_grads/ppermute | solution.py:19
  7.7 8.6 %collective-permute-start.1 = (bf16[32,1792]{1,0:T(8,128)(2,1)}, bf16[32,1792]{1,0:T(8,128)(2,1)S(1)}, u32[]{:S(2)}, u32[]{:S(2)}) collective-permute-start(bf16[32,1792]{1,0:T(8,128)(2,1)} %param.5), channel_id=1, source_target_pairs={{0,128},{64,192},{128,0},{192,64},{1,129},{65,193},{129,1},{193,65... | collective-permute-start | bytes 344072 | tf_op jit(solution)/shard_map/gather_line/ppermute | solution.py:19
  8.9 7.4 %collective-permute-start = (bf16[32,1792]{1,0:T(8,128)(2,1)}, bf16[32,1792]{1,0:T(8,128)(2,1)S(1)}, u32[]{:S(2)}, u32[]{:S(2)}) collective-permute-start(bf16[32,1792]{1,0:T(8,128)(2,1)} %param.5), channel_id=1, source_target_pairs={{0,64},{64,0},{128,192},{192,128},{1,65},{65,1},{129,193},{193,129... | collective-permute-start | bytes 344072 | tf_op jit(solution)/shard_map/gather_line/ppermute | solution.py:19
  9.7 9.0 %collective-permute-start.2 = (bf16[32,1792]{1,0:T(8,128)(2,1)}, bf16[32,1792]{1,0:T(8,128)(2,1)S(1)}, u32[]{:S(2)}, u32[]{:S(2)}) collective-permute-start(bf16[32,1792]{1,0:T(8,128)(2,1)} %param.5), channel_id=1, source_target_pairs={{0,192},{64,128},{128,64},{192,0},{1,193},{65,129},{129,65},{193,1... | collective-permute-start | bytes 344072 | tf_op jit(solution)/shard_map/gather_line/ppermute | solution.py:19
  19.6 12.6 %collective-permute-start.6 = (bf16[128,1792]{1,0:T(8,128)(2,1)S(1)}, bf16[128,1792]{1,0:T(8,128)(2,1)S(1)}, u32[]{:S(2)}, u32[]{:S(2)}) collective-permute-start(bf16[128,1792]{1,0:T(8,128)(2,1)S(1)} %pad_maximum_fusion.2), channel_id=1, source_target_pairs={{0,48},{16,0},{32,16},{48,32},{1,49},{17,1},{33,17},{49,33},{2,50}... | collective-permute-start | bytes 1376264 | tf_op jit(solution)/shard_map/gather_plane/ppermute | solution.py:14
  22.4 11.7 %collective-permute-start.5 = (bf16[128,1792]{1,0:T(8,128)(2,1)S(1)}, bf16[128,1792]{1,0:T(8,128)(2,1)S(1)}, u32[]{:S(2)}, u32[]{:S(2)}) collective-permute-start(bf16[128,1792]{1,0:T(8,128)(2,1)S(1)} %pad_maximum_fusion.2), channel_id=1, source_target_pairs={{0,32},{16,48},{32,0},{48,16},{1,33},{17,49},{33,1},{49,17},{2,34}... | collective-permute-start | bytes 1376264 | tf_op jit(solution)/shard_map/gather_plane/ppermute | solution.py:14
  22.7 23.4 %collective-permute-start.4 = (bf16[128,1792]{1,0:T(8,128)(2,1)S(1)}, bf16[128,1792]{1,0:T(8,128)(2,1)S(1)}, u32[]{:S(2)}, u32[]{:S(2)}) collective-permute-start(bf16[128,1792]{1,0:T(8,128)(2,1)S(1)} %pad_maximum_fusion.2), channel_id=1, source_target_pairs={{0,16},{16,32},{32,48},{48,0},{1,17},{17,33},{33,49},{49,1},{2,18}... | collective-permute-start | bytes 1376264 | tf_op jit(solution)/shard_map/gather_plane/ppermute | solution.py:14
  23.4 3.8 %collective-permute-start.9 = (bf16[64,512]{1,0:T(8,128)(2,1)S(1)}, bf16[64,512]{1,0:T(8,128)(2,1)S(1)}, u32[]{:S(2)}, u32[]{:S(2)}) collective-permute-start(bf16[64,512]{1,0:T(8,128)(2,1)S(1)} %pad_maximum_fusion.8), channel_id=1, source_target_pairs={{0,12},{4,0},{8,4},{12,8},{1,13},{5,1},{9,5},{13,9},{2,14},{6,2},{... | collective-permute-start | bytes 196616 | tf_op jit(solution)/shard_map/gather_grads/ppermute | solution.py:14
  25.9 4.9 %collective-permute-start.8 = (bf16[64,512]{1,0:T(8,128)(2,1)S(1)}, bf16[64,512]{1,0:T(8,128)(2,1)S(1)}, u32[]{:S(2)}, u32[]{:S(2)}) collective-permute-start(bf16[64,512]{1,0:T(8,128)(2,1)S(1)} %pad_maximum_fusion.8), channel_id=1, source_target_pairs={{0,8},{4,12},{8,0},{12,4},{1,9},{5,13},{9,1},{13,5},{2,10},{6,14},... | collective-permute-start | bytes 196616 | tf_op jit(solution)/shard_map/gather_grads/ppermute | solution.py:14
  27.2 4.9 %collective-permute-start.7 = (bf16[64,512]{1,0:T(8,128)(2,1)S(1)}, bf16[64,512]{1,0:T(8,128)(2,1)S(1)}, u32[]{:S(2)}, u32[]{:S(2)}) collective-permute-start(bf16[64,512]{1,0:T(8,128)(2,1)S(1)} %pad_maximum_fusion.8), channel_id=1, source_target_pairs={{0,4},{4,8},{8,12},{12,0},{1,5},{5,9},{9,13},{13,1},{2,6},{6,10},{... | collective-permute-start | bytes 196616 | tf_op jit(solution)/shard_map/gather_grads/ppermute | solution.py:14
  46.2 5.1 %collective-permute-start.15 = (bf16[256,512]{1,0:T(8,128)(2,1)S(1)}, bf16[256,512]{1,0:T(8,128)(2,1)S(1)}, u32[]{:S(2)}, u32[]{:S(2)}) collective-permute-start(bf16[256,512]{1,0:T(8,128)(2,1)S(1)} %pad_maximum_fusion.3), channel_id=1, source_target_pairs={{0,1},{1,0},{2,3},{3,2},{4,5},{5,4},{6,7},{7,6},{8,9},{9,8},{10,11... | collective-permute-start | bytes 786440 | tf_op jit(solution)/shard_map/gather_grads/ppermute | solution.py:19
  46.7 3.3 %copy-start.2 = (bf16[1792,1792]{1,0:T(8,128)(2,1)S(1)}, bf16[1792,1792]{1,0:T(8,128)(2,1)}, u32[]{:S(2)}) copy-start(bf16[1792,1792]{1,0:T(8,128)(2,1)} %param.7) | copy-start | bytes 19267588
  49.4 2.6 %collective-permute-start.11 = (bf16[512,384]{1,0:T(8,128)(2,1)S(1)}, bf16[512,384]{1,0:T(8,128)(2,1)S(1)}, u32[]{:S(2)}, u32[]{:S(2)}) collective-permute-start(bf16[512,384]{1,0:T(8,128)(2,1)S(1)} %fusion.30), channel_id=1, source_target_pairs={{0,1},{1,0},{2,3},{3,2},{4,5},{5,4},{6,7},{7,6},{8,9},{9,8},{10,11... | collective-permute-start | bytes 1179656 | tf_op jit(solution)/shard_map/rotate/ppermute | solution.py:19
  51.1 2.2 %collective-permute-start.10 = (bf16[512,512]{1,0:T(8,128)(2,1)S(1)}, bf16[512,512]{1,0:T(8,128)(2,1)S(1)}, u32[]{:S(2)}, u32[]{:S(2)}) collective-permute-start(bf16[512,512]{1,0:T(8,128)(2,1)S(1)} %fusion.24), channel_id=1, source_target_pairs={{0,1},{1,0},{2,3},{3,2},{4,5},{5,4},{6,7},{7,6},{8,9},{9,8},{10,11... | collective-permute-start | bytes 1572872 | tf_op jit(solution)/shard_map/rotate/ppermute | solution.py:19
  51.7 7.7 %collective-permute-start.16 = (bf16[256,512]{1,0:T(8,128)(2,1)S(1)}, bf16[256,512]{1,0:T(8,128)(2,1)S(1)}, u32[]{:S(2)}, u32[]{:S(2)}) collective-permute-start(bf16[256,512]{1,0:T(8,128)(2,1)S(1)} %fusion.43), channel_id=1, source_target_pairs={{0,16},{16,0},{32,48},{48,32},{1,17},{17,1},{33,49},{49,33},{2,18}... | collective-permute-start | bytes 786440 | tf_op jit(solution)/shard_map/sum_grads/ppermute | solution.py:19
  54.5 8.3 %collective-permute-start.13 = (bf16[128,896]{1,0:T(8,128)(2,1)S(1)}, bf16[128,896]{1,0:T(8,128)(2,1)S(1)}, u32[]{:S(2)}, u32[]{:S(2)}) collective-permute-start(bf16[128,896]{1,0:T(8,128)(2,1)S(1)} %pad_maximum_fusion.6), channel_id=1, source_target_pairs={{0,8},{4,12},{8,0},{12,4},{1,9},{5,13},{9,1},{13,5},{2,10},{6,14},... | collective-permute-start | bytes 688136 | tf_op jit(solution)/shard_map/sum_ring/ppermute | solution.py:14
  57.3 10.5 %collective-permute-start.14 = (bf16[128,896]{1,0:T(8,128)(2,1)S(1)}, bf16[128,896]{1,0:T(8,128)(2,1)S(1)}, u32[]{:S(2)}, u32[]{:S(2)}) collective-permute-start(bf16[128,896]{1,0:T(8,128)(2,1)S(1)} %pad_maximum_fusion.7), channel_id=1, source_target_pairs={{0,12},{4,0},{8,4},{12,8},{1,13},{5,1},{9,5},{13,9},{2,14},{6,2},{... | collective-permute-start | bytes 688136 | tf_op jit(solution)/shard_map/sum_ring/ppermute | solution.py:14
  58.3 9.8 %collective-permute-start.12 = (bf16[128,896]{1,0:T(8,128)(2,1)S(1)}, bf16[128,896]{1,0:T(8,128)(2,1)S(1)}, u32[]{:S(2)}, u32[]{:S(2)}) collective-permute-start(bf16[128,896]{1,0:T(8,128)(2,1)S(1)} %pad_maximum_fusion.5), channel_id=1, source_target_pairs={{0,4},{4,8},{8,12},{12,0},{1,5},{5,9},{9,13},{13,1},{2,6},{6,10},{... | collective-permute-start | bytes 688136 | tf_op jit(solution)/shard_map/sum_ring/ppermute | solution.py:14
  59.5 8.7 %collective-permute-start.17 = (f32[128,512]{1,0:T(8,128)S(1)}, f32[128,512]{1,0:T(8,128)S(1)}, u32[]{:S(2)}, u32[]{:S(2)}) collective-permute-start(f32[128,512]{1,0:T(8,128)S(1)} %dynamic-slice_bitcast_fusion), channel_id=1, source_target_pairs={{0,32},{16,48},{32,0},{48,16},{1,33},{17,49},{33,1},{49,17},{2,34}... | collective-permute-start | bytes 786440 | tf_op jit(solution)/shard_map/sum_grads/ppermute | solution.py:19
  68.2 29.8 %copy-start.1 = (s32[512]{0:T(512)S(1)}, s32[512]{0:T(512)}, u32[]{:S(2)}) copy-start(s32[512]{0:T(512)} %param.9) | copy-start | bytes 6148
  68.3 5.3 %collective-permute-start.19 = (bf16[128,512]{1,0:T(8,128)(2,1)S(1)}, bf16[128,512]{1,0:T(8,128)(2,1)S(1)}, u32[]{:S(2)}, u32[]{:S(2)}) collective-permute-start(bf16[128,512]{1,0:T(8,128)(2,1)S(1)} %convert_element_type.82), channel_id=1, source_target_pairs={{0,64},{64,0},{128,192},{192,128},{1,65},{65,1},{129,193},{193,129... | collective-permute-start | bytes 393224 | tf_op jit(solution)/shard_map/sum_grads/ppermute | solution.py:19
  71.2 11.1 %collective-permute-start.18 = (bf16[128,896]{1,0:T(8,128)(2,1)S(1)}, bf16[128,896]{1,0:T(8,128)(2,1)S(1)}, u32[]{:S(2)}, u32[]{:S(2)}) collective-permute-start(bf16[128,896]{1,0:T(8,128)(2,1)S(1)} %convert_element_type.79), channel_id=1, source_target_pairs={{0,2},{2,0},{1,3},{3,1},{4,6},{6,4},{5,7},{7,5},{8,10},{10,8},{9,1... | collective-permute-start | bytes 688136 | tf_op jit(solution)/shard_map/sum_far/ppermute | solution.py:19
  73.6 17.0 %collective-permute-start.20 = (bf16[128,512]{1,0:T(8,128)(2,1)S(1)}, bf16[128,512]{1,0:T(8,128)(2,1)S(1)}, u32[]{:S(2)}, u32[]{:S(2)}) collective-permute-start(bf16[128,512]{1,0:T(8,128)(2,1)S(1)} %fusion.44), channel_id=1, source_target_pairs={{0,128},{64,192},{128,0},{192,64},{1,129},{65,193},{129,1},{193,65... | collective-permute-start | bytes 393224 | tf_op jit(solution)/shard_map/sum_grads/ppermute | solution.py:19
  90.7 7.2 %collective-permute-start.24 = (bf16[128,512]{1,0:T(8,128)(2,1)S(1)}, bf16[128,512]{1,0:T(8,128)(2,1)S(1)}, u32[]{:S(2)}, u32[]{:S(2)}) collective-permute-start(bf16[128,512]{1,0:T(8,128)(2,1)S(1)} %add_convert_fusion.1), channel_id=1, source_target_pairs={{0,32},{16,48},{32,0},{48,16},{1,33},{17,49},{33,1},{49,17},{2,34}... | collective-permute-start | bytes 393224 | tf_op jit(solution)/shard_map/sum_grads/ppermute | solution.py:19
  92.1 9.6 %collective-permute-start.23 = (bf16[128,896]{1,0:T(8,128)(2,1)S(1)}, bf16[128,896]{1,0:T(8,128)(2,1)S(1)}, u32[]{:S(2)}, u32[]{:S(2)}) collective-permute-start(bf16[128,896]{1,0:T(8,128)(2,1)S(1)} %add_convert_fusion), channel_id=1, source_target_pairs={{0,12},{4,0},{8,4},{12,8},{1,13},{5,1},{9,5},{13,9},{2,14},{6,2},{... | collective-permute-start | bytes 688136 | tf_op jit(solution)/shard_map/gather_ring/ppermute | solution.py:14
  96.7 7.6 %collective-permute-start.22 = (bf16[128,896]{1,0:T(8,128)(2,1)S(1)}, bf16[128,896]{1,0:T(8,128)(2,1)S(1)}, u32[]{:S(2)}, u32[]{:S(2)}) collective-permute-start(bf16[128,896]{1,0:T(8,128)(2,1)S(1)} %add_convert_fusion), channel_id=1, source_target_pairs={{0,8},{4,12},{8,0},{12,4},{1,9},{5,13},{9,1},{13,5},{2,10},{6,14},... | collective-permute-start | bytes 688136 | tf_op jit(solution)/shard_map/gather_ring/ppermute | solution.py:14
  97.2 13.5 %collective-permute-start.21 = (bf16[128,896]{1,0:T(8,128)(2,1)S(1)}, bf16[128,896]{1,0:T(8,128)(2,1)S(1)}, u32[]{:S(2)}, u32[]{:S(2)}) collective-permute-start(bf16[128,896]{1,0:T(8,128)(2,1)S(1)} %add_convert_fusion), channel_id=1, source_target_pairs={{0,4},{4,8},{8,12},{12,0},{1,5},{5,9},{9,13},{13,1},{2,6},{6,10},{... | collective-permute-start | bytes 688136 | tf_op jit(solution)/shard_map/gather_ring/ppermute | solution.py:14
  97.9 12.9 %collective-permute-start.25 = (bf16[256,512]{1,0:T(8,128)(2,1)S(1)}, bf16[256,512]{1,0:T(8,128)(2,1)S(1)}, u32[]{:S(2)}, u32[]{:S(2)}) collective-permute-start(bf16[256,512]{1,0:T(8,128)(2,1)S(1)} %pad_maximum_fusion.4), channel_id=1, source_target_pairs={{0,16},{16,0},{32,48},{48,32},{1,17},{17,1},{33,49},{49,33},{2,18}... | collective-permute-start | bytes 786440 | tf_op jit(solution)/shard_map/sum_grads/ppermute | solution.py:19
  110.8 2.9 %collective-permute-start.26 = (bf16[512,896]{1,0:T(8,128)(2,1)S(1)}, bf16[512,896]{1,0:T(8,128)(2,1)S(1)}, u32[]{:S(2)}, u32[]{:S(2)}) collective-permute-start(bf16[512,896]{1,0:T(8,128)(2,1)S(1)} %pad_maximum_fusion), channel_id=1, source_target_pairs={{0,1},{1,0},{2,3},{3,2},{4,5},{5,4},{6,7},{7,6},{8,9},{9,8},{10,11... | collective-permute-start | bytes 2752520 | tf_op jit(solution)/shard_map/gather_ring/ppermute | solution.py:19

commit v4 on v3

--- a/solution.py
+++ b/solution.py
@@ -80,17 +80,15 @@
     totals[0], sums = tie(totals[0], sums)
     with jax.named_scope("sum_grads"):
         sums = sums + swap(sums.astype(BF16), "zl", 1).astype(F32)
-        sums = sums + swap(sums.astype(BF16), "zl", 2).astype(F32)
-        grad_rot = sums.astype(BF16)
     columns = []
     for total in totals:
         with jax.named_scope("sum_far"):
             mine = (total + swap(total.astype(BF16), "zh").astype(F32)).astype(BF16)
         if not columns:
-            mine, grad_rot = tie(mine, grad_rot)
+            mine, sums = tie(mine, sums)
             with jax.named_scope("sum_grads"):
-                grad_rot = jnp.concatenate([grad_rot, swap(grad_rot, "y", 2)])
-                grad_rot = jnp.concatenate([grad_rot, swap(grad_rot, "y", 1)])
+                part = (sums + swap(sums.astype(BF16), "zl", 2).astype(F32)).astype(BF16)
+                grad_rot = jnp.concatenate([part] + [shift(part, "y", s) for s in (1, 2, 3)])
         with jax.named_scope("gather_ring"):
             own = jnp.concatenate([mine] + [shift(mine, "x", s) for s in (1, 2, 3)])
             if not columns:
@@ -110,7 +108,8 @@
         row = lax.broadcasted_iota(jnp.int32, (1, example_ids.shape[0]), 1)
         within, outer, inner = row % block, row // group, row // block % 4
         act_token = ((zl ^ inner) * 4 + (y - x + outer) % 4) * block + within
-        gathered = ((y % 2) ^ (row // (2 * group))) * 8 + ((y // 2) ^ (outer % 2)) * 4 + inner
+        owner = (y - outer) % 4
+        gathered = owner % 2 * 8 + owner // 2 * 4 + inner
         from_x = (x - gathered // 2 % 4) % 4
         grad_token = (from_x * 4 + (zh ^ (gathered % 2)) * 2 + (core ^ (gathered // 8))) * block + within
         bounds = jnp.sum(example_ids[None, :] < jnp.arange(examples + 1)[:, None], axis=1)

time: 136 us -> 131 us (0.963)
  waiting for transfers between devices: 62.7 us -> 51.3 us
  starting transfers between devices: 40 us -> 45.4 us
    ppermute x12 -> x15, waiting for transfers between devices: 38.8 us -> 31.4 us  [shift(): return lax.ppermute(a, axis, [(i, (i + by) % 4) for i in range(4)])]
    ppermute x12 -> x15, starting transfers between devices: 17.9 us -> 23.2 us  [shift(): return lax.ppermute(a, axis, [(i, (i + by) % 4) for i in range(4)])]
    ppermute x15 -> x13, waiting for transfers between devices: 23.9 us -> 19.9 us  [swap(): return lax.ppermute(a, axis, [(i, i ^ by) for i in range(size)])]
    ppermute x15 -> x13, starting transfers between devices: 22.1 us -> 22.2 us  [swap(): return lax.ppermute(a, axis, [(i, i ^ by) for i in range(size)])]
  transfers between devices with their start and end apart: 27 -> 28, of which waited for: 18 -> 17; matrix products, arithmetic and copies ran while one was open for 7% -> 7% of each run, Pallas kernels for 0% -> 0%
where the time goes in v4:
time: 131 us; the launch traced here: 130 us
  waiting for transfers between devices  51.3 us (39%)
  starting transfers between devices  45.4 us (35%)
  matrix products  28.6 us (22%)
  other arithmetic  2.68 us (2%)
    ppermute x15, waiting for transfers between devices, shift(): return lax.ppermute(a, axis, [(i, (i + by) % 4) for i in range(4)])  31.4 us
    ppermute x15, starting transfers between devices, shift(): return lax.ppermute(a, axis, [(i, (i + by) % 4) for i in range(4)])  23.2 us
    ppermute x13, starting transfers between devices, swap(): return lax.ppermute(a, axis, [(i, i ^ by) for i in range(size)])  22.2 us
    ppermute x13, waiting for transfers between devices, swap(): return lax.ppermute(a, axis, [(i, i ^ by) for i in range(size)])  19.9 us
    dot_general x1, matrix products, local(): jnp.einsum('eki,ekj->eij', grad_rows, act_rows, preferred_element_type=F32)  19.3 us
    dot_general x7, matrix products, dot(): return jnp.dot(a, b, preferred_element_type=F32)  9.34 us
  transfers between devices with their start and end apart: 28, of which 17 were waited for; matrix products, arithmetic and copies ran while one was open for 7% of the time, Pallas kernels for 0%

profile of v4, /device:TPU:1, one launch (start us, length us, event | category | flops | bytes accessed | tf_op | source)
XLA Modules:
  0.0 129.6 jit_solution(4709612923468873137)
XLA Ops:
  0.0 7.7 %collective-permute-start.3 = (bf16[32,512]{1,0:T(8,128)(2,1)}, bf16[32,512]{1,0:T(8,128)(2,1)S(1)}, u32[]{:S(2)}, u32[]{:S(2)}) collective-permute-start(bf16[32,512]{1,0:T(8,128)(2,1)} %param.6), channel_id=1, source_target_pairs={{0,2},{2,0},{1,3},{3,1},{4,6},{6,4},{5,7},{7,5},{8,10},{10,8},{9,1... | collective-permute-start | bytes 98312 | tf_op jit(solution)/shard_map/gather_grads/ppermute | solution.py:19
  7.7 1.2 collective-permute-start.1
  9.7 1.6 %collective-permute-start.2 = (bf16[32,1792]{1,0:T(8,128)(2,1)}, bf16[32,1792]{1,0:T(8,128)(2,1)S(1)}, u32[]{:S(2)}, u32[]{:S(2)}) collective-permute-start(bf16[32,1792]{1,0:T(8,128)(2,1)} %param.5), channel_id=1, source_target_pairs={{0,192},{64,128},{128,64},{192,0},{1,193},{65,129},{129,65},{193,1... | collective-permute-start | bytes 344072 | tf_op jit(solution)/shard_map/gather_line/ppermute | solution.py:19
  12.1 4.3 %collective-permute-done.1 = bf16[32,1792]{1,0:T(8,128)(2,1)S(1)} collective-permute-done((bf16[32,1792]{1,0:T(8,128)(2,1)}, bf16[32,1792]{1,0:T(8,128)(2,1)S(1)}, u32[]{:S(2)}, u32[]{:S(2)}) %collective-permute-start.1) | collective-permute-done | bytes 114720 | tf_op jit(solution)/shard_map/gather_line/ppermute | solution.py:19
  16.3 2.3 %collective-permute-done.2 = bf16[32,1792]{1,0:T(8,128)(2,1)S(1)} collective-permute-done((bf16[32,1792]{1,0:T(8,128)(2,1)}, bf16[32,1792]{1,0:T(8,128)(2,1)S(1)}, u32[]{:S(2)}, u32[]{:S(2)}) %collective-permute-start.2) | collective-permute-done | bytes 114720 | tf_op jit(solution)/shard_map/gather_line/ppermute | solution.py:19
  19.6 2.8 %collective-permute-start.6 = (bf16[128,1792]{1,0:T(8,128)(2,1)S(1)}, bf16[128,1792]{1,0:T(8,128)(2,1)S(1)}, u32[]{:S(2)}, u32[]{:S(2)}) collective-permute-start(bf16[128,1792]{1,0:T(8,128)(2,1)S(1)} %pad_maximum_fusion.2), channel_id=1, source_target_pairs={{0,48},{16,0},{32,16},{48,32},{1,49},{17,1},{33,17},{49,33},{2,50}... | collective-permute-start | bytes 1376264 | tf_op jit(solution)/shard_map/gather_plane/ppermute | solution.py:14
  23.4 2.5 %collective-permute-start.9 = (bf16[64,512]{1,0:T(8,128)(2,1)S(1)}, bf16[64,512]{1,0:T(8,128)(2,1)S(1)}, u32[]{:S(2)}, u32[]{:S(2)}) collective-permute-start(bf16[64,512]{1,0:T(8,128)(2,1)S(1)} %pad_maximum_fusion.7), channel_id=1, source_target_pairs={{0,12},{4,0},{8,4},{12,8},{1,13},{5,1},{9,5},{13,9},{2,14},{6,2},{... | collective-permute-start | bytes 196616 | tf_op jit(solution)/shard_map/gather_grads/ppermute | solution.py:14
  28.1 2.7 %collective-permute-done.8 = bf16[64,512]{1,0:T(8,128)(2,1)S(1)} collective-permute-done((bf16[64,512]{1,0:T(8,128)(2,1)S(1)}, bf16[64,512]{1,0:T(8,128)(2,1)S(1)}, u32[]{:S(2)}, u32[]{:S(2)}) %collective-permute-start.8) | collective-permute-done | bytes 65568 | tf_op jit(solution)/shard_map/gather_grads/ppermute | solution.py:14
  30.8 1.4 %collective-permute-done.7 = bf16[64,512]{1,0:T(8,128)(2,1)S(1)} collective-permute-done((bf16[64,512]{1,0:T(8,128)(2,1)S(1)}, bf16[64,512]{1,0:T(8,128)(2,1)S(1)}, u32[]{:S(2)}, u32[]{:S(2)}) %collective-permute-start.7) | collective-permute-done | bytes 65568 | tf_op jit(solution)/shard_map/gather_grads/ppermute | solution.py:14
  32.2 1.9 %collective-permute-done.5 = bf16[128,1792]{1,0:T(8,128)(2,1)S(1)} collective-permute-done((bf16[128,1792]{1,0:T(8,128)(2,1)S(1)}, bf16[128,1792]{1,0:T(8,128)(2,1)S(1)}, u32[]{:S(2)}, u32[]{:S(2)}) %collective-permute-start.5) | collective-permute-done | bytes 458784 | tf_op jit(solution)/shard_map/gather_plane/ppermute | solution.py:14
  34.1 12.1 %collective-permute-done.4 = bf16[128,1792]{1,0:T(8,128)(2,1)S(1)} collective-permute-done((bf16[128,1792]{1,0:T(8,128)(2,1)S(1)}, bf16[128,1792]{1,0:T(8,128)(2,1)S(1)}, u32[]{:S(2)}, u32[]{:S(2)}) %collective-permute-start.4) | collective-permute-done | bytes 458784 | tf_op jit(solution)/shard_map/gather_plane/ppermute | solution.py:14
  46.8 2.6 %fusion.30 = bf16[512,384]{1,0:T(8,128)(2,1)S(1)} fusion(bf16[512,1792]{1,0:T(8,128)(2,1)S(1)} %constant_dynamic-update-slice_fusion, bf16[1792,1792]{1,0:T(8,128)(2,1)} %param.7, s32[]{:T(128)S(6)} %select_n.256), kind=kOutput, calls=%fused_computation.24 | convolution fusion | flops 704839680 | bytes 3604484 | tf_op jit(solution)/shard_map/rotate/dot_general | solution.py:27
  49.9 1.1 fusion.24
  52.0 1.1 fusion.27
  53.2 1.1 fusion.21
  54.5 2.8 %collective-permute-start.13 = (bf16[128,896]{1,0:T(8,128)(2,1)S(1)}, bf16[128,896]{1,0:T(8,128)(2,1)S(1)}, u32[]{:S(2)}, u32[]{:S(2)}) collective-permute-start(bf16[128,896]{1,0:T(8,128)(2,1)S(1)} %pad_maximum_fusion.5), channel_id=1, source_target_pairs={{0,8},{4,12},{8,0},{12,4},{1,9},{5,13},{9,1},{13,5},{2,10},{6,14},... | collective-permute-start | bytes 688136 | tf_op jit(solution)/shard_map/sum_ring/ppermute | solution.py:14
  57.3 0.9 collective-permute-start.14
  59.5 1.1 collective-permute-start.17
  60.7 2.1 %collective-permute-done.13 = bf16[128,896]{1,0:T(8,128)(2,1)S(1)} collective-permute-done((bf16[128,896]{1,0:T(8,128)(2,1)S(1)}, bf16[128,896]{1,0:T(8,128)(2,1)S(1)}, u32[]{:S(2)}, u32[]{:S(2)}) %collective-permute-start.13) | collective-permute-done | bytes 229408 | tf_op jit(solution)/shard_map/sum_ring/ppermute | solution.py:14
  62.8 5.0 %collective-permute-done.14 = bf16[128,896]{1,0:T(8,128)(2,1)S(1)} collective-permute-done((bf16[128,896]{1,0:T(8,128)(2,1)S(1)}, bf16[128,896]{1,0:T(8,128)(2,1)S(1)}, u32[]{:S(2)}, u32[]{:S(2)}) %collective-permute-start.14) | collective-permute-done | bytes 229408 | tf_op jit(solution)/shard_map/sum_ring/ppermute | solution.py:14
  68.3 2.9 %collective-permute-start.19 = (bf16[128,512]{1,0:T(8,128)(2,1)S(1)}, bf16[128,512]{1,0:T(8,128)(2,1)S(1)}, u32[]{:S(2)}, u32[]{:S(2)}) collective-permute-start(bf16[128,512]{1,0:T(8,128)(2,1)S(1)} %convert_element_type.82), channel_id=1, source_target_pairs={{0,64},{64,0},{128,192},{192,128},{1,65},{65,1},{129,193},{193,129... | collective-permute-start | bytes 393224 | tf_op jit(solution)/shard_map/sum_grads/ppermute | solution.py:19
  71.2 1.3 %collective-permute-start.18 = (bf16[128,896]{1,0:T(8,128)(2,1)S(1)}, bf16[128,896]{1,0:T(8,128)(2,1)S(1)}, u32[]{:S(2)}, u32[]{:S(2)}) collective-permute-start(bf16[128,896]{1,0:T(8,128)(2,1)S(1)} %convert_element_type.79), channel_id=1, source_target_pairs={{0,2},{2,0},{1,3},{3,1},{4,6},{6,4},{5,7},{7,5},{8,10},{10,8},{9,1... | collective-permute-start | bytes 688136 | tf_op jit(solution)/shard_map/sum_far/ppermute | solution.py:19
  72.6 1.0 collective-permute-done.19
  73.6 10.5 %collective-permute-done.18 = bf16[128,896]{1,0:T(8,128)(2,1)S(1)} collective-permute-done((bf16[128,896]{1,0:T(8,128)(2,1)S(1)}, bf16[128,896]{1,0:T(8,128)(2,1)S(1)}, u32[]{:S(2)}, u32[]{:S(2)}) %collective-permute-start.18) | collective-permute-done | bytes 229408 | tf_op jit(solution)/shard_map/sum_far/ppermute | solution.py:19
  84.7 3.8 %collective-permute-start.22 = (bf16[128,896]{1,0:T(8,128)(2,1)S(1)}, bf16[128,896]{1,0:T(8,128)(2,1)S(1)}, u32[]{:S(2)}, u32[]{:S(2)}) collective-permute-start(bf16[128,896]{1,0:T(8,128)(2,1)S(1)} %add_convert_fusion), channel_id=1, source_target_pairs={{0,12},{4,0},{8,4},{12,8},{1,13},{5,1},{9,5},{13,9},{2,14},{6,2},{... | collective-permute-start | bytes 688136 | tf_op jit(solution)/shard_map/gather_ring/ppermute | solution.py:14
  90.0 1.0 collective-permute-start.26
  91.0 3.7 %collective-permute-start.25 = (bf16[128,512]{1,0:T(8,128)(2,1)S(1)}, bf16[128,512]{1,0:T(8,128)(2,1)S(1)}, u32[]{:S(2)}, u32[]{:S(2)}) collective-permute-start(bf16[128,512]{1,0:T(8,128)(2,1)S(1)} %add_convert_fusion.1), channel_id=1, source_target_pairs={{0,32},{16,48},{32,0},{48,16},{1,33},{17,49},{33,1},{49,17},{2,34}... | collective-permute-start | bytes 393224 | tf_op jit(solution)/shard_map/sum_grads/ppermute | solution.py:14
  94.8 1.5 %collective-permute-start.24 = (bf16[128,512]{1,0:T(8,128)(2,1)S(1)}, bf16[128,512]{1,0:T(8,128)(2,1)S(1)}, u32[]{:S(2)}, u32[]{:S(2)}) collective-permute-start(bf16[128,512]{1,0:T(8,128)(2,1)S(1)} %add_convert_fusion.1), channel_id=1, source_target_pairs={{0,16},{16,32},{32,48},{48,0},{1,17},{17,33},{33,49},{49,1},{2,18}... | collective-permute-start | bytes 393224 | tf_op jit(solution)/shard_map/sum_grads/ppermute | solution.py:14
  96.2 4.9 %collective-permute-done.20 = bf16[128,896]{1,0:T(8,128)(2,1)S(1)} collective-permute-done((bf16[128,896]{1,0:T(8,128)(2,1)S(1)}, bf16[128,896]{1,0:T(8,128)(2,1)S(1)}, u32[]{:S(2)}, u32[]{:S(2)}) %collective-permute-start.20) | collective-permute-done | bytes 229408 | tf_op jit(solution)/shard_map/gather_ring/ppermute | solution.py:14
  101.5 4.2 %collective-permute-start.27 = (bf16[512,896]{1,0:T(8,128)(2,1)S(1)}, bf16[512,896]{1,0:T(8,128)(2,1)S(1)}, u32[]{:S(2)}, u32[]{:S(2)}) collective-permute-start(bf16[512,896]{1,0:T(8,128)(2,1)S(1)} %pad_maximum_fusion), channel_id=1, source_target_pairs={{0,1},{1,0},{2,3},{3,2},{4,5},{5,4},{6,7},{7,6},{8,9},{9,8},{10,11... | collective-permute-start | bytes 2752520 | tf_op jit(solution)/shard_map/gather_ring/ppermute | solution.py:19
  108.2 2.2 %convolution_convert_fusion = bf16[1024,1792]{1,0:T(8,128)(2,1)S(1)} fusion(bf16[512,384]{1,0:T(8,128)(2,1)S(1)} %slice.27, bf16[512,384]{1,0:T(8,128)(2,1)S(1)} %slice.26, bf16[512,512]{1,0:T(8,128)(2,1)S(1)} %slice.25, bf16[512,512]{1,0:T(8,128)(2,1)S(1)} %slice.24, s32[512]{0:T(512)S(1)} %get-tuple-element.39, s32[1024]{0:T(1024)S(1)} %compare_select_fusion), kind=kOutput, calls=%fused_computation.1 | convolution fusion | flops 1888747520 | bytes 5511168 | tf_op jit(solution)/shard_map/squares/dot_general | solution.py:27
  110.3 19.3 %multiply_reduce_fusion = f32[512,1792]{1,0:T(8,128)} fusion(bf16[32,32,512]{2,1,0:T(8,128)(2,1)S(1)} %bitcast.47, bf16[32,32,1792]{2,1,0:T(8,128)(2,1)S(1)} %bitcast.46), kind=kOutput, calls=%fused_computation | convolution fusion | flops 1966211072 | bytes 8388608 | tf_op jit(solution)/shard_map/squares/eki,ekj->eij/dot_general | solution.py:125
  (78 shorter events, 14.5 us)
Async XLA Ops:
  0.0 51.2 %copy-start = (bf16[512,512]{1,0:T(8,128)(2,1)S(1)}, bf16[512,512]{1,0:T(8,128)(2,1)}, u32[]{:S(2)}) copy-start(bf16[512,512]{1,0:T(8,128)(2,1)} %param.8) | copy-start | bytes 1572868
  0.0 11.3 %collective-permute-start.3 = (bf16[32,512]{1,0:T(8,128)(2,1)}, bf16[32,512]{1,0:T(8,128)(2,1)S(1)}, u32[]{:S(2)}, u32[]{:S(2)}) collective-permute-start(bf16[32,512]{1,0:T(8,128)(2,1)} %param.6), channel_id=1, source_target_pairs={{0,2},{2,0},{1,3},{3,1},{4,6},{6,4},{5,7},{7,5},{8,10},{10,8},{9,1... | collective-permute-start | bytes 98312 | tf_op jit(solution)/shard_map/gather_grads/ppermute | solution.py:19
  7.7 8.6 %collective-permute-start.1 = (bf16[32,1792]{1,0:T(8,128)(2,1)}, bf16[32,1792]{1,0:T(8,128)(2,1)S(1)}, u32[]{:S(2)}, u32[]{:S(2)}) collective-permute-start(bf16[32,1792]{1,0:T(8,128)(2,1)} %param.5), channel_id=1, source_target_pairs={{0,128},{64,192},{128,0},{192,64},{1,129},{65,193},{129,1},{193,65... | collective-permute-start | bytes 344072 | tf_op jit(solution)/shard_map/gather_line/ppermute | solution.py:19
  8.9 7.4 %collective-permute-start = (bf16[32,1792]{1,0:T(8,128)(2,1)}, bf16[32,1792]{1,0:T(8,128)(2,1)S(1)}, u32[]{:S(2)}, u32[]{:S(2)}) collective-permute-start(bf16[32,1792]{1,0:T(8,128)(2,1)} %param.5), channel_id=1, source_target_pairs={{0,64},{64,0},{128,192},{192,128},{1,65},{65,1},{129,193},{193,129... | collective-permute-start | bytes 344072 | tf_op jit(solution)/shard_map/gather_line/ppermute | solution.py:19
  9.7 9.0 %collective-permute-start.2 = (bf16[32,1792]{1,0:T(8,128)(2,1)}, bf16[32,1792]{1,0:T(8,128)(2,1)S(1)}, u32[]{:S(2)}, u32[]{:S(2)}) collective-permute-start(bf16[32,1792]{1,0:T(8,128)(2,1)} %param.5), channel_id=1, source_target_pairs={{0,192},{64,128},{128,64},{192,0},{1,193},{65,129},{129,65},{193,1... | collective-permute-start | bytes 344072 | tf_op jit(solution)/shard_map/gather_line/ppermute | solution.py:19
  19.6 12.6 %collective-permute-start.6 = (bf16[128,1792]{1,0:T(8,128)(2,1)S(1)}, bf16[128,1792]{1,0:T(8,128)(2,1)S(1)}, u32[]{:S(2)}, u32[]{:S(2)}) collective-permute-start(bf16[128,1792]{1,0:T(8,128)(2,1)S(1)} %pad_maximum_fusion.2), channel_id=1, source_target_pairs={{0,48},{16,0},{32,16},{48,32},{1,49},{17,1},{33,17},{49,33},{2,50}... | collective-permute-start | bytes 1376264 | tf_op jit(solution)/shard_map/gather_plane/ppermute | solution.py:14
  22.4 11.7 %collective-permute-start.5 = (bf16[128,1792]{1,0:T(8,128)(2,1)S(1)}, bf16[128,1792]{1,0:T(8,128)(2,1)S(1)}, u32[]{:S(2)}, u32[]{:S(2)}) collective-permute-start(bf16[128,1792]{1,0:T(8,128)(2,1)S(1)} %pad_maximum_fusion.2), channel_id=1, source_target_pairs={{0,32},{16,48},{32,0},{48,16},{1,33},{17,49},{33,1},{49,17},{2,34}... | collective-permute-start | bytes 1376264 | tf_op jit(solution)/shard_map/gather_plane/ppermute | solution.py:14
  22.7 23.4 %collective-permute-start.4 = (bf16[128,1792]{1,0:T(8,128)(2,1)S(1)}, bf16[128,1792]{1,0:T(8,128)(2,1)S(1)}, u32[]{:S(2)}, u32[]{:S(2)}) collective-permute-start(bf16[128,1792]{1,0:T(8,128)(2,1)S(1)} %pad_maximum_fusion.2), channel_id=1, source_target_pairs={{0,16},{16,32},{32,48},{48,0},{1,17},{17,33},{33,49},{49,1},{2,18}... | collective-permute-start | bytes 1376264 | tf_op jit(solution)/shard_map/gather_plane/ppermute | solution.py:14
  23.4 3.8 %collective-permute-start.9 = (bf16[64,512]{1,0:T(8,128)(2,1)S(1)}, bf16[64,512]{1,0:T(8,128)(2,1)S(1)}, u32[]{:S(2)}, u32[]{:S(2)}) collective-permute-start(bf16[64,512]{1,0:T(8,128)(2,1)S(1)} %pad_maximum_fusion.7), channel_id=1, source_target_pairs={{0,12},{4,0},{8,4},{12,8},{1,13},{5,1},{9,5},{13,9},{2,14},{6,2},{... | collective-permute-start | bytes 196616 | tf_op jit(solution)/shard_map/gather_grads/ppermute | solution.py:14
  25.9 4.9 %collective-permute-start.8 = (bf16[64,512]{1,0:T(8,128)(2,1)S(1)}, bf16[64,512]{1,0:T(8,128)(2,1)S(1)}, u32[]{:S(2)}, u32[]{:S(2)}) collective-permute-start(bf16[64,512]{1,0:T(8,128)(2,1)S(1)} %pad_maximum_fusion.7), channel_id=1, source_target_pairs={{0,8},{4,12},{8,0},{12,4},{1,9},{5,13},{9,1},{13,5},{2,10},{6,14},... | collective-permute-start | bytes 196616 | tf_op jit(solution)/shard_map/gather_grads/ppermute | solution.py:14
  27.2 4.9 %collective-permute-start.7 = (bf16[64,512]{1,0:T(8,128)(2,1)S(1)}, bf16[64,512]{1,0:T(8,128)(2,1)S(1)}, u32[]{:S(2)}, u32[]{:S(2)}) collective-permute-start(bf16[64,512]{1,0:T(8,128)(2,1)S(1)} %pad_maximum_fusion.7), channel_id=1, source_target_pairs={{0,4},{4,8},{8,12},{12,0},{1,5},{5,9},{9,13},{13,1},{2,6},{6,10},{... | collective-permute-start | bytes 196616 | tf_op jit(solution)/shard_map/gather_grads/ppermute | solution.py:14
  46.2 5.1 %collective-permute-start.15 = (bf16[256,512]{1,0:T(8,128)(2,1)S(1)}, bf16[256,512]{1,0:T(8,128)(2,1)S(1)}, u32[]{:S(2)}, u32[]{:S(2)}) collective-permute-start(bf16[256,512]{1,0:T(8,128)(2,1)S(1)} %pad_maximum_fusion.3), channel_id=1, source_target_pairs={{0,1},{1,0},{2,3},{3,2},{4,5},{5,4},{6,7},{7,6},{8,9},{9,8},{10,11... | collective-permute-start | bytes 786440 | tf_op jit(solution)/shard_map/gather_grads/ppermute | solution.py:19
  46.7 3.3 %copy-start.2 = (bf16[1792,1792]{1,0:T(8,128)(2,1)S(1)}, bf16[1792,1792]{1,0:T(8,128)(2,1)}, u32[]{:S(2)}) copy-start(bf16[1792,1792]{1,0:T(8,128)(2,1)} %param.7) | copy-start | bytes 19267588
  49.4 2.6 %collective-permute-start.11 = (bf16[512,384]{1,0:T(8,128)(2,1)S(1)}, bf16[512,384]{1,0:T(8,128)(2,1)S(1)}, u32[]{:S(2)}, u32[]{:S(2)}) collective-permute-start(bf16[512,384]{1,0:T(8,128)(2,1)S(1)} %fusion.30), channel_id=1, source_target_pairs={{0,1},{1,0},{2,3},{3,2},{4,5},{5,4},{6,7},{7,6},{8,9},{9,8},{10,11... | collective-permute-start | bytes 1179656 | tf_op jit(solution)/shard_map/rotate/ppermute | solution.py:19
  51.1 2.2 %collective-permute-start.10 = (bf16[512,512]{1,0:T(8,128)(2,1)S(1)}, bf16[512,512]{1,0:T(8,128)(2,1)S(1)}, u32[]{:S(2)}, u32[]{:S(2)}) collective-permute-start(bf16[512,512]{1,0:T(8,128)(2,1)S(1)} %fusion.24), channel_id=1, source_target_pairs={{0,1},{1,0},{2,3},{3,2},{4,5},{5,4},{6,7},{7,6},{8,9},{9,8},{10,11... | collective-permute-start | bytes 1572872 | tf_op jit(solution)/shard_map/rotate/ppermute | solution.py:19
  51.7 7.7 %collective-permute-start.16 = (bf16[256,512]{1,0:T(8,128)(2,1)S(1)}, bf16[256,512]{1,0:T(8,128)(2,1)S(1)}, u32[]{:S(2)}, u32[]{:S(2)}) collective-permute-start(bf16[256,512]{1,0:T(8,128)(2,1)S(1)} %fusion.43), channel_id=1, source_target_pairs={{0,16},{16,0},{32,48},{48,32},{1,17},{17,1},{33,49},{49,33},{2,18}... | collective-permute-start | bytes 786440 | tf_op jit(solution)/shard_map/sum_grads/ppermute | solution.py:19
  54.5 8.3 %collective-permute-start.13 = (bf16[128,896]{1,0:T(8,128)(2,1)S(1)}, bf16[128,896]{1,0:T(8,128)(2,1)S(1)}, u32[]{:S(2)}, u32[]{:S(2)}) collective-permute-start(bf16[128,896]{1,0:T(8,128)(2,1)S(1)} %pad_maximum_fusion.5), channel_id=1, source_target_pairs={{0,8},{4,12},{8,0},{12,4},{1,9},{5,13},{9,1},{13,5},{2,10},{6,14},... | collective-permute-start | bytes 688136 | tf_op jit(solution)/shard_map/sum_ring/ppermute | solution.py:14
  57.3 10.5 %collective-permute-start.14 = (bf16[128,896]{1,0:T(8,128)(2,1)S(1)}, bf16[128,896]{1,0:T(8,128)(2,1)S(1)}, u32[]{:S(2)}, u32[]{:S(2)}) collective-permute-start(bf16[128,896]{1,0:T(8,128)(2,1)S(1)} %pad_maximum_fusion.6), channel_id=1, source_target_pairs={{0,12},{4,0},{8,4},{12,8},{1,13},{5,1},{9,5},{13,9},{2,14},{6,2},{... | collective-permute-start | bytes 688136 | tf_op jit(solution)/shard_map/sum_ring/ppermute | solution.py:14
  58.3 9.8 %collective-permute-start.12 = (bf16[128,896]{1,0:T(8,128)(2,1)S(1)}, bf16[128,896]{1,0:T(8,128)(2,1)S(1)}, u32[]{:S(2)}, u32[]{:S(2)}) collective-permute-start(bf16[128,896]{1,0:T(8,128)(2,1)S(1)} %pad_maximum_fusion.4), channel_id=1, source_target_pairs={{0,4},{4,8},{8,12},{12,0},{1,5},{5,9},{9,13},{13,1},{2,6},{6,10},{... | collective-permute-start | bytes 688136 | tf_op jit(solution)/shard_map/sum_ring/ppermute | solution.py:14
  59.5 8.7 %collective-permute-start.17 = (f32[128,512]{1,0:T(8,128)S(1)}, f32[128,512]{1,0:T(8,128)S(1)}, u32[]{:S(2)}, u32[]{:S(2)}) collective-permute-start(f32[128,512]{1,0:T(8,128)S(1)} %dynamic-slice_bitcast_fusion), channel_id=1, source_target_pairs={{0,32},{16,48},{32,0},{48,16},{1,33},{17,49},{33,1},{49,17},{2,34}... | collective-permute-start | bytes 786440 | tf_op jit(solution)/shard_map/sum_grads/ppermute | solution.py:19
  68.2 16.4 %copy-start.1 = (s32[512]{0:T(512)S(1)}, s32[512]{0:T(512)}, u32[]{:S(2)}) copy-start(s32[512]{0:T(512)} %param.9) | copy-start | bytes 6148
  68.3 5.3 %collective-permute-start.19 = (bf16[128,512]{1,0:T(8,128)(2,1)S(1)}, bf16[128,512]{1,0:T(8,128)(2,1)S(1)}, u32[]{:S(2)}, u32[]{:S(2)}) collective-permute-start(bf16[128,512]{1,0:T(8,128)(2,1)S(1)} %convert_element_type.82), channel_id=1, source_target_pairs={{0,64},{64,0},{128,192},{192,128},{1,65},{65,1},{129,193},{193,129... | collective-permute-start | bytes 393224 | tf_op jit(solution)/shard_map/sum_grads/ppermute | solution.py:19
  71.2 12.9 %collective-permute-start.18 = (bf16[128,896]{1,0:T(8,128)(2,1)S(1)}, bf16[128,896]{1,0:T(8,128)(2,1)S(1)}, u32[]{:S(2)}, u32[]{:S(2)}) collective-permute-start(bf16[128,896]{1,0:T(8,128)(2,1)S(1)} %convert_element_type.79), channel_id=1, source_target_pairs={{0,2},{2,0},{1,3},{3,1},{4,6},{6,4},{5,7},{7,5},{8,10},{10,8},{9,1... | collective-permute-start | bytes 688136 | tf_op jit(solution)/shard_map/sum_far/ppermute | solution.py:19
  84.2 5.8 %collective-permute-start.23 = (bf16[128,512]{1,0:T(8,128)(2,1)S(1)}, bf16[128,512]{1,0:T(8,128)(2,1)S(1)}, u32[]{:S(2)}, u32[]{:S(2)}) collective-permute-start(bf16[128,512]{1,0:T(8,128)(2,1)S(1)} %convert_element_type.84), channel_id=1, source_target_pairs={{0,128},{64,192},{128,0},{192,64},{1,129},{65,193},{129,1},{193,65... | collective-permute-start | bytes 393224 | tf_op jit(solution)/shard_map/sum_grads/ppermute | solution.py:19
  84.7 10.1 %collective-permute-start.22 = (bf16[128,896]{1,0:T(8,128)(2,1)S(1)}, bf16[128,896]{1,0:T(8,128)(2,1)S(1)}, u32[]{:S(2)}, u32[]{:S(2)}) collective-permute-start(bf16[128,896]{1,0:T(8,128)(2,1)S(1)} %add_convert_fusion), channel_id=1, source_target_pairs={{0,12},{4,0},{8,4},{12,8},{1,13},{5,1},{9,5},{13,9},{2,14},{6,2},{... | collective-permute-start | bytes 688136 | tf_op jit(solution)/shard_map/gather_ring/ppermute | solution.py:14
  88.4 7.8 %collective-permute-start.21 = (bf16[128,896]{1,0:T(8,128)(2,1)S(1)}, bf16[128,896]{1,0:T(8,128)(2,1)S(1)}, u32[]{:S(2)}, u32[]{:S(2)}) collective-permute-start(bf16[128,896]{1,0:T(8,128)(2,1)S(1)} %add_convert_fusion), channel_id=1, source_target_pairs={{0,8},{4,12},{8,0},{12,4},{1,9},{5,13},{9,1},{13,5},{2,10},{6,14},... | collective-permute-start | bytes 688136 | tf_op jit(solution)/shard_map/gather_ring/ppermute | solution.py:14
  88.9 12.2 %collective-permute-start.20 = (bf16[128,896]{1,0:T(8,128)(2,1)S(1)}, bf16[128,896]{1,0:T(8,128)(2,1)S(1)}, u32[]{:S(2)}, u32[]{:S(2)}) collective-permute-start(bf16[128,896]{1,0:T(8,128)(2,1)S(1)} %add_convert_fusion), channel_id=1, source_target_pairs={{0,4},{4,8},{8,12},{12,0},{1,5},{5,9},{9,13},{13,1},{2,6},{6,10},{... | collective-permute-start | bytes 688136 | tf_op jit(solution)/shard_map/gather_ring/ppermute | solution.py:14
  90.0 11.2 %collective-permute-start.26 = (bf16[128,512]{1,0:T(8,128)(2,1)S(1)}, bf16[128,512]{1,0:T(8,128)(2,1)S(1)}, u32[]{:S(2)}, u32[]{:S(2)}) collective-permute-start(bf16[128,512]{1,0:T(8,128)(2,1)S(1)} %add_convert_fusion.1), channel_id=1, source_target_pairs={{0,48},{16,0},{32,16},{48,32},{1,49},{17,1},{33,17},{49,33},{2,50}... | collective-permute-start | bytes 393224 | tf_op jit(solution)/shard_map/sum_grads/ppermute | solution.py:14
  91.0 10.2 %collective-permute-start.25 = (bf16[128,512]{1,0:T(8,128)(2,1)S(1)}, bf16[128,512]{1,0:T(8,128)(2,1)S(1)}, u32[]{:S(2)}, u32[]{:S(2)}) collective-permute-start(bf16[128,512]{1,0:T(8,128)(2,1)S(1)} %add_convert_fusion.1), channel_id=1, source_target_pairs={{0,32},{16,48},{32,0},{48,16},{1,33},{17,49},{33,1},{49,17},{2,34}... | collective-permute-start | bytes 393224 | tf_op jit(solution)/shard_map/sum_grads/ppermute | solution.py:14
  94.8 6.7 %collective-permute-start.24 = (bf16[128,512]{1,0:T(8,128)(2,1)S(1)}, bf16[128,512]{1,0:T(8,128)(2,1)S(1)}, u32[]{:S(2)}, u32[]{:S(2)}) collective-permute-start(bf16[128,512]{1,0:T(8,128)(2,1)S(1)} %add_convert_fusion.1), channel_id=1, source_target_pairs={{0,16},{16,32},{32,48},{48,0},{1,17},{17,33},{33,49},{49,1},{2,18}... | collective-permute-start | bytes 393224 | tf_op jit(solution)/shard_map/sum_grads/ppermute | solution.py:14
  101.5 6.3 %collective-permute-start.27 = (bf16[512,896]{1,0:T(8,128)(2,1)S(1)}, bf16[512,896]{1,0:T(8,128)(2,1)S(1)}, u32[]{:S(2)}, u32[]{:S(2)}) collective-permute-start(bf16[512,896]{1,0:T(8,128)(2,1)S(1)} %pad_maximum_fusion), channel_id=1, source_target_pairs={{0,1},{1,0},{2,3},{3,2},{4,5},{5,4},{6,7},{7,6},{8,9},{9,8},{10,11... | collective-permute-start | bytes 2752520 | tf_op jit(solution)/shard_map/gather_ring/ppermute | solution.py:19

commit v5 on v4

--- a/solution.py
+++ b/solution.py
@@ -47,7 +47,10 @@
         ring = [line] + [shift(line, "y", s) for s in (1, 2, 3)]
     with jax.named_scope("gather_grads"):
         grads = jnp.concatenate([grads] + [shift(grads, "x", s) for s in (1, 2, 3)])
-        ring[1], ring[2], ring[3], grads = tie(ring[1], ring[2], ring[3], grads)
+        parts = []
+        for lo, wide in ((0, chunks[0]), (2 * chunks[0], chunks[1])):
+            parts += [lax.dynamic_slice_in_dim(eigen_act, lo + side * wide, wide, 1) for side in (core, 1 - core)]
+        ring[1], ring[2], ring[3], grads, *parts = tie(ring[1], ring[2], ring[3], grads, *parts)
         grads = jnp.concatenate([grads, swap(grads, "core")])
     with jax.named_scope("gather_plane"):
         tokens = jnp.concatenate(ring)
@@ -62,8 +65,7 @@
     lo = 0
     for wide in chunks:
         with jax.named_scope("rotate"):
-            eigen_own = lax.dynamic_slice_in_dim(eigen_act, lo + core * wide, wide, 1)
-            eigen_away = lax.dynamic_slice_in_dim(eigen_act, lo + (1 - core) * wide, wide, 1)
+            eigen_own, eigen_away = parts[:2] if lo == 0 else parts[2:]
             away = dot(tokens, eigen_away).astype(BF16)
             pair = dot(tokens, eigen_own) + swap(away, "core").astype(F32)
             pairs.append([pair.reshape(4, group, wide)])

time: 131 us -> 129 us (0.985)
  local copies, waits for them, and re-layouts: 1.24 us -> 9.97 us
  waiting for transfers between devices: 51.3 us -> 44.6 us
  other arithmetic: 2.68 us -> 1.02 us
  matrix products: 28.6 us -> 27.1 us
    dynamic_slice x0 -> x2, local copies, waits for them, and re-layouts: none -> 7.12 us  [local(): lax.dynamic_slice_in_dim(eigen_act, lo + side * wide, wide, 1)]
    ppermute x13, starting transfers between devices: 22.2 us -> 28.8 us  [swap(): return lax.ppermute(a, axis, [(i, i ^ by) for i in range(size)])]
    ppermute x15, starting transfers between devices: 23.2 us -> 16.9 us  [shift(): return lax.ppermute(a, axis, [(i, (i + by) % 4) for i in range(4)])]
    ppermute x13, waiting for transfers between devices: 19.9 us -> 14.5 us  [swap(): return lax.ppermute(a, axis, [(i, i ^ by) for i in range(size)])]
    dot_general x7, matrix products: 9.34 us -> 7.8 us  [dot(): return jnp.dot(a, b, preferred_element_type=F32)]
    ppermute x15, waiting for transfers between devices: 31.4 us -> 30.1 us  [shift(): return lax.ppermute(a, axis, [(i, (i + by) % 4) for i in range(4)])]
  transfers between devices with their start and end apart: 28 -> 28, of which waited for: 17 -> 16; matrix products, arithmetic and copies ran while one was open for 7% -> 10% of each run, Pallas kernels for 0% -> 0%
where the time goes in v5:
time: 129 us
  starting transfers between devices  45.8 us (36%)
  waiting for transfers between devices  44.6 us (35%)
  matrix products  27.1 us (21%)
  local copies, waits for them, and re-layouts  9.97 us (8%)
    ppermute x15, waiting for transfers between devices, shift(): return lax.ppermute(a, axis, [(i, (i + by) % 4) for i in range(4)])  30.1 us
    ppermute x13, starting transfers between devices, swap(): return lax.ppermute(a, axis, [(i, i ^ by) for i in range(size)])  28.8 us
    dot_general x1, matrix products, local(): jnp.einsum('eki,ekj->eij', grad_rows, act_rows, preferred_element_type=F32)  19.3 us
    ppermute x15, starting transfers between devices, shift(): return lax.ppermute(a, axis, [(i, (i + by) % 4) for i in range(4)])  16.9 us
    ppermute x13, waiting for transfers between devices, swap(): return lax.ppermute(a, axis, [(i, i ^ by) for i in range(size)])  14.5 us
    dot_general x7, matrix products, dot(): return jnp.dot(a, b, preferred_element_type=F32)  7.8 us
    dynamic_slice x2, local copies, waits for them, and re-layouts, local(): lax.dynamic_slice_in_dim(eigen_act, lo + side * wide, wide, 1)  7.12 us
  transfers between devices with their start and end apart: 28, of which 16 were waited for; matrix products, arithmetic and copies ran while one was open for 10% of the time, Pallas kernels for 0%

profile of v5, /device:TPU:1, one launch (start us, length us, event | category | flops | bytes accessed | tf_op | source)
XLA Modules:
  0.0 128.8 jit_solution(7420296789103142369)
XLA Ops:
  0.0 5.2 %collective-permute-start.2 = (bf16[32,1792]{1,0:T(8,128)(2,1)}, bf16[32,1792]{1,0:T(8,128)(2,1)S(1)}, u32[]{:S(2)}, u32[]{:S(2)}) collective-permute-start(bf16[32,1792]{1,0:T(8,128)(2,1)} %param.5), channel_id=1, source_target_pairs={{0,192},{64,128},{128,64},{192,0},{1,193},{65,129},{129,65},{193,1... | collective-permute-start | bytes 344072 | tf_op jit(solution)/shard_map/gather_line/ppermute | solution.py:19
  5.6 5.7 %collective-permute-start.3 = (bf16[32,512]{1,0:T(8,128)(2,1)}, bf16[32,512]{1,0:T(8,128)(2,1)S(1)}, u32[]{:S(2)}, u32[]{:S(2)}) collective-permute-start(bf16[32,512]{1,0:T(8,128)(2,1)} %param.6), channel_id=1, source_target_pairs={{0,2},{2,0},{1,3},{3,1},{4,6},{6,4},{5,7},{7,5},{8,10},{10,8},{9,1... | collective-permute-start | bytes 98312 | tf_op jit(solution)/shard_map/gather_grads/ppermute | solution.py:19
  11.3 3.6 %constant_dynamic-slice_fusion.2 = (bf16[1792,512]{1,0:T(8,128)(2,1)}, bf16[1792,512]{1,0:T(8,128)(2,1)S(1)}) fusion(bf16[1792,1792]{1,0:T(8,128)(2,1)} %param.7, s32[]{:T(128)S(6)} %select_n.252, s32[]{:T(128)S(6)} %select_n.251), kind=kLoop, calls=%fused_computation.73 | loop fusion | bytes 7340040 | tf_op jit(solution)/shard_map/gather_grads/dynamic_slice | solution.py:52
  14.9 3.1 %collective-permute-done.3 = bf16[32,512]{1,0:T(8,128)(2,1)S(1)} collective-permute-done((bf16[32,512]{1,0:T(8,128)(2,1)}, bf16[32,512]{1,0:T(8,128)(2,1)S(1)}, u32[]{:S(2)}, u32[]{:S(2)}) %collective-permute-start.3) | collective-permute-done | bytes 32800 | tf_op jit(solution)/shard_map/gather_grads/ppermute | solution.py:19
  18.0 1.4 %collective-permute-start.4 = (bf16[128,1792]{1,0:T(8,128)(2,1)S(1)}, bf16[128,1792]{1,0:T(8,128)(2,1)S(1)}, u32[]{:S(2)}, u32[]{:S(2)}) collective-permute-start(bf16[128,1792]{1,0:T(8,128)(2,1)S(1)} %pad_maximum_fusion.2), channel_id=1, source_target_pairs={{0,16},{16,32},{32,48},{48,0},{1,17},{17,33},{33,49},{49,1},{2,18}... | collective-permute-start | bytes 1376264 | tf_op jit(solution)/shard_map/gather_plane/ppermute | solution.py:14
  19.4 2.6 %collective-permute-start.5 = (bf16[128,1792]{1,0:T(8,128)(2,1)S(1)}, bf16[128,1792]{1,0:T(8,128)(2,1)}, u32[]{:S(2)}, u32[]{:S(2)}) collective-permute-start(bf16[128,1792]{1,0:T(8,128)(2,1)S(1)} %pad_maximum_fusion.2), channel_id=1, source_target_pairs={{0,32},{16,48},{32,0},{48,16},{1,33},{17,49},{33,1},{49,17},{2,34}... | collective-permute-start | bytes 1376264 | tf_op jit(solution)/shard_map/gather_plane/ppermute | solution.py:14
  22.0 1.1 collective-permute-start.6
  23.1 2.5 %collective-permute-start.9 = (bf16[64,512]{1,0:T(8,128)(2,1)S(1)}, bf16[64,512]{1,0:T(8,128)(2,1)S(1)}, u32[]{:S(2)}, u32[]{:S(2)}) collective-permute-start(bf16[64,512]{1,0:T(8,128)(2,1)S(1)} %pad_maximum_fusion.7), channel_id=1, source_target_pairs={{0,12},{4,0},{8,4},{12,8},{1,13},{5,1},{9,5},{13,9},{2,14},{6,2},{... | collective-permute-start | bytes 196616 | tf_op jit(solution)/shard_map/gather_grads/ppermute | solution.py:14
  25.5 3.6 %constant_dynamic-slice_fusion = (bf16[1792,384]{1,0:T(8,128)(2,1)}, bf16[1792,384]{1,0:T(8,128)(2,1)}) fusion(bf16[1792,1792]{1,0:T(8,128)(2,1)} %param.7, s32[]{:T(128)S(6)} %select_n.254, s32[]{:T(128)S(6)} %select_n.253), kind=kLoop, calls=%fused_computation.71 | loop fusion | bytes 5505032 | tf_op jit(solution)/shard_map/gather_grads/dynamic_slice | solution.py:52
  30.3 3.5 %collective-permute-done.8 = bf16[64,512]{1,0:T(8,128)(2,1)S(1)} collective-permute-done((bf16[64,512]{1,0:T(8,128)(2,1)S(1)}, bf16[64,512]{1,0:T(8,128)(2,1)S(1)}, u32[]{:S(2)}, u32[]{:S(2)}) %collective-permute-start.8) | collective-permute-done | bytes 65568 | tf_op jit(solution)/shard_map/gather_grads/ppermute | solution.py:14
  34.5 6.1 %collective-permute-done.5 = bf16[128,1792]{1,0:T(8,128)(2,1)} collective-permute-done((bf16[128,1792]{1,0:T(8,128)(2,1)S(1)}, bf16[128,1792]{1,0:T(8,128)(2,1)}, u32[]{:S(2)}, u32[]{:S(2)}) %collective-permute-start.5) | collective-permute-done | bytes 458784 | tf_op jit(solution)/shard_map/gather_plane/ppermute | solution.py:14
  41.3 1.1 constant_dynamic-update-slice_fusion.1
  43.4 1.1 convolution_convert_fusion.2
  44.6 2.2 %collective-permute-start.11 = (bf16[512,384]{1,0:T(8,128)(2,1)S(1)}, bf16[512,384]{1,0:T(8,128)(2,1)S(1)}, u32[]{:S(2)}, u32[]{:S(2)}) collective-permute-start(bf16[512,384]{1,0:T(8,128)(2,1)S(1)} %convolution_convert_fusion.2), channel_id=1, source_target_pairs={{0,1},{1,0},{2,3},{3,2},{4,5},{5,4},{6,7},{7,6},{8,9},{9,8},{10,11... | collective-permute-start | bytes 1179656 | tf_op jit(solution)/shard_map/rotate/ppermute | solution.py:19
  46.9 1.1 convolution_convert_fusion.1
  49.0 1.2 collective-permute-start.16
  50.2 1.1 convolution_add_fusion.1
  51.4 1.1 convolution_add_fusion
  52.7 2.6 %collective-permute-start.14 = (bf16[128,896]{1,0:T(8,128)(2,1)S(1)}, bf16[128,896]{1,0:T(8,128)(2,1)S(1)}, u32[]{:S(2)}, u32[]{:S(2)}) collective-permute-start(bf16[128,896]{1,0:T(8,128)(2,1)S(1)} %pad_maximum_fusion.6), channel_id=1, source_target_pairs={{0,12},{4,0},{8,4},{12,8},{1,13},{5,1},{9,5},{13,9},{2,14},{6,2},{... | collective-permute-start | bytes 688136 | tf_op jit(solution)/shard_map/sum_ring/ppermute | solution.py:14
  56.9 2.4 %collective-permute-start.17 = (f32[128,512]{1,0:T(8,128)S(1)}, f32[128,512]{1,0:T(8,128)S(1)}, u32[]{:S(2)}, u32[]{:S(2)}) collective-permute-start(f32[128,512]{1,0:T(8,128)S(1)} %dynamic-slice_bitcast_fusion), channel_id=1, source_target_pairs={{0,32},{16,48},{32,0},{48,16},{1,33},{17,49},{33,1},{49,17},{2,34}... | collective-permute-start | bytes 786440 | tf_op jit(solution)/shard_map/sum_grads/ppermute | solution.py:19
  60.3 2.7 %collective-permute-done.13 = bf16[128,896]{1,0:T(8,128)(2,1)S(1)} collective-permute-done((bf16[128,896]{1,0:T(8,128)(2,1)S(1)}, bf16[128,896]{1,0:T(8,128)(2,1)S(1)}, u32[]{:S(2)}, u32[]{:S(2)}) %collective-permute-start.13) | collective-permute-done | bytes 229408 | tf_op jit(solution)/shard_map/sum_ring/ppermute | solution.py:14
  63.0 6.2 %collective-permute-done.12 = bf16[128,896]{1,0:T(8,128)(2,1)S(1)} collective-permute-done((bf16[128,896]{1,0:T(8,128)(2,1)S(1)}, bf16[128,896]{1,0:T(8,128)(2,1)S(1)}, u32[]{:S(2)}, u32[]{:S(2)}) %collective-permute-start.12) | collective-permute-done | bytes 229408 | tf_op jit(solution)/shard_map/sum_ring/ppermute | solution.py:14
  70.1 3.0 %collective-permute-start.18 = (bf16[128,896]{1,0:T(8,128)(2,1)S(1)}, bf16[128,896]{1,0:T(8,128)(2,1)S(1)}, u32[]{:S(2)}, u32[]{:S(2)}) collective-permute-start(bf16[128,896]{1,0:T(8,128)(2,1)S(1)} %convert_element_type.79), channel_id=1, source_target_pairs={{0,2},{2,0},{1,3},{3,1},{4,6},{6,4},{5,7},{7,5},{8,10},{10,8},{9,1... | collective-permute-start | bytes 688136 | tf_op jit(solution)/shard_map/sum_far/ppermute | solution.py:19
  73.1 1.1 collective-permute-done.19
  74.2 8.5 %collective-permute-done.18 = bf16[128,896]{1,0:T(8,128)(2,1)S(1)} collective-permute-done((bf16[128,896]{1,0:T(8,128)(2,1)S(1)}, bf16[128,896]{1,0:T(8,128)(2,1)S(1)}, u32[]{:S(2)}, u32[]{:S(2)}) %collective-permute-start.18) | collective-permute-done | bytes 229408 | tf_op jit(solution)/shard_map/sum_far/ppermute | solution.py:19
  82.8 4.3 %collective-permute-start.23 = (bf16[128,512]{1,0:T(8,128)(2,1)S(1)}, bf16[128,512]{1,0:T(8,128)(2,1)S(1)}, u32[]{:S(2)}, u32[]{:S(2)}) collective-permute-start(bf16[128,512]{1,0:T(8,128)(2,1)S(1)} %convert_element_type.84), channel_id=1, source_target_pairs={{0,128},{64,192},{128,0},{192,64},{1,129},{65,193},{129,1},{193,65... | collective-permute-start | bytes 393224 | tf_op jit(solution)/shard_map/sum_grads/ppermute | solution.py:19
  89.5 1.7 %collective-permute-start.26 = (bf16[128,512]{1,0:T(8,128)(2,1)S(1)}, bf16[128,512]{1,0:T(8,128)(2,1)S(1)}, u32[]{:S(2)}, u32[]{:S(2)}) collective-permute-start(bf16[128,512]{1,0:T(8,128)(2,1)S(1)} %add_convert_fusion.1), channel_id=1, source_target_pairs={{0,48},{16,0},{32,16},{48,32},{1,49},{17,1},{33,17},{49,33},{2,50}... | collective-permute-start | bytes 393224 | tf_op jit(solution)/shard_map/sum_grads/ppermute | solution.py:14
  93.1 1.5 %collective-permute-done.21 = bf16[128,896]{1,0:T(8,128)(2,1)S(1)} collective-permute-done((bf16[128,896]{1,0:T(8,128)(2,1)S(1)}, bf16[128,896]{1,0:T(8,128)(2,1)S(1)}, u32[]{:S(2)}, u32[]{:S(2)}) %collective-permute-start.21) | collective-permute-done | bytes 229408 | tf_op jit(solution)/shard_map/gather_ring/ppermute | solution.py:14
  94.6 6.8 %collective-permute-done.20 = bf16[128,896]{1,0:T(8,128)(2,1)S(1)} collective-permute-done((bf16[128,896]{1,0:T(8,128)(2,1)S(1)}, bf16[128,896]{1,0:T(8,128)(2,1)S(1)}, u32[]{:S(2)}, u32[]{:S(2)}) %collective-permute-start.20) | collective-permute-done | bytes 229408 | tf_op jit(solution)/shard_map/gather_ring/ppermute | solution.py:14
  101.6 3.2 %collective-permute-start.27 = (bf16[512,896]{1,0:T(8,128)(2,1)S(1)}, bf16[512,896]{1,0:T(8,128)(2,1)S(1)}, u32[]{:S(2)}, u32[]{:S(2)}) collective-permute-start(bf16[512,896]{1,0:T(8,128)(2,1)S(1)} %pad_maximum_fusion), channel_id=1, source_target_pairs={{0,1},{1,0},{2,3},{3,2},{4,5},{5,4},{6,7},{7,6},{8,9},{9,8},{10,11... | collective-permute-start | bytes 2752520 | tf_op jit(solution)/shard_map/gather_ring/ppermute | solution.py:19
  107.3 2.2 %convolution_convert_fusion = bf16[1024,1792]{1,0:T(8,128)(2,1)S(1)} fusion(bf16[512,384]{1,0:T(8,128)(2,1)S(1)} %slice.27, bf16[512,384]{1,0:T(8,128)(2,1)S(1)} %slice.26, bf16[512,512]{1,0:T(8,128)(2,1)S(1)} %slice.25, bf16[512,512]{1,0:T(8,128)(2,1)S(1)} %slice.24, s32[512]{0:T(512)S(1)} %get-tuple-element.51, s32[1024]{0:T(1024)S(1)} %compare_select_fusion), kind=kOutput, calls=%fused_computation.1 | convolution fusion | flops 1888747520 | bytes 5511168 | tf_op jit(solution)/shard_map/squares/dot_general | solution.py:27
  109.5 19.3 %multiply_reduce_fusion = f32[512,1792]{1,0:T(8,128)} fusion(bf16[32,32,512]{2,1,0:T(8,128)(2,1)S(1)} %bitcast.51, bf16[32,32,1792]{2,1,0:T(8,128)(2,1)S(1)} %bitcast.50), kind=kOutput, calls=%fused_computation | convolution fusion | flops 1966211072 | bytes 8388608 | tf_op jit(solution)/shard_map/squares/eki,ekj->eij/dot_general | solution.py:127
  (88 shorter events, 15.7 us)
Async XLA Ops:
  0.0 48.5 %copy-start = (bf16[512,512]{1,0:T(8,128)(2,1)S(1)}, bf16[512,512]{1,0:T(8,128)(2,1)}, u32[]{:S(2)}) copy-start(bf16[512,512]{1,0:T(8,128)(2,1)} %param.8) | copy-start | bytes 1572868
  0.0 17.9 %collective-permute-start.2 = (bf16[32,1792]{1,0:T(8,128)(2,1)}, bf16[32,1792]{1,0:T(8,128)(2,1)S(1)}, u32[]{:S(2)}, u32[]{:S(2)}) collective-permute-start(bf16[32,1792]{1,0:T(8,128)(2,1)} %param.5), channel_id=1, source_target_pairs={{0,192},{64,128},{128,64},{192,0},{1,193},{65,129},{129,65},{193,1... | collective-permute-start | bytes 344072 | tf_op jit(solution)/shard_map/gather_line/ppermute | solution.py:19
  5.2 12.8 %collective-permute-start.1 = (bf16[32,1792]{1,0:T(8,128)(2,1)}, bf16[32,1792]{1,0:T(8,128)(2,1)S(1)}, u32[]{:S(2)}, u32[]{:S(2)}) collective-permute-start(bf16[32,1792]{1,0:T(8,128)(2,1)} %param.5), channel_id=1, source_target_pairs={{0,128},{64,192},{128,0},{192,64},{1,129},{65,193},{129,1},{193,65... | collective-permute-start | bytes 344072 | tf_op jit(solution)/shard_map/gather_line/ppermute | solution.py:19
  5.2 12.8 %collective-permute-start = (bf16[32,1792]{1,0:T(8,128)(2,1)}, bf16[32,1792]{1,0:T(8,128)(2,1)S(1)}, u32[]{:S(2)}, u32[]{:S(2)}) collective-permute-start(bf16[32,1792]{1,0:T(8,128)(2,1)} %param.5), channel_id=1, source_target_pairs={{0,64},{64,0},{128,192},{192,128},{1,65},{65,1},{129,193},{193,129... | collective-permute-start | bytes 344072 | tf_op jit(solution)/shard_map/gather_line/ppermute | solution.py:19
  5.6 12.4 %collective-permute-start.3 = (bf16[32,512]{1,0:T(8,128)(2,1)}, bf16[32,512]{1,0:T(8,128)(2,1)S(1)}, u32[]{:S(2)}, u32[]{:S(2)}) collective-permute-start(bf16[32,512]{1,0:T(8,128)(2,1)} %param.6), channel_id=1, source_target_pairs={{0,2},{2,0},{1,3},{3,1},{4,6},{6,4},{5,7},{7,5},{8,10},{10,8},{9,1... | collective-permute-start | bytes 98312 | tf_op jit(solution)/shard_map/gather_grads/ppermute | solution.py:19
  11.3 6.7 %copy-start.4 = (bf16[32,1792]{1,0:T(8,128)(2,1)S(1)}, bf16[32,1792]{1,0:T(8,128)(2,1)}, u32[]{:S(2)}) copy-start(bf16[32,1792]{1,0:T(8,128)(2,1)} %param.5) | copy-start | bytes 344068
  18.0 16.4 %collective-permute-start.4 = (bf16[128,1792]{1,0:T(8,128)(2,1)S(1)}, bf16[128,1792]{1,0:T(8,128)(2,1)S(1)}, u32[]{:S(2)}, u32[]{:S(2)}) collective-permute-start(bf16[128,1792]{1,0:T(8,128)(2,1)S(1)} %pad_maximum_fusion.2), channel_id=1, source_target_pairs={{0,16},{16,32},{32,48},{48,0},{1,17},{17,33},{33,49},{49,1},{2,18}... | collective-permute-start | bytes 1376264 | tf_op jit(solution)/shard_map/gather_plane/ppermute | solution.py:14
  19.4 21.2 %collective-permute-start.5 = (bf16[128,1792]{1,0:T(8,128)(2,1)S(1)}, bf16[128,1792]{1,0:T(8,128)(2,1)}, u32[]{:S(2)}, u32[]{:S(2)}) collective-permute-start(bf16[128,1792]{1,0:T(8,128)(2,1)S(1)} %pad_maximum_fusion.2), channel_id=1, source_target_pairs={{0,32},{16,48},{32,0},{48,16},{1,33},{17,49},{33,1},{49,17},{2,34}... | collective-permute-start | bytes 1376264 | tf_op jit(solution)/shard_map/gather_plane/ppermute | solution.py:14
  22.0 19.3 %collective-permute-start.6 = (bf16[128,1792]{1,0:T(8,128)(2,1)S(1)}, bf16[128,1792]{1,0:T(8,128)(2,1)}, u32[]{:S(2)}, u32[]{:S(2)}) collective-permute-start(bf16[128,1792]{1,0:T(8,128)(2,1)S(1)} %pad_maximum_fusion.2), channel_id=1, source_target_pairs={{0,48},{16,0},{32,16},{48,32},{1,49},{17,1},{33,17},{49,33},{2,50}... | collective-permute-start | bytes 1376264 | tf_op jit(solution)/shard_map/gather_plane/ppermute | solution.py:14
  23.1 6.6 %collective-permute-start.9 = (bf16[64,512]{1,0:T(8,128)(2,1)S(1)}, bf16[64,512]{1,0:T(8,128)(2,1)S(1)}, u32[]{:S(2)}, u32[]{:S(2)}) collective-permute-start(bf16[64,512]{1,0:T(8,128)(2,1)S(1)} %pad_maximum_fusion.7), channel_id=1, source_target_pairs={{0,12},{4,0},{8,4},{12,8},{1,13},{5,1},{9,5},{13,9},{2,14},{6,2},{... | collective-permute-start | bytes 196616 | tf_op jit(solution)/shard_map/gather_grads/ppermute | solution.py:14
  29.1 4.7 %collective-permute-start.8 = (bf16[64,512]{1,0:T(8,128)(2,1)S(1)}, bf16[64,512]{1,0:T(8,128)(2,1)S(1)}, u32[]{:S(2)}, u32[]{:S(2)}) collective-permute-start(bf16[64,512]{1,0:T(8,128)(2,1)S(1)} %pad_maximum_fusion.7), channel_id=1, source_target_pairs={{0,8},{4,12},{8,0},{12,4},{1,9},{5,13},{9,1},{13,5},{2,10},{6,14},... | collective-permute-start | bytes 196616 | tf_op jit(solution)/shard_map/gather_grads/ppermute | solution.py:14
  29.6 4.8 %collective-permute-start.7 = (bf16[64,512]{1,0:T(8,128)(2,1)S(1)}, bf16[64,512]{1,0:T(8,128)(2,1)S(1)}, u32[]{:S(2)}, u32[]{:S(2)}) collective-permute-start(bf16[64,512]{1,0:T(8,128)(2,1)S(1)} %pad_maximum_fusion.7), channel_id=1, source_target_pairs={{0,4},{4,8},{8,12},{12,0},{1,5},{5,9},{9,13},{13,1},{2,6},{6,10},{... | collective-permute-start | bytes 196616 | tf_op jit(solution)/shard_map/gather_grads/ppermute | solution.py:14
  30.3 13.2 %copy-start.3 = (bf16[1792,384]{1,0:T(8,128)(2,1)S(1)}, bf16[1792,384]{1,0:T(8,128)(2,1)}, u32[]{:S(2)}) copy-start(bf16[1792,384]{1,0:T(8,128)(2,1)} %get-tuple-element.29) | copy-start | bytes 4128772
  44.6 5.7 %collective-permute-start.11 = (bf16[512,384]{1,0:T(8,128)(2,1)S(1)}, bf16[512,384]{1,0:T(8,128)(2,1)S(1)}, u32[]{:S(2)}, u32[]{:S(2)}) collective-permute-start(bf16[512,384]{1,0:T(8,128)(2,1)S(1)} %convolution_convert_fusion.2), channel_id=1, source_target_pairs={{0,1},{1,0},{2,3},{3,2},{4,5},{5,4},{6,7},{7,6},{8,9},{9,8},{10,11... | collective-permute-start | bytes 1179656 | tf_op jit(solution)/shard_map/rotate/ppermute | solution.py:19
  46.8 1.7 %collective-permute-start.15 = (bf16[256,512]{1,0:T(8,128)(2,1)S(1)}, bf16[256,512]{1,0:T(8,128)(2,1)S(1)}, u32[]{:S(2)}, u32[]{:S(2)}) collective-permute-start(bf16[256,512]{1,0:T(8,128)(2,1)S(1)} %pad_maximum_fusion.3), channel_id=1, source_target_pairs={{0,1},{1,0},{2,3},{3,2},{4,5},{5,4},{6,7},{7,6},{8,9},{9,8},{10,11... | collective-permute-start | bytes 786440 | tf_op jit(solution)/shard_map/gather_grads/ppermute | solution.py:19
  48.0 3.4 %collective-permute-start.10 = (bf16[512,512]{1,0:T(8,128)(2,1)S(1)}, bf16[512,512]{1,0:T(8,128)(2,1)S(1)}, u32[]{:S(2)}, u32[]{:S(2)}) collective-permute-start(bf16[512,512]{1,0:T(8,128)(2,1)S(1)} %convolution_convert_fusion.1), channel_id=1, source_target_pairs={{0,1},{1,0},{2,3},{3,2},{4,5},{5,4},{6,7},{7,6},{8,9},{9,8},{10,11... | collective-permute-start | bytes 1572872 | tf_op jit(solution)/shard_map/rotate/ppermute | solution.py:19
  49.0 7.8 %collective-permute-start.16 = (bf16[256,512]{1,0:T(8,128)(2,1)S(1)}, bf16[256,512]{1,0:T(8,128)(2,1)S(1)}, u32[]{:S(2)}, u32[]{:S(2)}) collective-permute-start(bf16[256,512]{1,0:T(8,128)(2,1)S(1)} %fusion.23), channel_id=1, source_target_pairs={{0,16},{16,0},{32,48},{48,32},{1,17},{17,1},{33,49},{49,33},{2,18}... | collective-permute-start | bytes 786440 | tf_op jit(solution)/shard_map/sum_grads/ppermute | solution.py:19
  52.7 7.7 %collective-permute-start.14 = (bf16[128,896]{1,0:T(8,128)(2,1)S(1)}, bf16[128,896]{1,0:T(8,128)(2,1)S(1)}, u32[]{:S(2)}, u32[]{:S(2)}) collective-permute-start(bf16[128,896]{1,0:T(8,128)(2,1)S(1)} %pad_maximum_fusion.6), channel_id=1, source_target_pairs={{0,12},{4,0},{8,4},{12,8},{1,13},{5,1},{9,5},{13,9},{2,14},{6,2},{... | collective-permute-start | bytes 688136 | tf_op jit(solution)/shard_map/sum_ring/ppermute | solution.py:14
  55.2 7.8 %collective-permute-start.13 = (bf16[128,896]{1,0:T(8,128)(2,1)S(1)}, bf16[128,896]{1,0:T(8,128)(2,1)S(1)}, u32[]{:S(2)}, u32[]{:S(2)}) collective-permute-start(bf16[128,896]{1,0:T(8,128)(2,1)S(1)} %pad_maximum_fusion.5), channel_id=1, source_target_pairs={{0,8},{4,12},{8,0},{12,4},{1,9},{5,13},{9,1},{13,5},{2,10},{6,14},... | collective-permute-start | bytes 688136 | tf_op jit(solution)/shard_map/sum_ring/ppermute | solution.py:14
  55.9 13.4 %collective-permute-start.12 = (bf16[128,896]{1,0:T(8,128)(2,1)S(1)}, bf16[128,896]{1,0:T(8,128)(2,1)S(1)}, u32[]{:S(2)}, u32[]{:S(2)}) collective-permute-start(bf16[128,896]{1,0:T(8,128)(2,1)S(1)} %pad_maximum_fusion.4), channel_id=1, source_target_pairs={{0,4},{4,8},{8,12},{12,0},{1,5},{5,9},{9,13},{13,1},{2,6},{6,10},{... | collective-permute-start | bytes 688136 | tf_op jit(solution)/shard_map/sum_ring/ppermute | solution.py:14
  56.9 12.5 %collective-permute-start.17 = (f32[128,512]{1,0:T(8,128)S(1)}, f32[128,512]{1,0:T(8,128)S(1)}, u32[]{:S(2)}, u32[]{:S(2)}) collective-permute-start(f32[128,512]{1,0:T(8,128)S(1)} %dynamic-slice_bitcast_fusion), channel_id=1, source_target_pairs={{0,32},{16,48},{32,0},{48,16},{1,33},{17,49},{33,1},{49,17},{2,34}... | collective-permute-start | bytes 786440 | tf_op jit(solution)/shard_map/sum_grads/ppermute | solution.py:19
  69.4 17.8 %copy-start.6 = (s32[512]{0:T(512)S(1)}, s32[512]{0:T(512)}, u32[]{:S(2)}) copy-start(s32[512]{0:T(512)} %param.9) | copy-start | bytes 6148
  69.5 4.7 %collective-permute-start.19 = (bf16[128,512]{1,0:T(8,128)(2,1)S(1)}, bf16[128,512]{1,0:T(8,128)(2,1)S(1)}, u32[]{:S(2)}, u32[]{:S(2)}) collective-permute-start(bf16[128,512]{1,0:T(8,128)(2,1)S(1)} %convert_element_type.82), channel_id=1, source_target_pairs={{0,64},{64,0},{128,192},{192,128},{1,65},{65,1},{129,193},{193,129... | collective-permute-start | bytes 393224 | tf_op jit(solution)/shard_map/sum_grads/ppermute | solution.py:19
  70.1 12.6 %collective-permute-start.18 = (bf16[128,896]{1,0:T(8,128)(2,1)S(1)}, bf16[128,896]{1,0:T(8,128)(2,1)S(1)}, u32[]{:S(2)}, u32[]{:S(2)}) collective-permute-start(bf16[128,896]{1,0:T(8,128)(2,1)S(1)} %convert_element_type.79), channel_id=1, source_target_pairs={{0,2},{2,0},{1,3},{3,1},{4,6},{6,4},{5,7},{7,5},{8,10},{10,8},{9,1... | collective-permute-start | bytes 688136 | tf_op jit(solution)/shard_map/sum_far/ppermute | solution.py:19
  82.8 6.7 %collective-permute-start.23 = (bf16[128,512]{1,0:T(8,128)(2,1)S(1)}, bf16[128,512]{1,0:T(8,128)(2,1)S(1)}, u32[]{:S(2)}, u32[]{:S(2)}) collective-permute-start(bf16[128,512]{1,0:T(8,128)(2,1)S(1)} %convert_element_type.84), channel_id=1, source_target_pairs={{0,128},{64,192},{128,0},{192,64},{1,129},{65,193},{129,1},{193,65... | collective-permute-start | bytes 393224 | tf_op jit(solution)/shard_map/sum_grads/ppermute | solution.py:19
  87.2 5.4 %collective-permute-start.22 = (bf16[128,896]{1,0:T(8,128)(2,1)S(1)}, bf16[128,896]{1,0:T(8,128)(2,1)S(1)}, u32[]{:S(2)}, u32[]{:S(2)}) collective-permute-start(bf16[128,896]{1,0:T(8,128)(2,1)S(1)} %add_convert_fusion), channel_id=1, source_target_pairs={{0,12},{4,0},{8,4},{12,8},{1,13},{5,1},{9,5},{13,9},{2,14},{6,2},{... | collective-permute-start | bytes 688136 | tf_op jit(solution)/shard_map/gather_ring/ppermute | solution.py:14
  87.6 7.0 %collective-permute-start.21 = (bf16[128,896]{1,0:T(8,128)(2,1)S(1)}, bf16[128,896]{1,0:T(8,128)(2,1)S(1)}, u32[]{:S(2)}, u32[]{:S(2)}) collective-permute-start(bf16[128,896]{1,0:T(8,128)(2,1)S(1)} %add_convert_fusion), channel_id=1, source_target_pairs={{0,8},{4,12},{8,0},{12,4},{1,9},{5,13},{9,1},{13,5},{2,10},{6,14},... | collective-permute-start | bytes 688136 | tf_op jit(solution)/shard_map/gather_ring/ppermute | solution.py:14
  88.1 13.3 %collective-permute-start.20 = (bf16[128,896]{1,0:T(8,128)(2,1)S(1)}, bf16[128,896]{1,0:T(8,128)(2,1)S(1)}, u32[]{:S(2)}, u32[]{:S(2)}) collective-permute-start(bf16[128,896]{1,0:T(8,128)(2,1)S(1)} %add_convert_fusion), channel_id=1, source_target_pairs={{0,4},{4,8},{8,12},{12,0},{1,5},{5,9},{9,13},{13,1},{2,6},{6,10},{... | collective-permute-start | bytes 688136 | tf_op jit(solution)/shard_map/gather_ring/ppermute | solution.py:14
  89.5 12.1 %collective-permute-start.26 = (bf16[128,512]{1,0:T(8,128)(2,1)S(1)}, bf16[128,512]{1,0:T(8,128)(2,1)S(1)}, u32[]{:S(2)}, u32[]{:S(2)}) collective-permute-start(bf16[128,512]{1,0:T(8,128)(2,1)S(1)} %add_convert_fusion.1), channel_id=1, source_target_pairs={{0,48},{16,0},{32,16},{48,32},{1,49},{17,1},{33,17},{49,33},{2,50}... | collective-permute-start | bytes 393224 | tf_op jit(solution)/shard_map/sum_grads/ppermute | solution.py:14
  91.2 10.4 %collective-permute-start.25 = (bf16[128,512]{1,0:T(8,128)(2,1)S(1)}, bf16[128,512]{1,0:T(8,128)(2,1)S(1)}, u32[]{:S(2)}, u32[]{:S(2)}) collective-permute-start(bf16[128,512]{1,0:T(8,128)(2,1)S(1)} %add_convert_fusion.1), channel_id=1, source_target_pairs={{0,32},{16,48},{32,0},{48,16},{1,33},{17,49},{33,1},{49,17},{2,34}... | collective-permute-start | bytes 393224 | tf_op jit(solution)/shard_map/sum_grads/ppermute | solution.py:14
  92.6 8.9 %collective-permute-start.24 = (bf16[128,512]{1,0:T(8,128)(2,1)S(1)}, bf16[128,512]{1,0:T(8,128)(2,1)S(1)}, u32[]{:S(2)}, u32[]{:S(2)}) collective-permute-start(bf16[128,512]{1,0:T(8,128)(2,1)S(1)} %add_convert_fusion.1), channel_id=1, source_target_pairs={{0,16},{16,32},{32,48},{48,0},{1,17},{17,33},{33,49},{49,1},{2,18}... | collective-permute-start | bytes 393224 | tf_op jit(solution)/shard_map/sum_grads/ppermute | solution.py:14
  101.6 5.3 %collective-permute-start.27 = (bf16[512,896]{1,0:T(8,128)(2,1)S(1)}, bf16[512,896]{1,0:T(8,128)(2,1)S(1)}, u32[]{:S(2)}, u32[]{:S(2)}) collective-permute-start(bf16[512,896]{1,0:T(8,128)(2,1)S(1)} %pad_maximum_fusion), channel_id=1, source_target_pairs={{0,1},{1,0},{2,3},{3,2},{4,5},{5,4},{6,7},{7,6},{8,9},{9,8},{10,11... | collective-permute-start | bytes 2752520 | tf_op jit(solution)/shard_map/gather_ring/ppermute | solution.py:19
  (3 other events, 12.3 us)
